TPU v7x, 512 devices: a whole 4x8x8 slice. The times are simulated.
512 devices in a mesh: stream: 64 (over x, z, core), azi: 8 (over y).
Axes of the slice: x: 4, y: 8, z: 8, core: 2. Of those that a mesh axis runs over, the one named last changes fastest.
Arguments:
- right_sides: float32 [1024, 320, 128], P(('stream', 'azi')), may hold values from -2.5 to 2.5
- inverse_blocks: float32 [1024, 320, 320], P(('stream', 'azi')), may hold values from -1 to 2
- lower_faces: float32 [1024, 80, 240], P(('stream', 'azi')), may hold values from -2 to 1
- upper_faces: float32 [1024, 80, 240], P(('stream', 'azi')), may hold values from -2 to 1
- upwind_index: int32 [1024, 3], P(('stream', 'azi')), may hold values from 0 to 2, as said below
- wake_rows: float32 [32768, 320], P(('stream', 'azi')), may hold values from -2 to 2
- wake_target: int32 [32768], P(('stream', 'azi')), may hold values from 0 to 15
Outputs:
- solution: float32 [1024, 320, 128], P(('stream', 'azi'))
Inputs may be any that keep to these rules, and one draw needn't show every extreme that they name: `upwind_index`: row n = (k * 8 + a) * 2 + e: every entry is an element place below e, or exactly 2, which names the last element of the previous slab in the same sector; the three entries of every row with e = 0 are 2.
All inputs are finite; a program needn't handle non-finite values.
Results may differ from a plain program's by a relative error of at most 0.0003.
Values sent between devices are 32-bit elements; how exact they have to be, the bound alone decides.
No kernel may reach another device: no remote copies, remote signals or barrier semaphores. Data moves between devices by JAX's collectives and lax.ppermute only.
A program may use at most 64 MiB of HBM per device.

v0:
```python
import jax
import jax.numpy as jnp
from jax import lax
from jax.sharding import PartitionSpec as P

FIELDS = 5
POINTS = 4
TRACE = 80


PRECISE = lax.Precision.HIGHEST


def prefix(value, axis, combine, identity, reverse):
    count, mine = (lax.axis_size(axis), lax.axis_index(axis))
    everything = jax.tree.map(lambda part: lax.all_gather(part, axis), value)
    start = jax.tree.map(
        lambda part, zero: jnp.broadcast_to(jnp.asarray(zero, part.dtype), part.shape),
        value,
        identity,
    )

    def step(k, before):
        at = count - 1 - k if reverse else k
        reached = at > mine if reverse else at < mine
        new = combine(before, jax.tree.map(lambda part: part[at], everything))
        return jax.tree.map(lambda a, b: jnp.where(reached, a, b), new, before)

    return lax.fori_loop(0, count, step, start)


def matmul(operand_a, operand_b):
    return jnp.dot(operand_a, operand_b, precision=PRECISE, preferred_element_type=jnp.float32)


def take_face(values, face_slot):
    cubed = values.reshape(FIELDS, POINTS, POINTS, POINTS, values.shape[-1])
    side_index = 0 if face_slot % 2 == 0 else POINTS - 1
    face_plane = lax.index_in_dim(cubed, side_index, face_slot // 2 + 1, keepdims=False)
    return face_plane.reshape(FIELDS * POINTS * POINTS, values.shape[-1])


def put_face(values, face_rows, face_slot):
    cubed = values.reshape(FIELDS, POINTS, POINTS, POINTS, values.shape[-1])
    side_index = 0 if face_slot % 2 == 0 else POINTS - 1
    position = [slice(None)] * 5
    position[face_slot // 2 + 1] = side_index
    face_plane = face_rows.reshape(FIELDS, POINTS, POINTS, values.shape[-1])
    return cubed.at[tuple(position)].add(face_plane).reshape(values.shape)


def lower_sweep(source, inverse, lower, upwind, inflow):
    local_count = source.shape[0]
    trace_rows = inflow.shape[0]
    solved = []
    for element in range(local_count):
        summed = source[element]
        for face_no in range(3):
            options = [take_face(solved[earlier], 2 * face_no + 1) for earlier in range(element)]
            stacked = jnp.stack(options + [inflow])
            chosen = jnp.minimum(upwind[element, face_no], element)
            traced = lax.dynamic_index_in_dim(stacked, chosen, 0, keepdims=False)
            coupling = lower[element, :, face_no * trace_rows : (face_no + 1) * trace_rows]
            summed = put_face(summed, -matmul(coupling, traced), 2 * face_no)
        solved.append(matmul(inverse[element], summed))
    return (jnp.stack(solved), take_face(solved[-1], 1))


def upper_sweep(base, inverse, upper, upwind, incoming):
    local_count = base.shape[0]
    trace_rows = incoming.shape[0]
    results = [None] * local_count
    pending = []
    outgoing = jnp.zeros_like(incoming)
    for element in reversed(range(local_count)):
        summed = jnp.zeros_like(base[element])
        for later_elem, face_no, coupled in pending:
            matches = (upwind[later_elem, face_no] == element).astype(jnp.float32)
            summed = put_face(summed, matches * coupled, 2 * face_no + 1)
        if element == local_count - 1:
            summed = put_face(summed, incoming, 1)
        solved = base[element] - matmul(inverse[element], summed)
        results[element] = solved
        for face_no in range(3):
            coupling = upper[element, :, face_no * trace_rows : (face_no + 1) * trace_rows]
            coupled = matmul(coupling, take_face(solved, 2 * face_no))
            pending.append((element, face_no, coupled))
            crossing = (upwind[element, face_no] == local_count).astype(jnp.float32)
            outgoing = outgoing + crossing * coupled
    return (jnp.stack(results), outgoing)


def compose(earlier, later):
    return (matmul(later[0], earlier[0]), matmul(later[0], earlier[1]) + later[1])


def shards(
    right_sides, inverse_blocks, lower_faces, upper_faces, upwind_index, wake_rows, wake_target
):
    local_count = right_sides.shape[0]
    block_rows = right_sides.shape[1]
    columns = right_sides.shape[2]
    groups = lax.axis_size("azi")
    row_ids = lax.broadcasted_iota(jnp.int32, (groups * local_count, wake_target.shape[0]), 0)
    onehot = (row_ids == wake_target[None, :]).astype(jnp.float32)
    partial_value = matmul(onehot, wake_rows)
    wake = lax.psum_scatter(partial_value, "azi", scatter_dimension=0, tiled=True)
    source = right_sides + wake[:, :, None]
    identity = jnp.eye(TRACE, dtype=jnp.float32)
    no_offset = jnp.zeros((TRACE, columns), jnp.float32)
    unit_side = jnp.concatenate([no_offset, identity], axis=1)
    extra_zeros = jnp.zeros((local_count, block_rows, TRACE), jnp.float32)
    wide_source = jnp.concatenate([source, extra_zeros], axis=2)
    solved_wide, outflow = lower_sweep(
        wide_source, inverse_blocks, lower_faces, upwind_index, unit_side
    )
    matrix = outflow[:, columns:]
    offset = outflow[:, :columns]
    inflow = prefix((matrix, offset), "stream", compose, (identity, no_offset), False)[1]
    lowered, _ = lower_sweep(source, inverse_blocks, lower_faces, upwind_index, inflow)
    wide_base = jnp.concatenate([lowered, extra_zeros], axis=2)
    back_wide, returned = upper_sweep(
        wide_base, inverse_blocks, upper_faces, upwind_index, unit_side
    )
    back_matrix = returned[:, columns:]
    back_offset = returned[:, :columns]
    incoming = prefix((back_matrix, back_offset), "stream", compose, (identity, no_offset), True)[1]
    solution, _ = upper_sweep(lowered, inverse_blocks, upper_faces, upwind_index, incoming)
    return solution


def solution(mesh):
    return jax.shard_map(
        shards,
        mesh=mesh,
        in_specs=(
            P(("stream", "azi"), None, None),
            P(("stream", "azi"), None, None),
            P(("stream", "azi"), None, None),
            P(("stream", "azi"), None, None),
            P(("stream", "azi"), None),
            P(("stream", "azi"), None),
            P(("stream", "azi")),
        ),
        out_specs=P(("stream", "azi"), None, None),
        check_vma=False,
    )
```

profile of v0, /device:TPU:6, one launch (start us, length us, event | category | flops | bytes accessed | tf_op | source)
XLA Modules:
  0.0 549.5 jit_solution(17896973219501210680)
XLA Ops:
  6.5 1.6 fusion.139
  11.1 1.1 fusion.29
  12.2 1.0 fusion.28
  14.1 30.4 %all-reduce.7 = f32[16,320]{1,0:T(8,128)S(1)} all-reduce(f32[16,320]{1,0:T(8,128)S(1)} %fusion.127), channel_id=6, replica_groups=mesh['stream'=64,'azi'=8] {'azi'}, use_global_device_ids=true, to_apply=%region_0.0.clone | all-reduce | flops 5120 | bytes 40960
  44.4 1.3 dynamic-slice.142
  46.4 1.1 broadcast_add_fusion
  48.0 2.4 scatter-add.70
  50.5 1.4 convolution_bitcast_fusion.3
  52.6 1.0 fusion.54
  54.8 2.4 scatter-add.75
  57.4 1.4 convolution_bitcast_fusion.2
  66.7 78.0 %all-gather.9.cloned.1.call-done = f32[5120,80]{1,0:T(8,128)} async-done(((f32[80,80]{1,0:T(8,128)}), f32[5120,80]{1,0:T(8,128)}) %all-gather.9.cloned.1.call-update) | async-done | bytes 1638416 | tf_op jit(solution)/shard_map/all_gather | solution.py:16
  144.7 84.4 %all-gather.11.cloned.1.call-done = f32[5120,128]{1,0:T(8,128)} async-done(((f32[80,128]{1,0:T(8,128)}), f32[5120,128]{1,0:T(8,128)}) %all-gather.11.cloned.1.call-update) | async-done | bytes 2621456 | tf_op jit(solution)/shard_map/all_gather | solution.py:16
  229.0 65.2 %while.50 = (s32[]{:T(128)}, f32[80,128]{1,0:T(8,128)S(1)}, s32[]{:T(128)}, f32[64,80,80]{2,1,0:T(8,128)}, f32[64,80,128]{2,1,0:T(8,128)}, /*index=5*/s32[]{:T(128)}, s32[]{:T(128)}) while((s32[]{:T(128)}, f32[80,128]{1,0:T(8,128)S(1)}, s32[]{:T(128)}, f32[64,80,80]{2,1,0:T(8,128)}, f32[64,80,128]{2,1,0:T(8,128)}, ...), condition=%wide.region_2.3_spmd.clone, body=%wide.region_1.2_spmd.clone.sunk | while | flops 9871364 | bytes 289375 | solution.py:29
  295.0 1.5 scatter-add.80
  298.0 1.5 scatter-add.85
  302.5 2.4 scatter-add.91
  308.4 80.5 %all-gather.13.cloned.1.call-done = f32[5120,80]{1,0:T(8,128)} async-done(((f32[80,80]{1,0:T(8,128)}), f32[5120,80]{1,0:T(8,128)}) %all-gather.13.cloned.1.call-update) | async-done | bytes 1638416 | tf_op jit(solution)/shard_map/all_gather | solution.py:16
  388.8 84.2 %all-gather.15.cloned.1.call-done = f32[5120,128]{1,0:T(8,128)} async-done(((f32[80,128]{1,0:T(8,128)}), f32[5120,128]{1,0:T(8,128)}) %all-gather.15.cloned.1.call-update) | async-done | bytes 2621456 | tf_op jit(solution)/shard_map/all_gather | solution.py:16
  473.1 65.7 %while.51 = (s32[]{:T(128)}, f32[80,128]{1,0:T(8,128)S(1)}, s32[]{:T(128)}, f32[64,80,80]{2,1,0:T(8,128)}, f32[64,80,128]{2,1,0:T(8,128)}, /*index=5*/s32[]{:T(128)}, s32[]{:T(128)}, s32[]{:T(128)}, s32[]{:T(128)}) while((s32[]{:T(128)}, f32[80,128]{1,0:T(8,128)S(1)}, s32[]{:T(128)}, f32[64,80,80]{2,1,0:T(8,128)}, ...), condition=%wide.region_4.5_spmd.clone, body=%wide.region_3.4_spmd.clone.sunk | while | flops 9871368 | bytes 289437 | solution.py:29
  478.2 1.0 fusion.172
  479.2 1.0 fusion.172
  480.2 1.0 fusion.172
  540.2 1.5 scatter-add.99
  (379 shorter events, 140.0 us)
Async XLA Ops:
  6.5 6.7 %copy-start = (f32[64,320]{1,0:T(8,128)S(1)}, f32[64,320]{1,0:T(8,128)}, u32[]{:S(2)}) copy-start(f32[64,320]{1,0:T(8,128)} %param.56) | copy-start | bytes 245764
  6.5 43.9 %copy-start.1 = (f32[2,320,320]{2,1,0:T(8,128)S(1)}, f32[2,320,320]{2,1,0:T(8,128)}, u32[]{:S(2)}) copy-start(f32[2,320,320]{2,1,0:T(8,128)} %param.52) | copy-start | bytes 2457604
  6.5 138.1 %all-gather.9.cloned.1.call-start = ((), (), s32[]{:S(2)}) async-start(), calls=%async_computation | async-start | bytes 2662400 | tf_op jit(solution)/shard_map/all_gather | solution.py:16
  47.8 5.8 %copy-start.2 = (f32[2,80,240]{2,1,0:T(8,128)S(1)}, f32[2,80,240]{2,1,0:T(8,128)}, u32[]{:S(2)}) copy-start(f32[2,80,240]{2,1,0:T(8,128)} %param.53) | copy-start | bytes 460804
  59.7 169.3 %all-gather.11.cloned.1.call-start = ((), (), s32[]{:S(2)}) async-start(), calls=%async_computation.1 | async-start | bytes 2662400 | tf_op jit(solution)/shard_map/all_gather | solution.py:16
  60.4 328.4 %all-gather.13.cloned.1.call-start = ((), (), s32[]{:S(2)}) async-start(), calls=%async_computation.2 | async-start | bytes 2662400 | tf_op jit(solution)/shard_map/all_gather | solution.py:16
  297.6 3.6 copy-start.3
  307.7 165.4 %all-gather.15.cloned.1.call-start = ((), (), s32[]{:S(2)}) async-start(), calls=%async_computation.3 | async-start | bytes 2662400 | tf_op jit(solution)/shard_map/all_gather | solution.py:16
Sparse Core Ops, SparseCore 0:
  59.8 84.8 all-gather.8
  148.0 80.9 all-gather.10
  307.8 81.0 all-gather.12
  392.0 81.0 all-gather.14
where the time goes:
time: 560 us; the launch traced here: 550 us
  waiting for transfers between devices  327 us (58%)
  matrix products  139 us (25%)
  blocking collectives  30.4 us (5%)
  between operations  22.4 us (4%)
  local copies, waits for them, and re-layouts  21 us (4%)
    all_gather x4, waiting for transfers between devices, prefix(): everything = jax.tree.map(lambda part: lax.all_gather(part, axis), value)  327 us
    dot_general x158, matrix products, matmul(): jnp.dot(operand_a, operand_b, precision=PRECISE, preferred_element_type=j...  139 us
    unnamed x1, blocking collectives  30.4 us
    scatter-add x10, local copies, waits for them, and re-layouts, put_face(): return cubed.at[tuple(position)].add(face_plane).reshape(values.shape)  11.9 us
  transfers between devices with their start and end apart: 4, of which 4 were waited for; matrix products, arithmetic and copies ran while one was open for 0% of the time, Pallas kernels for 0%

commit v1 on v0

v1 whole, which is shorter than its diff:
```python
import functools

import jax
import jax.numpy as jnp
from jax import lax
from jax.experimental import pallas as pl
from jax.experimental.pallas import tpu as pltpu
from jax.sharding import PartitionSpec as P

TRACE = 80
BLOCK = 320
COLUMNS = 128
PLANE = 16
CUBE = 64
HALF = 128
F32 = jnp.float32
BF16 = jnp.bfloat16
VMEM = pl.BlockSpec(memory_space=pltpu.VMEM)
SMEM = pl.BlockSpec(memory_space=pltpu.SMEM)


def split(value):
    high = value.astype(BF16)
    return high, (value - high.astype(F32)).astype(BF16)


def dot(left, right):
    return jnp.dot(left, right, preferred_element_type=F32)


def product(left, right):
    return dot(left[0], right[0]) + (dot(left[0], right[1]) + dot(left[1], right[0]))


def select_rows(onehot, value):
    return dot(onehot, value[0]), dot(onehot, value[1])


def wake_kernel(target_ref, rows_ref, out_ref):
    ids = lax.broadcasted_iota(jnp.int32, (out_ref.shape[0], target_ref.shape[1]), 0)
    onehot = jnp.where(ids == target_ref[...], 1.0, 0.0).astype(BF16)
    high, low = split(rows_ref[...])
    out_ref[...] = dot(onehot, high) + dot(onehot, low)


def face_block(ref, element, face):
    return ref[element, :, face * TRACE : (face + 1) * TRACE]


def rows_of(slots, transposed):
    shape = (1, 3 * TRACE) if transposed else (3 * TRACE, 1)
    place = lax.broadcasted_iota(jnp.int32, shape, 1 if transposed else 0)
    which = jnp.where(place >= 2 * TRACE, 2, jnp.where(place >= TRACE, 1, 0))
    trace = place - which * TRACE
    field, upper, lower = trace >> 4, (trace >> 2) & 3, trace & 3
    side = 3 * (slots[0] % 2)
    row = jnp.where(
        which == 0,
        side * 16 + upper * 4 + lower,
        jnp.where(which == 1, upper * 16 + side * 4 + lower, upper * 16 + lower * 4 + side),
    )
    row = field * CUBE + row
    whole = (BLOCK, 3 * TRACE) if transposed else (3 * TRACE, BLOCK)
    rows = lax.broadcasted_iota(jnp.int32, whole, 0 if transposed else 1)
    return jnp.where(rows == row, 1.0, 0.0).astype(BF16)


def last_plane(value):
    return jnp.concatenate(
        [value[at + CUBE - PLANE : at + CUBE] for at in range(0, BLOCK, CUBE)], axis=0
    )


def pack(first, second, third, fourth):
    lead = TRACE
    spare = HALF - lead
    mid = third[:, :HALF]
    return jnp.concatenate(
        [
            first[:, :lead],
            mid[:, :spare],
            first[:, HALF:],
            fourth[:, :lead],
            mid[:, spare:lead],
            jnp.zeros((TRACE, 2 * spare - lead), F32),
            third[:, HALF:],
        ],
        axis=1,
    )


def unpack(value):
    lead = TRACE
    spare = HALF - lead
    zeros = jnp.zeros((TRACE, spare), F32)
    forward = value[:, : 2 * HALF]
    mixed = jnp.concatenate(
        [
            value[:, lead:HALF],
            value[:, 2 * HALF + lead : 2 * HALF + lead + (lead - spare)],
            zeros,
            value[:, 3 * HALF :],
        ],
        axis=1,
    )
    return forward, mixed, value[:, 2 * HALF : 2 * HALF + lead]


def local_kernel(upwind_ref, rhs_ref, inv_ref, low_ref, up_ref, wake_ref, total_ref, keep_ref):
    put_even = rows_of((0, 2, 4), True)
    take_even = rows_of((0, 2, 4), False)
    put_odd = rows_of((1, 3, 5), True)
    take_odd = rows_of((1, 3, 5), False)
    ones = jnp.ones((wake_ref.shape[1], COLUMNS), BF16)

    def source(element):
        high, low = split(wake_ref[element])
        dims = (((0,), (0,)), ((), ()))
        wake = lax.dot_general(high, ones, dims, preferred_element_type=F32)
        wake += lax.dot_general(low, ones, dims, preferred_element_type=F32)
        return rhs_ref[element] + wake

    inverse = [split(inv_ref[0]), split(inv_ref[1])]
    crosses = [upwind_ref[1, face] == 2 for face in range(3)]
    zeros_low = jnp.zeros((TRACE, HALF - TRACE), F32)
    eye = jnp.where(
        lax.broadcasted_iota(jnp.int32, (TRACE, 2 * HALF), 0)
        == lax.broadcasted_iota(jnp.int32, (TRACE, 2 * HALF), 1),
        1.0,
        0.0,
    )

    stacked = jnp.concatenate([face_block(low_ref, 0, face) for face in range(3)], axis=0)
    stacked = jnp.concatenate([stacked, jnp.zeros((3 * TRACE, HALF - TRACE), F32)], axis=1)
    spread = sum(select_rows(put_even, split(stacked)))
    first = product(inverse[0], split(jnp.concatenate([-spread, source(0)], axis=1)))

    traced = select_rows(take_odd, split(first))
    coupled = []
    for face in range(3):
        at = slice(face * TRACE, (face + 1) * TRACE)
        high = jnp.where(crosses[face], eye, traced[0][at]).astype(BF16)
        lows = jnp.where(crosses[face], 0.0, traced[1][at]).astype(BF16)
        coupled.append(product(split(face_block(low_ref, 1, face)), (high, lows)))
    spread = sum(select_rows(put_even, split(jnp.concatenate(coupled, axis=0))))
    base = jnp.concatenate([jnp.zeros((BLOCK, HALF), F32), source(1)], axis=1)
    second = product(inverse[1], split(base - spread))
    forward = last_plane(second)

    side = put_odd[:, :HALF]
    returned = -(dot(inverse[1][0], side) + dot(inverse[1][1], side))
    lane = lax.broadcasted_iota(jnp.int32, (BLOCK, HALF), 1)
    returned = jnp.where(lane < TRACE, returned, 0.0)
    second = jnp.concatenate([second, returned], axis=1)
    keep_ref[1] = second
    traced = select_rows(take_even, split(second))
    outgoing = jnp.zeros((TRACE, 3 * HALF), F32)
    coupled = []
    for face in range(3):
        at = slice(face * TRACE, (face + 1) * TRACE)
        pair = (traced[0][at].astype(BF16), traced[1][at].astype(BF16))
        value = product(split(face_block(up_ref, 1, face)), pair)
        outgoing += jnp.where(crosses[face], value, 0.0)
        coupled.append(jnp.where(crosses[face], 0.0, value))
    spread = sum(select_rows(put_odd, split(jnp.concatenate(coupled, axis=0))))
    first = jnp.concatenate([first, jnp.zeros((BLOCK, HALF), F32)], axis=1)
    first = first - product(inverse[0], split(spread))
    keep_ref[0] = first
    traced = select_rows(take_even, split(first))
    pair = (traced[0].astype(BF16), traced[1].astype(BF16))
    outgoing += product(split(up_ref[0]), pair)
    total_ref[...] = pack(forward, None, outgoing[:, : 2 * HALF], outgoing[:, 2 * HALF :])


def is_upper(level):
    return (lax.axis_index("stream") >> level) & 1


def ordered(level, mine_ref, other_ref):
    upper = is_upper(level) == 1
    mine, other = mine_ref[...], other_ref[...]
    return unpack(jnp.where(upper, other, mine)), unpack(jnp.where(upper, mine, other))


def combine_kernel(level, mine_ref, other_ref, total_ref, cross_ref):
    (forward1, mixed1, back1), (forward2, mixed2, back2) = ordered(level, mine_ref, other_ref)
    lane = lax.broadcasted_iota(jnp.int32, (TRACE, 2 * HALF), 1)
    columns = lane >= HALF
    clean = columns | (lane < TRACE)
    forward_pair = split(jnp.where(clean, forward1, 0.0))
    cross = product(split(mixed2[:, :TRACE]), forward_pair) + jnp.where(columns, mixed2, 0.0)
    forward = product(split(forward2[:, :TRACE]), forward_pair)
    forward = forward + jnp.where(columns, forward2, 0.0)
    back_pair = split(back1)
    mixed = mixed1 + product(back_pair, split(cross))
    back = product(back_pair, split(back2))
    total_ref[...] = pack(forward, None, mixed, back)
    cross_ref[...] = cross


def track_first_kernel(level, mine_ref, other_ref, cross_ref, state_ref):
    (forward1, _, _), (_, _, back2) = ordered(level, mine_ref, other_ref)
    upper = is_upper(level) == 1
    lane = lax.broadcasted_iota(jnp.int32, (TRACE, 2 * HALF), 1)
    row = lax.broadcasted_iota(jnp.int32, (TRACE, 2 * HALF), 0)
    eye = jnp.where(lane == row, 1.0, 0.0)
    clean = (lane >= HALF) | (lane < TRACE)
    state_ref[:, : 2 * HALF] = jnp.where(upper, jnp.where(clean, forward1, 0.0), eye)
    state_ref[:, 2 * HALF : 4 * HALF] = jnp.where(upper, 0.0, cross_ref[...])
    back2 = jnp.concatenate([back2, jnp.zeros((TRACE, HALF - TRACE), F32)], axis=1)
    state_ref[:, 4 * HALF :] = jnp.where(upper, eye[:, :HALF], back2)


def track_kernel(level, mine_ref, other_ref, cross_ref, old_ref, state_ref):
    lane = lax.broadcasted_iota(jnp.int32, (TRACE, 2 * HALF), 1)
    columns = lane >= HALF

    @pl.when(is_upper(level) == 1)
    def _():
        forward1 = jnp.where(columns | (lane < TRACE), other_ref[:, : 2 * HALF], 0.0)
        pair = split(forward1)
        here = old_ref[:, : 2 * HALF]
        back = old_ref[:, 2 * HALF : 4 * HALF]
        state_ref[:, : 2 * HALF] = product(split(here[:, :TRACE]), pair) + jnp.where(columns, here, 0.0)
        state_ref[:, 2 * HALF : 4 * HALF] = product(split(back[:, :TRACE]), pair) + jnp.where(columns, back, 0.0)
        state_ref[:, 4 * HALF :] = old_ref[:, 4 * HALF :]

    @pl.when(is_upper(level) == 0)
    def _():
        gain = split(old_ref[:, 4 * HALF : 4 * HALF + TRACE])
        back2 = jnp.where(lane[:, :HALF] < TRACE, other_ref[:, 2 * HALF : 3 * HALF], 0.0)
        state_ref[:, : 2 * HALF] = old_ref[:, : 2 * HALF]
        state_ref[:, 2 * HALF : 4 * HALF] = old_ref[:, 2 * HALF : 4 * HALF] + product(gain, split(cross_ref[...]))
        state_ref[:, 4 * HALF :] = product(gain, split(back2))


def last_kernel(level, mine_ref, other_ref, old_ref, keep_ref, out_ref, ends_ref):
    @pl.when(is_upper(level) == 1)
    def _():
        inflow = split(other_ref[:, HALF : 2 * HALF])
        ends_ref[0] = old_ref[:, HALF : 2 * HALF] + product(split(old_ref[:, :TRACE]), inflow)
        ends_ref[1] = old_ref[:, 3 * HALF : 4 * HALF] + product(split(old_ref[:, 2 * HALF : 2 * HALF + TRACE]), inflow)

    @pl.when(is_upper(level) == 0)
    def _():
        outflow = split(mine_ref[:, HALF : 2 * HALF])
        value = other_ref[:, HALF : 2 * HALF] + product(split(other_ref[:, :TRACE]), outflow)
        gain = split(old_ref[:, 4 * HALF : 4 * HALF + TRACE])
        ends_ref[0] = old_ref[:, HALF : 2 * HALF]
        ends_ref[1] = old_ref[:, 3 * HALF : 4 * HALF] + product(gain, split(value))

    inflow = split(ends_ref[0])
    incoming = split(ends_ref[1])
    for element in range(2):
        known = keep_ref[element]
        out_ref[element] = (
            known[:, HALF : 2 * HALF]
            + product(split(known[:, :TRACE]), inflow)
            + product(split(known[:, 2 * HALF : 2 * HALF + TRACE]), incoming)
        )


def call(kernel, shapes, operands, flops, scalars=0, scratch=()):
    moved = 4 * sum(v.size for v in operands) + 4 * sum(s.size for s in shapes)
    single = len(shapes) == 1
    return pl.pallas_call(
        kernel,
        out_shape=shapes[0] if single else shapes,
        in_specs=[SMEM] * scalars + [VMEM] * (len(operands) - scalars),
        out_specs=VMEM if single else [VMEM] * len(shapes),
        scratch_shapes=list(scratch),
        compiler_params=pltpu.CompilerParams(vmem_limit_bytes=40 * 1024 * 1024),
        cost_estimate=pl.CostEstimate(flops=flops, bytes_accessed=moved, transcendentals=0),
    )(*operands)


def shape(*dims):
    return jax.ShapeDtypeStruct(dims, F32)


PARTNERS = ((0, 0, 1), (0, 1, 0), (0, 2, 0), (0, 6, 0), (1, 0, 0), (3, 0, 0))


def exchange(value, level):
    across, along, core = PARTNERS[level]
    mask = (across * 8 + along) * 2 + core
    count = lax.axis_size("stream")
    return lax.ppermute(value, "stream", [(k, k ^ mask) for k in range(count)])


def shards(rhs, inverse, lower, upper, upwind, rows, target):
    groups = lax.axis_size("azi")
    local = rhs.shape[0]
    partial = call(wake_kernel, [shape(groups * local, BLOCK)], [target.reshape(1, -1), rows], 10**6)
    parts = lax.all_to_all(partial.reshape(groups, local, BLOCK), "azi", 0, 0)
    parts = jnp.swapaxes(parts, 0, 1)
    total, keep = call(
        local_kernel,
        [shape(TRACE, 4 * HALF), shape(local, BLOCK, 3 * HALF)],
        [upwind, rhs, inverse, lower, upper, parts],
        2 * 10**9,
        scalars=1,
    )
    state = None
    for level in range(5):
        other = exchange(total, level)
        merged, cross = call(
            functools.partial(combine_kernel, level),
            [shape(TRACE, 4 * HALF), shape(TRACE, 2 * HALF)],
            [total, other],
            2 * 10**7,
        )
        if level == 0:
            state = call(
                functools.partial(track_first_kernel, level),
                [shape(TRACE, 5 * HALF)],
                [total, other, cross],
                10**6,
            )
        else:
            state = call(
                functools.partial(track_kernel, level),
                [shape(TRACE, 5 * HALF)],
                [total, other, cross, state],
                10**7,
            )
        total = merged
    top = (lax.axis_index("stream") >> 5) & 1
    forward, mixed, _ = unpack(total)
    other = exchange(jnp.where(top == 1, mixed, forward), 5)
    return call(
        functools.partial(last_kernel, 5),
        [shape(local, BLOCK, COLUMNS)],
        [total, other, state, keep],
        10**8,
        scratch=[pltpu.VMEM((2, TRACE, COLUMNS), F32)],
    )


def solution(mesh):
    both = ("stream", "azi")
    return jax.shard_map(
        shards,
        mesh=mesh,
        in_specs=(
            P(both, None, None),
            P(both, None, None),
            P(both, None, None),
            P(both, None, None),
            P(both, None),
            P(both, None),
            P(both),
        ),
        out_specs=P(both, None, None),
        check_vma=False,
    )
```

time: 560 us -> 83.2 us (0.15)
  the two profiles are of different devices: /device:TPU:6 before, /device:TPU:64 now
where the time goes in v1:
time: 83.2 us; the launch traced here: 82.7 us
  starting transfers between devices  27.8 us (33%)
  waiting for transfers between devices  23.7 us (28%)
  blocking collectives  14.7 us (18%)
  Pallas kernels  10.6 us (13%)
  local copies, waits for them, and re-layouts  5.57 us (7%)
    ppermute x6, starting transfers between devices, exchange(): return lax.ppermute(value, 'stream', [(k, k ^ mask) for k in range(count)])  27.8 us
    ppermute x6, waiting for transfers between devices, exchange(): return lax.ppermute(value, 'stream', [(k, k ^ mask) for k in range(count)])  23.7 us
    all_to_all x1, blocking collectives, shards(): parts = lax.all_to_all(partial.reshape(groups, local, BLOCK), 'azi', 0, 0)  14.7 us
    pallas_call x13, Pallas kernels, call(): pl.pallas_call(kernel, out_shape=shapes[0] if single else shapes, in_spec...  10.6 us
    unnamed x14, local copies, waits for them, and re-layouts  5.31 us
  transfers between devices with their start and end apart: 6, of which 6 were waited for; matrix products, arithmetic and copies ran while one was open for 0% of the time, Pallas kernels for 1%

profile of v1, /device:TPU:64, one launch (start us, length us, event | category | flops | bytes accessed | tf_op | source)
XLA Modules:
  0.0 82.7 jit_solution(1454974009908631345)
XLA Ops:
  0.0 0.7 copy-done.1
  0.7 0.9 %copy-done = f32[64,320]{1,0:T(8,128)S(1)} copy-done((f32[64,320]{1,0:T(8,128)S(1)}, f32[64,320]{1,0:T(8,128)}, u32[]{:S(2)}) %copy-start) | copy-done | bytes 81944
  1.7 14.7 %all_to_all.5 = f32[8,2,320]{2,1,0:T(2,128)S(1)} all-to-all(f32[8,2,320]{2,1,0:T(2,128)S(1)} %reshape.7), channel_id=1, replica_groups=mesh['stream'=64,'azi'=8] {'azi'}, dimensions={0} | all-to-all | bytes 40960 | tf_op jit(solution)/shard_map/all_to_all | solution.py:295
  16.4 0.7 copy-done.6
  17.1 1.2 %copy-done.2 = f32[2,320,320]{2,1,0:T(8,128)S(1)} copy-done((f32[2,320,320]{2,1,0:T(8,128)S(1)}, f32[2,320,320]{2,1,0:T(8,128)}, u32[]{:S(2)}) %copy-start.2) | copy-done | bytes 819224
  18.3 1.0 %copy-done.3 = f32[2,320,128]{2,1,0:T(8,128)S(1)} copy-done((f32[2,320,128]{2,1,0:T(8,128)S(1)}, f32[2,320,128]{2,1,0:T(8,128)}, u32[]{:S(2)}) %copy-start.3) | copy-done | bytes 327704
  19.3 0.9 %copy-done.5 = f32[2,80,240]{2,1,0:T(8,128)S(1)} copy-done((f32[2,80,240]{2,1,0:T(8,128)S(1)}, f32[2,80,240]{2,1,0:T(8,128)}, u32[]{:S(2)}) %copy-start.5) | copy-done | bytes 153624
  20.2 5.5 %shard_map.74 = (f32[80,512]{1,0:T(8,128)S(1)}, f32[2,320,384]{2,1,0:T(8,128)S(1)}) custom-call(s32[2,3]{1,0:T(2,128)S(1)} %copy-done.6, f32[2,320,128]{2,1,0:T(8,128)S(1)} %copy-done.3, f32[2,320,320]{2,1,0:T(8,128)S(1)} %copy-done.2, f32[2,80,240]{2,1,0:T(8,128)S(1)} %copy-done.4, f32[2,80,240]{2,1,0:T(8,128)S(1)} %copy-done.5, f32[2,8,320]{2,1,0:T(8,128)S(1)} %bitcast.4), custom_call_target="tpu_custom_call" | custom-call | flops 2000000000 | bytes 2621464 | tf_op jit(solution)/shard_map/pallas_call | solution.py:266
  25.7 1.9 %collective-permute-start = (f32[80,512]{1,0:T(8,128)S(1)}, f32[80,512]{1,0:T(8,128)S(1)}, u32[]{:S(2)}, u32[]{:S(2)}) collective-permute-start(f32[80,512]{1,0:T(8,128)S(1)} %get-tuple-element.17.mine_ref), channel_id=1, source_target_pairs={{0,8},{8,0},{16,24},{24,16},{32,40},{40,32},{48,56},{56,48},{64,72... | collective-permute-start | bytes 491528 | tf_op jit(solution)/shard_map/ppermute | solution.py:288
  27.6 1.4 %collective-permute-done.other_ref = f32[80,512]{1,0:T(8,128)S(1)} collective-permute-done((f32[80,512]{1,0:T(8,128)S(1)}, f32[80,512]{1,0:T(8,128)S(1)}, u32[]{:S(2)}, u32[]{:S(2)}) %collective-permute-start) | collective-permute-done | bytes 163872 | tf_op jit(solution)/shard_map/ppermute | solution.py:288
  29.0 0.5 shard_map.75
  29.5 2.5 %collective-permute-start.1 = (f32[80,512]{1,0:T(8,128)S(1)}, f32[80,512]{1,0:T(8,128)S(1)}, u32[]{:S(2)}, u32[]{:S(2)}) collective-permute-start(f32[80,512]{1,0:T(8,128)S(1)} %get-tuple-element.18.mine_ref), channel_id=1, source_target_pairs={{0,16},{8,24},{16,0},{24,8},{32,48},{40,56},{48,32},{56,40},{64,80... | collective-permute-start | bytes 491528 | tf_op jit(solution)/shard_map/ppermute | solution.py:288
  32.1 5.6 %collective-permute-done.1.other_ref = f32[80,512]{1,0:T(8,128)S(1)} collective-permute-done((f32[80,512]{1,0:T(8,128)S(1)}, f32[80,512]{1,0:T(8,128)S(1)}, u32[]{:S(2)}, u32[]{:S(2)}) %collective-permute-start.1) | collective-permute-done | bytes 163872 | tf_op jit(solution)/shard_map/ppermute | solution.py:288
  37.7 0.5 shard_map.76
  38.2 6.1 %collective-permute-start.2 = (f32[80,512]{1,0:T(8,128)S(1)}, f32[80,512]{1,0:T(8,128)S(1)}, u32[]{:S(2)}, u32[]{:S(2)}) collective-permute-start(f32[80,512]{1,0:T(8,128)S(1)} %get-tuple-element.19.mine_ref), channel_id=1, source_target_pairs={{0,32},{8,40},{16,48},{24,56},{32,0},{40,8},{48,16},{56,24},{64,96... | collective-permute-start | bytes 491528 | tf_op jit(solution)/shard_map/ppermute | solution.py:288
  44.3 6.4 %collective-permute-done.2.other_ref = f32[80,512]{1,0:T(8,128)S(1)} collective-permute-done((f32[80,512]{1,0:T(8,128)S(1)}, f32[80,512]{1,0:T(8,128)S(1)}, u32[]{:S(2)}, u32[]{:S(2)}) %collective-permute-start.2) | collective-permute-done | bytes 163872 | tf_op jit(solution)/shard_map/ppermute | solution.py:288
  51.2 9.2 %collective-permute-start.3 = (f32[80,512]{1,0:T(8,128)S(1)}, f32[80,512]{1,0:T(8,128)S(1)}, u32[]{:S(2)}, u32[]{:S(2)}) collective-permute-start(f32[80,512]{1,0:T(8,128)S(1)} %get-tuple-element.20.mine_ref), channel_id=1, source_target_pairs={{0,96},{8,104},{16,112},{24,120},{32,64},{40,72},{48,80},{56,88},{... | collective-permute-start | bytes 491528 | tf_op jit(solution)/shard_map/ppermute | solution.py:288
  60.5 4.4 %collective-permute-done.3.other_ref = f32[80,512]{1,0:T(8,128)S(1)} collective-permute-done((f32[80,512]{1,0:T(8,128)S(1)}, f32[80,512]{1,0:T(8,128)S(1)}, u32[]{:S(2)}, u32[]{:S(2)}) %collective-permute-start.3) | collective-permute-done | bytes 163872 | tf_op jit(solution)/shard_map/ppermute | solution.py:288
  64.9 0.5 shard_map.78
  65.4 3.4 %collective-permute-start.4 = (f32[80,512]{1,0:T(8,128)S(1)}, f32[80,512]{1,0:T(8,128)S(1)}, u32[]{:S(2)}, u32[]{:S(2)}) collective-permute-start(f32[80,512]{1,0:T(8,128)S(1)} %get-tuple-element.21.mine_ref), channel_id=1, source_target_pairs={{0,128},{8,136},{16,144},{24,152},{32,160},{40,168},{48,176},{56,1... | collective-permute-start | bytes 491528 | tf_op jit(solution)/shard_map/ppermute | solution.py:288
  68.9 4.0 %collective-permute-done.4.other_ref = f32[80,512]{1,0:T(8,128)S(1)} collective-permute-done((f32[80,512]{1,0:T(8,128)S(1)}, f32[80,512]{1,0:T(8,128)S(1)}, u32[]{:S(2)}, u32[]{:S(2)}) %collective-permute-start.4) | collective-permute-done | bytes 163872 | tf_op jit(solution)/shard_map/ppermute | solution.py:288
  73.7 4.7 %collective-permute-start.5 = (f32[80,256]{1,0:T(8,128)S(1)}, f32[80,256]{1,0:T(8,128)S(1)}, u32[]{:S(2)}, u32[]{:S(2)}) collective-permute-start(f32[80,256]{1,0:T(8,128)S(1)} %maximum_select_fusion), channel_id=1, source_target_pairs={{0,384},{8,392},{16,400},{24,408},{32,416},{40,424},{48,432},{56,4... | collective-permute-start | bytes 245768 | tf_op jit(solution)/shard_map/ppermute | solution.py:288
  79.3 1.9 %collective-permute-done.5.other_ref = f32[80,256]{1,0:T(8,128)S(1)} collective-permute-done((f32[80,256]{1,0:T(8,128)S(1)}, f32[80,256]{1,0:T(8,128)S(1)}, u32[]{:S(2)}, u32[]{:S(2)}) %collective-permute-start.5) | collective-permute-done | bytes 81952 | tf_op jit(solution)/shard_map/ppermute | solution.py:288
  81.3 1.5 %shard_map.85 = f32[2,320,128]{2,1,0:T(8,128)} custom-call(f32[80,512]{1,0:T(8,128)S(1)} %get-tuple-element.22.mine_ref, f32[80,256]{1,0:T(8,128)S(1)} %collective-permute-done.5.other_ref, f32[80,640]{1,0:T(8,128)S(1)} %shard_map.84.old_ref, f32[2,320,384]{2,1,0:T(8,128)S(1)} %get-tuple-element.28.keep_ref), custom_call_target="tpu_custom_call" | custom-call | flops 100000000 | bytes 1761280 | tf_op jit(solution)/shard_map/pallas_call | solution.py:266
  (24 shorter events, 2.5 us)
Async XLA Ops:
  0.0 0.7 copy-start.1
  0.7 0.9 %copy-start = (f32[64,320]{1,0:T(8,128)S(1)}, f32[64,320]{1,0:T(8,128)}, u32[]{:S(2)}) copy-start(f32[64,320]{1,0:T(8,128)} %rows_ref.1) | copy-start | bytes 245764
  1.5 14.9 %copy-start.4 = (f32[2,80,240]{2,1,0:T(8,128)S(1)}, f32[2,80,240]{2,1,0:T(8,128)}, u32[]{:S(2)}) copy-start(f32[2,80,240]{2,1,0:T(8,128)} %low_ref.1) | copy-start | bytes 460804
  16.4 0.7 copy-start.6
  17.1 1.2 %copy-start.2 = (f32[2,320,320]{2,1,0:T(8,128)S(1)}, f32[2,320,320]{2,1,0:T(8,128)}, u32[]{:S(2)}) copy-start(f32[2,320,320]{2,1,0:T(8,128)} %inv_ref.1) | copy-start | bytes 2457604
  18.3 1.0 %copy-start.3 = (f32[2,320,128]{2,1,0:T(8,128)S(1)}, f32[2,320,128]{2,1,0:T(8,128)}, u32[]{:S(2)}) copy-start(f32[2,320,128]{2,1,0:T(8,128)} %rhs_ref.1) | copy-start | bytes 983044
  19.3 0.9 %copy-start.5 = (f32[2,80,240]{2,1,0:T(8,128)S(1)}, f32[2,80,240]{2,1,0:T(8,128)}, u32[]{:S(2)}) copy-start(f32[2,80,240]{2,1,0:T(8,128)} %up_ref.1) | copy-start | bytes 460804
  25.7 3.3 %collective-permute-start = (f32[80,512]{1,0:T(8,128)S(1)}, f32[80,512]{1,0:T(8,128)S(1)}, u32[]{:S(2)}, u32[]{:S(2)}) collective-permute-start(f32[80,512]{1,0:T(8,128)S(1)} %get-tuple-element.17.mine_ref), channel_id=1, source_target_pairs={{0,8},{8,0},{16,24},{24,16},{32,40},{40,32},{48,56},{56,48},{64,72... | collective-permute-start | bytes 491528 | tf_op jit(solution)/shard_map/ppermute | solution.py:288
  29.5 8.1 %collective-permute-start.1 = (f32[80,512]{1,0:T(8,128)S(1)}, f32[80,512]{1,0:T(8,128)S(1)}, u32[]{:S(2)}, u32[]{:S(2)}) collective-permute-start(f32[80,512]{1,0:T(8,128)S(1)} %get-tuple-element.18.mine_ref), channel_id=1, source_target_pairs={{0,16},{8,24},{16,0},{24,8},{32,48},{40,56},{48,32},{56,40},{64,80... | collective-permute-start | bytes 491528 | tf_op jit(solution)/shard_map/ppermute | solution.py:288
  38.2 12.5 %collective-permute-start.2 = (f32[80,512]{1,0:T(8,128)S(1)}, f32[80,512]{1,0:T(8,128)S(1)}, u32[]{:S(2)}, u32[]{:S(2)}) collective-permute-start(f32[80,512]{1,0:T(8,128)S(1)} %get-tuple-element.19.mine_ref), channel_id=1, source_target_pairs={{0,32},{8,40},{16,48},{24,56},{32,0},{40,8},{48,16},{56,24},{64,96... | collective-permute-start | bytes 491528 | tf_op jit(solution)/shard_map/ppermute | solution.py:288
  51.2 13.6 %collective-permute-start.3 = (f32[80,512]{1,0:T(8,128)S(1)}, f32[80,512]{1,0:T(8,128)S(1)}, u32[]{:S(2)}, u32[]{:S(2)}) collective-permute-start(f32[80,512]{1,0:T(8,128)S(1)} %get-tuple-element.20.mine_ref), channel_id=1, source_target_pairs={{0,96},{8,104},{16,112},{24,120},{32,64},{40,72},{48,80},{56,88},{... | collective-permute-start | bytes 491528 | tf_op jit(solution)/shard_map/ppermute | solution.py:288
  65.4 7.5 %collective-permute-start.4 = (f32[80,512]{1,0:T(8,128)S(1)}, f32[80,512]{1,0:T(8,128)S(1)}, u32[]{:S(2)}, u32[]{:S(2)}) collective-permute-start(f32[80,512]{1,0:T(8,128)S(1)} %get-tuple-element.21.mine_ref), channel_id=1, source_target_pairs={{0,128},{8,136},{16,144},{24,152},{32,160},{40,168},{48,176},{56,1... | collective-permute-start | bytes 491528 | tf_op jit(solution)/shard_map/ppermute | solution.py:288
  73.7 7.5 %collective-permute-start.5 = (f32[80,256]{1,0:T(8,128)S(1)}, f32[80,256]{1,0:T(8,128)S(1)}, u32[]{:S(2)}, u32[]{:S(2)}) collective-permute-start(f32[80,256]{1,0:T(8,128)S(1)} %maximum_select_fusion), channel_id=1, source_target_pairs={{0,384},{8,392},{16,400},{24,408},{32,416},{40,424},{48,432},{56,4... | collective-permute-start | bytes 245768 | tf_op jit(solution)/shard_map/ppermute | solution.py:288

commit v2 on v1

--- a/solution.py
+++ b/solution.py
@@ -17,6 +17,7 @@
 BF16 = jnp.bfloat16
 VMEM = pl.BlockSpec(memory_space=pltpu.VMEM)
 SMEM = pl.BlockSpec(memory_space=pltpu.SMEM)
+HBM = pl.BlockSpec(memory_space=pltpu.HBM)
 
 
 def split(value):
@@ -36,7 +37,16 @@
     return dot(onehot, value[0]), dot(onehot, value[1])
 
 
-def wake_kernel(target_ref, rows_ref, out_ref):
+def fetch(sources, buffers, sems):
+    copies = [pltpu.make_async_copy(a, b, sems.at[i]) for i, (a, b) in enumerate(zip(sources, buffers))]
+    for copy in copies:
+        copy.start()
+    return copies
+
+
+def wake_kernel(target_hbm, rows_hbm, out_ref, target_ref, rows_ref, sems):
+    for copy in fetch((target_hbm, rows_hbm), (target_ref, rows_ref), sems):
+        copy.wait()
     ids = lax.broadcasted_iota(jnp.int32, (out_ref.shape[0], target_ref.shape[1]), 0)
     onehot = jnp.where(ids == target_ref[...], 1.0, 0.0).astype(BF16)
     high, low = split(rows_ref[...])
@@ -106,7 +116,27 @@
     return forward, mixed, value[:, 2 * HALF : 2 * HALF + lead]
 
 
-def local_kernel(upwind_ref, rhs_ref, inv_ref, low_ref, up_ref, wake_ref, total_ref, keep_ref):
+def local_kernel(
+    upwind_ref,
+    wake_ref,
+    low_hbm,
+    inv_hbm,
+    rhs_hbm,
+    up_hbm,
+    total_ref,
+    keep_ref,
+    low_ref,
+    first_inv_ref,
+    second_inv_ref,
+    rhs_ref,
+    up_ref,
+    sems,
+):
+    copies = fetch(
+        (low_hbm, rhs_hbm, inv_hbm.at[0], inv_hbm.at[1], up_hbm),
+        (low_ref, rhs_ref, first_inv_ref, second_inv_ref, up_ref),
+        sems,
+    )
     put_even = rows_of((0, 2, 4), True)
     take_even = rows_of((0, 2, 4), False)
     put_odd = rows_of((1, 3, 5), True)
@@ -120,7 +150,6 @@
         wake += lax.dot_general(low, ones, dims, preferred_element_type=F32)
         return rhs_ref[element] + wake
 
-    inverse = [split(inv_ref[0]), split(inv_ref[1])]
     crosses = [upwind_ref[1, face] == 2 for face in range(3)]
     zeros_low = jnp.zeros((TRACE, HALF - TRACE), F32)
     eye = jnp.where(
@@ -130,10 +159,14 @@
         0.0,
     )
 
+    copies[0].wait()
     stacked = jnp.concatenate([face_block(low_ref, 0, face) for face in range(3)], axis=0)
     stacked = jnp.concatenate([stacked, jnp.zeros((3 * TRACE, HALF - TRACE), F32)], axis=1)
     spread = sum(select_rows(put_even, split(stacked)))
-    first = product(inverse[0], split(jnp.concatenate([-spread, source(0)], axis=1)))
+    copies[1].wait()
+    copies[2].wait()
+    inverse = split(first_inv_ref[...])
+    first = product(inverse, split(jnp.concatenate([-spread, source(0)], axis=1)))
 
     traced = select_rows(take_odd, split(first))
     coupled = []
@@ -144,16 +177,19 @@
         coupled.append(product(split(face_block(low_ref, 1, face)), (high, lows)))
     spread = sum(select_rows(put_even, split(jnp.concatenate(coupled, axis=0))))
     base = jnp.concatenate([jnp.zeros((BLOCK, HALF), F32), source(1)], axis=1)
-    second = product(inverse[1], split(base - spread))
+    copies[3].wait()
+    later_inverse = split(second_inv_ref[...])
+    second = product(later_inverse, split(base - spread))
     forward = last_plane(second)
 
     side = put_odd[:, :HALF]
-    returned = -(dot(inverse[1][0], side) + dot(inverse[1][1], side))
+    returned = -(dot(later_inverse[0], side) + dot(later_inverse[1], side))
     lane = lax.broadcasted_iota(jnp.int32, (BLOCK, HALF), 1)
     returned = jnp.where(lane < TRACE, returned, 0.0)
     second = jnp.concatenate([second, returned], axis=1)
     keep_ref[1] = second
     traced = select_rows(take_even, split(second))
+    copies[4].wait()
     outgoing = jnp.zeros((TRACE, 3 * HALF), F32)
     coupled = []
     for face in range(3):
@@ -164,7 +200,7 @@
         coupled.append(jnp.where(crosses[face], 0.0, value))
     spread = sum(select_rows(put_odd, split(jnp.concatenate(coupled, axis=0))))
     first = jnp.concatenate([first, jnp.zeros((BLOCK, HALF), F32)], axis=1)
-    first = first - product(inverse[0], split(spread))
+    first = first - product(inverse, split(spread))
     keep_ref[0] = first
     traced = select_rows(take_even, split(first))
     pair = (traced[0].astype(BF16), traced[1].astype(BF16))
@@ -176,14 +212,9 @@
     return (lax.axis_index("stream") >> level) & 1
 
 
-def ordered(level, mine_ref, other_ref):
-    upper = is_upper(level) == 1
-    mine, other = mine_ref[...], other_ref[...]
-    return unpack(jnp.where(upper, other, mine)), unpack(jnp.where(upper, mine, other))
-
-
-def combine_kernel(level, mine_ref, other_ref, total_ref, cross_ref):
-    (forward1, mixed1, back1), (forward2, mixed2, back2) = ordered(level, mine_ref, other_ref)
+def combine_kernel(last, pair_ref, total_ref, cross_ref):
+    forward1, mixed1, back1 = unpack(pair_ref[0])
+    forward2, mixed2, back2 = unpack(pair_ref[1])
     lane = lax.broadcasted_iota(jnp.int32, (TRACE, 2 * HALF), 1)
     columns = lane >= HALF
     clean = columns | (lane < TRACE)
@@ -193,31 +224,32 @@
     forward = forward + jnp.where(columns, forward2, 0.0)
     back_pair = split(back1)
     mixed = mixed1 + product(back_pair, split(cross))
-    back = product(back_pair, split(back2))
-    total_ref[...] = pack(forward, None, mixed, back)
+    if last:
+        total_ref[...] = jnp.where(is_upper(last) == 1, mixed, forward)
+    else:
+        total_ref[...] = pack(forward, None, mixed, product(back_pair, split(back2)))
     cross_ref[...] = cross
 
 
-def track_first_kernel(level, mine_ref, other_ref, cross_ref, state_ref):
-    (forward1, _, _), (_, _, back2) = ordered(level, mine_ref, other_ref)
+def track_first_kernel(level, pair_ref, cross_ref, state_ref):
     upper = is_upper(level) == 1
     lane = lax.broadcasted_iota(jnp.int32, (TRACE, 2 * HALF), 1)
     row = lax.broadcasted_iota(jnp.int32, (TRACE, 2 * HALF), 0)
     eye = jnp.where(lane == row, 1.0, 0.0)
-    clean = (lane >= HALF) | (lane < TRACE)
-    state_ref[:, : 2 * HALF] = jnp.where(upper, jnp.where(clean, forward1, 0.0), eye)
+    forward1 = jnp.where((lane >= HALF) | (lane < TRACE), pair_ref[0, :, : 2 * HALF], 0.0)
+    back2 = jnp.where(lane[:, :HALF] < TRACE, pair_ref[1, :, 2 * HALF : 3 * HALF], 0.0)
+    state_ref[:, : 2 * HALF] = jnp.where(upper, forward1, eye)
     state_ref[:, 2 * HALF : 4 * HALF] = jnp.where(upper, 0.0, cross_ref[...])
-    back2 = jnp.concatenate([back2, jnp.zeros((TRACE, HALF - TRACE), F32)], axis=1)
     state_ref[:, 4 * HALF :] = jnp.where(upper, eye[:, :HALF], back2)
 
 
-def track_kernel(level, mine_ref, other_ref, cross_ref, old_ref, state_ref):
+def track_kernel(level, pair_ref, cross_ref, old_ref, state_ref):
     lane = lax.broadcasted_iota(jnp.int32, (TRACE, 2 * HALF), 1)
     columns = lane >= HALF
 
     @pl.when(is_upper(level) == 1)
     def _():
-        forward1 = jnp.where(columns | (lane < TRACE), other_ref[:, : 2 * HALF], 0.0)
+        forward1 = jnp.where(columns | (lane < TRACE), pair_ref[0, :, : 2 * HALF], 0.0)
         pair = split(forward1)
         here = old_ref[:, : 2 * HALF]
         back = old_ref[:, 2 * HALF : 4 * HALF]
@@ -228,23 +260,23 @@
     @pl.when(is_upper(level) == 0)
     def _():
         gain = split(old_ref[:, 4 * HALF : 4 * HALF + TRACE])
-        back2 = jnp.where(lane[:, :HALF] < TRACE, other_ref[:, 2 * HALF : 3 * HALF], 0.0)
+        back2 = jnp.where(lane[:, :HALF] < TRACE, pair_ref[1, :, 2 * HALF : 3 * HALF], 0.0)
         state_ref[:, : 2 * HALF] = old_ref[:, : 2 * HALF]
         state_ref[:, 2 * HALF : 4 * HALF] = old_ref[:, 2 * HALF : 4 * HALF] + product(gain, split(cross_ref[...]))
         state_ref[:, 4 * HALF :] = product(gain, split(back2))
 
 
-def last_kernel(level, mine_ref, other_ref, old_ref, keep_ref, out_ref, ends_ref):
+def last_kernel(level, pair_ref, old_ref, keep_ref, out_ref, ends_ref):
     @pl.when(is_upper(level) == 1)
     def _():
-        inflow = split(other_ref[:, HALF : 2 * HALF])
+        inflow = split(pair_ref[0, :, HALF:])
         ends_ref[0] = old_ref[:, HALF : 2 * HALF] + product(split(old_ref[:, :TRACE]), inflow)
         ends_ref[1] = old_ref[:, 3 * HALF : 4 * HALF] + product(split(old_ref[:, 2 * HALF : 2 * HALF + TRACE]), inflow)
 
     @pl.when(is_upper(level) == 0)
     def _():
-        outflow = split(mine_ref[:, HALF : 2 * HALF])
-        value = other_ref[:, HALF : 2 * HALF] + product(split(other_ref[:, :TRACE]), outflow)
+        outflow = split(pair_ref[0, :, HALF:])
+        value = pair_ref[1, :, HALF:] + product(split(pair_ref[1, :, :TRACE]), outflow)
         gain = split(old_ref[:, 4 * HALF : 4 * HALF + TRACE])
         ends_ref[0] = old_ref[:, HALF : 2 * HALF]
         ends_ref[1] = old_ref[:, 3 * HALF : 4 * HALF] + product(gain, split(value))
@@ -260,16 +292,16 @@
         )
 
 
-def call(kernel, shapes, operands, flops, scalars=0, scratch=()):
+def call(kernel, shapes, operands, flops, specs=None, scratch=(), limit=8 * 1024):
     moved = 4 * sum(v.size for v in operands) + 4 * sum(s.size for s in shapes)
     single = len(shapes) == 1
     return pl.pallas_call(
         kernel,
         out_shape=shapes[0] if single else shapes,
-        in_specs=[SMEM] * scalars + [VMEM] * (len(operands) - scalars),
+        in_specs=specs or [VMEM] * len(operands),
         out_specs=VMEM if single else [VMEM] * len(shapes),
         scratch_shapes=list(scratch),
-        compiler_params=pltpu.CompilerParams(vmem_limit_bytes=40 * 1024 * 1024),
+        compiler_params=pltpu.CompilerParams(vmem_limit_bytes=limit * 1024),
         cost_estimate=pl.CostEstimate(flops=flops, bytes_accessed=moved, transcendentals=0),
     )(*operands)
 
@@ -278,60 +310,70 @@
     return jax.ShapeDtypeStruct(dims, F32)
 
 
-PARTNERS = ((0, 0, 1), (0, 1, 0), (0, 2, 0), (0, 6, 0), (1, 0, 0), (3, 0, 0))
+PARTNERS = ((0, 0, 1), (0, 1, 0), (0, 2, 0), (0, 7, 0), (1, 0, 0), (3, 0, 0))
 
 
 def exchange(value, level):
     across, along, core = PARTNERS[level]
     mask = (across * 8 + along) * 2 + core
     count = lax.axis_size("stream")
-    return lax.ppermute(value, "stream", [(k, k ^ mask) for k in range(count)])
+    pairs = [[k, k ^ mask] for k in range(count) if k < k ^ mask]
+    return lax.all_gather(value, "stream", axis_index_groups=pairs)
 
 
 def shards(rhs, inverse, lower, upper, upwind, rows, target):
     groups = lax.axis_size("azi")
     local = rhs.shape[0]
-    partial = call(wake_kernel, [shape(groups * local, BLOCK)], [target.reshape(1, -1), rows], 10**6)
+    top = len(PARTNERS) - 1
+    target = target.reshape(1, -1)
+    partial = call(
+        wake_kernel,
+        [shape(groups * local, BLOCK)],
+        [target, rows],
+        10**6,
+        specs=[HBM, HBM],
+        scratch=[
+            pltpu.VMEM(target.shape, jnp.int32),
+            pltpu.VMEM(rows.shape, F32),
+            pltpu.SemaphoreType.DMA((2,)),
+        ],
+        limit=56 * 1024,
+    )
     parts = lax.all_to_all(partial.reshape(groups, local, BLOCK), "azi", 0, 0)
     parts = jnp.swapaxes(parts, 0, 1)
     total, keep = call(
         local_kernel,
         [shape(TRACE, 4 * HALF), shape(local, BLOCK, 3 * HALF)],
-        [upwind, rhs, inverse, lower, upper, parts],
+        [upwind, parts, lower, inverse, rhs, upper],
         2 * 10**9,
-        scalars=1,
+        specs=[SMEM, VMEM, HBM, HBM, HBM, HBM],
+        scratch=[
+            pltpu.VMEM(lower.shape, F32),
+            pltpu.VMEM(inverse.shape[1:], F32),
+            pltpu.VMEM(inverse.shape[1:], F32),
+            pltpu.VMEM(rhs.shape, F32),
+            pltpu.VMEM(upper.shape, F32),
+            pltpu.SemaphoreType.DMA((5,)),
+        ],
+        limit=56 * 1024,
     )
     state = None
-    for level in range(5):
-        other = exchange(total, level)
-        merged, cross = call(
-            functools.partial(combine_kernel, level),
-            [shape(TRACE, 4 * HALF), shape(TRACE, 2 * HALF)],
-            [total, other],
+    for level in range(top):
+        pair = exchange(total, level)
+        last = top if level == top - 1 else 0
+        total, cross = call(
+            functools.partial(combine_kernel, last),
+            [shape(TRACE, (2 if last else 4) * HALF), shape(TRACE, 2 * HALF)],
+            [pair],
             2 * 10**7,
         )
-        if level == 0:
-            state = call(
-                functools.partial(track_first_kernel, level),
-                [shape(TRACE, 5 * HALF)],
-                [total, other, cross],
-                10**6,
-            )
-        else:
-            state = call(
-                functools.partial(track_kernel, level),
-                [shape(TRACE, 5 * HALF)],
-                [total, other, cross, state],
-                10**7,
-            )
-        total = merged
-    top = (lax.axis_index("stream") >> 5) & 1
-    forward, mixed, _ = unpack(total)
-    other = exchange(jnp.where(top == 1, mixed, forward), 5)
+        track = functools.partial(track_kernel if level else track_first_kernel, level)
+        operands = [pair, cross, state] if level else [pair, cross]
+        state = call(track, [shape(TRACE, 5 * HALF)], operands, 10**7)
     return call(
-        functools.partial(last_kernel, 5),
+        functools.partial(last_kernel, top),
         [shape(local, BLOCK, COLUMNS)],
-        [total, other, state, keep],
+        [exchange(total, top), state, keep],
         10**8,
         scratch=[pltpu.VMEM((2, TRACE, COLUMNS), F32)],
     )

time: 83.2 us -> 79.2 us (0.952)
  the two profiles are of different devices: /device:TPU:64 before, /device:TPU:6 now
where the time goes in v2:
time: 79.2 us; the launch traced here: 78.8 us
  blocking collectives  62.6 us (79%)
  Pallas kernels  14 us (18%)
  local copies, waits for them, and re-layouts  2.12 us (3%)
    all_gather x6, blocking collectives, exchange(): return lax.all_gather(value, 'stream', axis_index_groups=pairs)  47.8 us
    all_to_all x1, blocking collectives, shards(): parts = lax.all_to_all(partial.reshape(groups, local, BLOCK), 'azi', 0, 0)  14.7 us
    pallas_call x13, Pallas kernels, call(): pl.pallas_call(kernel, out_shape=shapes[0] if single else shapes, in_spec...  14 us

profile of v2, /device:TPU:6, one launch (start us, length us, event | category | flops | bytes accessed | tf_op | source)
XLA Modules:
  0.0 78.8 jit_solution(1701171783055214974)
XLA Ops:
  0.0 1.7 %shard_map.73 = f32[16,320]{1,0:T(8,128)} custom-call(s32[1,64]{1,0:T(1,128)} %bitcast.22, f32[64,320]{1,0:T(8,128)} %rows_hbm.1), custom_call_target="tpu_custom_call" | custom-call | flops 1000000 | bytes 102656 | tf_op jit(solution)/shard_map/pallas_call | solution.py:298
  1.7 0.8 reshape.7
  2.4 14.7 %all_to_all.5 = f32[8,2,320]{2,1,0:T(2,128)S(1)} all-to-all(f32[8,2,320]{2,1,0:T(2,128)S(1)} %reshape.7), channel_id=1, replica_groups=mesh['stream'=64,'azi'=8] {'azi'}, dimensions={0} | all-to-all | bytes 40960 | tf_op jit(solution)/shard_map/all_to_all | solution.py:342
  17.2 0.6 copy.11
  17.8 7.7 %shard_map.74 = (f32[80,512]{1,0:T(8,128)}, f32[2,320,384]{2,1,0:T(8,128)}) custom-call(s32[2,3]{1,0:T(2,128)} %upwind_ref.1, f32[2,8,320]{2,1,0:T(8,128)} %bitcast.21, f32[2,80,240]{2,1,0:T(8,128)} %low_hbm.1, f32[2,320,320]{2,1,0:T(8,128)} %inv_hbm.1, f32[2,320,128]{2,1,0:T(8,128)} %rhs_hbm.1, f32[2,80,240]{2,1,0:T(8,128)} %up_hbm.1), custom_call_target="tpu_custom_call" | custom-call | flops 2000000000 | bytes 2621464 | tf_op jit(solution)/shard_map/pallas_call | solution.py:298
  25.5 2.3 %all-gather = f32[160,512]{1,0:T(8,128)S(1)} all-gather(f32[80,512]{1,0:T(8,128)} %get-tuple-element.17), channel_id=2, replica_groups={{0,8},{16,24},{32,40},{48,56},{64,72},{80,88},{96,104},{112,120},{128,1..., dimensions={0}, use_global_device_ids=true | all-gather | bytes 491520 | tf_op jit(solution)/shard_map/all_gather | solution.py:321
  27.8 0.5 shard_map.75
  28.3 7.5 %all-gather.1 = f32[160,512]{1,0:T(8,128)S(1)} all-gather(f32[80,512]{1,0:T(8,128)S(1)} %get-tuple-element.18), channel_id=3, replica_groups={{0,16},{8,24},{32,48},{40,56},{64,80},{72,88},{96,112},{104,120},{128,1..., dimensions={0}, use_global_device_ids=true | all-gather | bytes 491520 | tf_op jit(solution)/shard_map/all_gather | solution.py:321
  35.9 0.5 shard_map.76
  36.4 12.3 %all-gather.2 = f32[160,512]{1,0:T(8,128)S(1)} all-gather(f32[80,512]{1,0:T(8,128)S(1)} %get-tuple-element.19), channel_id=4, replica_groups={{0,32},{8,40},{16,48},{24,56},{64,96},{72,104},{80,112},{88,120},{128,1..., dimensions={0}, use_global_device_ids=true | all-gather | bytes 491520 | tf_op jit(solution)/shard_map/all_gather | solution.py:321
  48.7 0.5 shard_map.77
  49.2 12.5 %all-gather.3 = f32[160,512]{1,0:T(8,128)S(1)} all-gather(f32[80,512]{1,0:T(8,128)S(1)} %get-tuple-element.20), channel_id=5, replica_groups={{0,112},{8,120},{16,96},{24,104},{32,80},{40,88},{48,64},{56,72},{128,2..., dimensions={0}, use_global_device_ids=true | all-gather | bytes 491520 | tf_op jit(solution)/shard_map/all_gather | solution.py:321
  61.8 0.5 shard_map.78
  62.3 6.8 %all-gather.4 = f32[160,512]{1,0:T(8,128)S(1)} all-gather(f32[80,512]{1,0:T(8,128)S(1)} %get-tuple-element.21), channel_id=6, replica_groups={{0,128},{8,136},{16,144},{24,152},{32,160},{40,168},{48,176},{56,184},{..., dimensions={0}, use_global_device_ids=true | all-gather | bytes 491520 | tf_op jit(solution)/shard_map/all_gather | solution.py:321
  69.1 0.4 shard_map.79
  69.5 6.3 %all-gather.5 = f32[160,256]{1,0:T(8,128)S(1)} all-gather(f32[80,256]{1,0:T(8,128)S(1)} %get-tuple-element.22), channel_id=7, replica_groups={{0,384},{8,392},{16,400},{24,408},{32,416},{40,424},{48,432},{56,440},{..., dimensions={0}, use_global_device_ids=true | all-gather | bytes 245760 | tf_op jit(solution)/shard_map/all_gather | solution.py:321
  75.8 0.2 shard_map.81.old_ref
  76.1 0.2 shard_map.82.old_ref
  76.3 0.0 copy-start
  76.3 0.2 shard_map.83.old_ref
  76.5 0.2 shard_map.84.old_ref
  76.8 0.7 copy-done
  77.5 1.3 %shard_map.85 = f32[2,320,128]{2,1,0:T(8,128)} custom-call(f32[2,80,256]{2,1,0:T(8,128)S(1)} %bitcast.20, f32[80,640]{1,0:T(8,128)S(1)} %shard_map.84.old_ref, f32[2,320,384]{2,1,0:T(8,128)S(1)} %copy-done), custom_call_target="tpu_custom_call" | custom-call | flops 100000000 | bytes 1679360 | tf_op jit(solution)/shard_map/pallas_call | solution.py:298
  (1 shorter events, 0.0 us)
Async XLA Ops:
  76.3 1.2 %copy-start = (f32[2,320,384]{2,1,0:T(8,128)S(1)}, f32[2,320,384]{2,1,0:T(8,128)}, u32[]{:S(2)}) copy-start(f32[2,320,384]{2,1,0:T(8,128)} %get-tuple-element.28.keep_ref) | copy-start | bytes 2949124

commit v3 on v2

v3 whole, which is shorter than its diff:
```python
import functools

import jax
import jax.numpy as jnp
from jax import lax
from jax.experimental import pallas as pl
from jax.experimental.pallas import tpu as pltpu
from jax.sharding import PartitionSpec as P

TRACE = 80
BLOCK = 320
COLUMNS = 128
PLANE = 16
CUBE = 64
HALF = 128
F32 = jnp.float32
BF16 = jnp.bfloat16
VMEM = pl.BlockSpec(memory_space=pltpu.VMEM)
SMEM = pl.BlockSpec(memory_space=pltpu.SMEM)
HBM = pl.BlockSpec(memory_space=pltpu.HBM)


def split(value):
    high = value.astype(BF16)
    return high, (value - high.astype(F32)).astype(BF16)


def dot(left, right):
    return jnp.dot(left, right, preferred_element_type=F32)


def product(left, right):
    return dot(left[0], right[0]) + (dot(left[0], right[1]) + dot(left[1], right[0]))


def select_rows(onehot, value):
    return dot(onehot, value[0]), dot(onehot, value[1])


def fetch(sources, buffers, sems):
    copies = [pltpu.make_async_copy(a, b, sems.at[i]) for i, (a, b) in enumerate(zip(sources, buffers))]
    for copy in copies:
        copy.start()
    return copies


def wake_kernel(target_hbm, rows_hbm, out_ref, target_ref, rows_ref, sems):
    for copy in fetch((target_hbm, rows_hbm), (target_ref, rows_ref), sems):
        copy.wait()
    ids = lax.broadcasted_iota(jnp.int32, (out_ref.shape[0], target_ref.shape[1]), 0)
    onehot = jnp.where(ids == target_ref[...], 1.0, 0.0).astype(BF16)
    high, low = split(rows_ref[...])
    out_ref[...] = dot(onehot, high) + dot(onehot, low)


def face_block(ref, element, face):
    return ref[element, :, face * TRACE : (face + 1) * TRACE]


def rows_of(slots, transposed):
    shape = (1, 3 * TRACE) if transposed else (3 * TRACE, 1)
    place = lax.broadcasted_iota(jnp.int32, shape, 1 if transposed else 0)
    which = jnp.where(place >= 2 * TRACE, 2, jnp.where(place >= TRACE, 1, 0))
    trace = place - which * TRACE
    field, upper, lower = trace >> 4, (trace >> 2) & 3, trace & 3
    side = 3 * (slots[0] % 2)
    row = jnp.where(
        which == 0,
        side * 16 + upper * 4 + lower,
        jnp.where(which == 1, upper * 16 + side * 4 + lower, upper * 16 + lower * 4 + side),
    )
    row = field * CUBE + row
    whole = (BLOCK, 3 * TRACE) if transposed else (3 * TRACE, BLOCK)
    rows = lax.broadcasted_iota(jnp.int32, whole, 0 if transposed else 1)
    return jnp.where(rows == row, 1.0, 0.0).astype(BF16)


def last_plane(value):
    return jnp.concatenate(
        [value[at + CUBE - PLANE : at + CUBE] for at in range(0, BLOCK, CUBE)], axis=0
    )


def pack(first, second, third, fourth):
    lead = TRACE
    spare = HALF - lead
    mid = third[:, :HALF]
    return jnp.concatenate(
        [
            first[:, :lead],
            mid[:, :spare],
            first[:, HALF:],
            fourth[:, :lead],
            mid[:, spare:lead],
            jnp.zeros((TRACE, 2 * spare - lead), F32),
            third[:, HALF:],
        ],
        axis=1,
    )


def unpack(value):
    lead = TRACE
    spare = HALF - lead
    zeros = jnp.zeros((TRACE, spare), F32)
    forward = value[:, : 2 * HALF]
    mixed = jnp.concatenate(
        [
            value[:, lead:HALF],
            value[:, 2 * HALF + lead : 2 * HALF + lead + (lead - spare)],
            zeros,
            value[:, 3 * HALF :],
        ],
        axis=1,
    )
    return forward, mixed, value[:, 2 * HALF : 2 * HALF + lead]


def expand(block, take):
    high, low = split(block)
    return dot(high, take) + dot(low, take)


def local_kernel(
    wake_ref,
    upwind_hbm,
    low_hbm,
    up_hbm,
    inv_hbm,
    rhs_hbm,
    total_ref,
    keep_ref,
    upwind_ref,
    low_ref,
    up_ref,
    first_inv_ref,
    second_inv_ref,
    rhs_ref,
    sems,
):
    copies = fetch(
        (upwind_hbm, low_hbm, up_hbm, inv_hbm.at[0], rhs_hbm, inv_hbm.at[1]),
        (upwind_ref, low_ref, up_ref, first_inv_ref, rhs_ref, second_inv_ref),
        sems,
    )
    put_even = rows_of((0, 2, 4), True)
    take_even = rows_of((0, 2, 4), False)
    put_odd = rows_of((1, 3, 5), True)
    take_odd = rows_of((1, 3, 5), False)
    ones = jnp.ones((wake_ref.shape[1], COLUMNS), BF16)
    spare = jnp.zeros((3 * TRACE, HALF - TRACE), F32)
    at = [slice(face * TRACE, (face + 1) * TRACE) for face in range(3)]

    def source(element):
        high, low = split(wake_ref[element])
        dims = (((0,), (0,)), ((), ()))
        wake = lax.dot_general(high, ones, dims, preferred_element_type=F32)
        wake += lax.dot_general(low, ones, dims, preferred_element_type=F32)
        return rhs_ref[element] + wake

    def put(onehot, rows):
        return sum(select_rows(onehot, split(rows)))

    for copy in copies[:3]:
        copy.wait()
    crosses = [upwind_ref[1, face] == 2 for face in range(3)]

    def kept(values, crossing):
        return [jnp.where(cross == crossing, v, 0.0) for cross, v in zip(crosses, values)]

    def wide(values):
        return jnp.concatenate([jnp.concatenate(values, axis=0), spare], axis=1)

    from_first = put(put_even, wide([face_block(low_ref, 0, face) for face in range(3)]))
    blocks = [face_block(low_ref, 1, face) for face in range(3)]
    from_second = put(put_even, wide(kept(blocks, True)))
    inside = [expand(blocks[face], take_odd[at[face]]) for face in range(3)]
    down = split(put(put_even, jnp.concatenate(kept(inside, False), axis=0)))
    inside = [expand(face_block(up_ref, 1, face), take_even[at[face]]) for face in range(3)]
    up = split(put(put_odd, jnp.concatenate(kept(inside, False), axis=0)))
    leave_second = split(sum(kept(inside, True)))
    leave_first = split(expand(up_ref[0], take_even))

    for copy in copies[3:]:
        copy.wait()
    inverse = split(first_inv_ref[...])
    later_inverse = split(second_inv_ref[...])
    first = product(inverse, split(jnp.concatenate([-from_first, source(0)], axis=1)))

    side = put_odd[:, :HALF]
    lane = lax.broadcasted_iota(jnp.int32, (BLOCK, HALF), 1)
    returned = -(dot(later_inverse[0], side) + dot(later_inverse[1], side))
    returned = jnp.where(lane < TRACE, returned, 0.0)
    returned_pair = split(returned)
    keep_ref[1, :, 2 * HALF :] = returned

    inner = product(down, split(first))
    earlier = -product(inverse, split(product(up, returned_pair)))
    keep_ref[0, :, 2 * HALF :] = earlier

    base = jnp.concatenate([-from_second, source(1)], axis=1)
    second = product(later_inverse, split(base - inner))
    keep_ref[1, :, : 2 * HALF] = second
    second_pair = split(second)
    back = product(leave_second, returned_pair) + product(leave_first, split(earlier))
    inner = product(up, second_pair)
    first = first - product(inverse, split(inner))
    keep_ref[0, :, : 2 * HALF] = first
    mixed = product(leave_second, second_pair) + product(leave_first, split(first))
    total_ref[...] = pack(last_plane(second), None, mixed, back)


def is_upper(level):
    return (lax.axis_index("stream") >> level) & 1


def combine_kernel(level, sends, pair_ref, *refs):
    total_ref, state_ref = refs[-2:]
    forward1, mixed1, back1 = unpack(pair_ref[0])
    forward2, mixed2, back2 = unpack(pair_ref[1])
    lane = lax.broadcasted_iota(jnp.int32, (TRACE, 2 * HALF), 1)
    columns = lane >= HALF
    forward1 = jnp.where(columns | (lane < TRACE), forward1, 0.0)
    forward_pair = split(forward1)
    cross = product(split(mixed2[:, :TRACE]), forward_pair) + jnp.where(columns, mixed2, 0.0)
    forward = product(split(forward2[:, :TRACE]), forward_pair)
    forward = forward + jnp.where(columns, forward2, 0.0)
    back_pair = split(back1)
    mixed = mixed1 + product(back_pair, split(cross))
    if sends == "top":
        total_ref[...] = jnp.where(is_upper(level + 1) == 1, mixed, forward)
    else:
        total = pack(forward, None, mixed, product(back_pair, split(back2)))
        if sends == "half":
            half = TRACE // 2
            total = jnp.where(is_upper(0) == 1, total[half:], total[:half])
        total_ref[...] = total

    upper = is_upper(level) == 1
    back2 = jnp.concatenate([back2, jnp.zeros((TRACE, HALF - TRACE), F32)], axis=1)
    if level == 0:
        row = lax.broadcasted_iota(jnp.int32, (TRACE, 2 * HALF), 0)
        eye = jnp.where(lane == row, 1.0, 0.0)
        state_ref[:, : 2 * HALF] = jnp.where(upper, forward1, eye)
        state_ref[:, 2 * HALF : 4 * HALF] = jnp.where(upper, 0.0, cross)
        state_ref[:, 4 * HALF :] = jnp.where(upper, eye[:, :HALF], back2)
        return
    old_ref = refs[0]

    @pl.when(upper)
    def _():
        here = old_ref[:, : 2 * HALF]
        back = old_ref[:, 2 * HALF : 4 * HALF]
        state_ref[:, : 2 * HALF] = product(split(here[:, :TRACE]), forward_pair) + jnp.where(columns, here, 0.0)
        state_ref[:, 2 * HALF : 4 * HALF] = product(split(back[:, :TRACE]), forward_pair) + jnp.where(columns, back, 0.0)
        state_ref[:, 4 * HALF :] = old_ref[:, 4 * HALF :]

    @pl.when(jnp.logical_not(upper))
    def _():
        gain = split(old_ref[:, 4 * HALF : 4 * HALF + TRACE])
        state_ref[:, : 2 * HALF] = old_ref[:, : 2 * HALF]
        state_ref[:, 2 * HALF : 4 * HALF] = old_ref[:, 2 * HALF : 4 * HALF] + product(gain, split(cross))
        state_ref[:, 4 * HALF :] = product(gain, split(back2))


def last_kernel(level, pair_ref, old_ref, keep_ref, out_ref, ends_ref):
    @pl.when(is_upper(level) == 1)
    def _():
        inflow = split(pair_ref[0, :, HALF:])
        ends_ref[0] = old_ref[:, HALF : 2 * HALF] + product(split(old_ref[:, :TRACE]), inflow)
        ends_ref[1] = old_ref[:, 3 * HALF : 4 * HALF] + product(split(old_ref[:, 2 * HALF : 2 * HALF + TRACE]), inflow)

    @pl.when(is_upper(level) == 0)
    def _():
        outflow = split(pair_ref[0, :, HALF:])
        value = pair_ref[1, :, HALF:] + product(split(pair_ref[1, :, :TRACE]), outflow)
        gain = split(old_ref[:, 4 * HALF : 4 * HALF + TRACE])
        ends_ref[0] = old_ref[:, HALF : 2 * HALF]
        ends_ref[1] = old_ref[:, 3 * HALF : 4 * HALF] + product(gain, split(value))

    inflow = split(ends_ref[0])
    incoming = split(ends_ref[1])
    for element in range(2):
        known = keep_ref[element]
        out_ref[element] = (
            known[:, HALF : 2 * HALF]
            + product(split(known[:, :TRACE]), inflow)
            + product(split(known[:, 2 * HALF : 2 * HALF + TRACE]), incoming)
        )


def call(kernel, shapes, operands, flops, specs=None, scratch=(), limit=8 * 1024):
    moved = 4 * sum(v.size for v in operands) + 4 * sum(s.size for s in shapes)
    single = len(shapes) == 1
    return pl.pallas_call(
        kernel,
        out_shape=shapes[0] if single else shapes,
        in_specs=specs or [VMEM] * len(operands),
        out_specs=VMEM if single else [VMEM] * len(shapes),
        scratch_shapes=list(scratch),
        compiler_params=pltpu.CompilerParams(vmem_limit_bytes=limit * 1024),
        cost_estimate=pl.CostEstimate(flops=flops, bytes_accessed=moved, transcendentals=0),
    )(*operands)


def shape(*dims):
    return jax.ShapeDtypeStruct(dims, F32)


LEVELS = (
    ((0, 0, 1), "whole"),
    ((0, 1, 0), "whole"),
    ((0, 2, 0), "half"),
    ((0, 6, 0), "half"),
    ((1, 0, 0), "whole"),
    ((3, 0, 0), "top"),
)


def exchange(value, level):
    (across, along, core), sends = LEVELS[level]
    mask = (across * 8 + along) * 2 + core
    count = lax.axis_size("stream")
    if sends == "half":
        groups = [[k, k + 1, k ^ mask, (k ^ mask) + 1] for k in range(0, count, 2) if k < k ^ mask]
    else:
        groups = [[k, k ^ mask] for k in range(count) if k < k ^ mask]
    gathered = lax.all_gather(value, "stream", axis_index_groups=groups)
    return gathered.reshape(2, TRACE, value.shape[-1])


def shards(rhs, inverse, lower, upper, upwind, rows, target):
    groups = lax.axis_size("azi")
    local = rhs.shape[0]
    top = len(LEVELS) - 1
    target = target.reshape(1, -1)
    rhs, inverse, lower, upper, upwind, rows, target = [
        pltpu.with_memory_space_constraint(v, pltpu.HBM)
        for v in (rhs, inverse, lower, upper, upwind, rows, target)
    ]
    partial = call(
        wake_kernel,
        [shape(groups * local, BLOCK)],
        [target, rows],
        10**6,
        specs=[HBM, HBM],
        scratch=[
            pltpu.VMEM(target.shape, jnp.int32),
            pltpu.VMEM(rows.shape, F32),
            pltpu.SemaphoreType.DMA((2,)),
        ],
    )
    parts = lax.all_to_all(partial.reshape(groups, local, BLOCK), "azi", 0, 0)
    parts = jnp.swapaxes(parts, 0, 1)
    total, keep = call(
        local_kernel,
        [shape(TRACE, 4 * HALF), shape(local, BLOCK, 3 * HALF)],
        [parts, upwind, lower, upper, inverse, rhs],
        2 * 10**9,
        specs=[VMEM, HBM, HBM, HBM, HBM, HBM],
        scratch=[
            pltpu.SMEM(upwind.shape, jnp.int32),
            pltpu.VMEM(lower.shape, F32),
            pltpu.VMEM(upper.shape, F32),
            pltpu.VMEM(inverse.shape[1:], F32),
            pltpu.VMEM(inverse.shape[1:], F32),
            pltpu.VMEM(rhs.shape, F32),
            pltpu.SemaphoreType.DMA((6,)),
        ],
        limit=24 * 1024,
    )
    state = []
    for level in range(top):
        sends = LEVELS[level + 1][1]
        height = TRACE // 2 if sends == "half" else TRACE
        width = 2 * HALF if sends == "top" else 4 * HALF
        total, after = call(
            functools.partial(combine_kernel, level, sends),
            [shape(height, width), shape(TRACE, 5 * HALF)],
            [exchange(total, level)] + state,
            3 * 10**7,
        )
        state = [after]
    return call(
        functools.partial(last_kernel, top),
        [shape(local, BLOCK, COLUMNS)],
        [exchange(total, top), state[0], keep],
        10**8,
        scratch=[pltpu.VMEM((2, TRACE, COLUMNS), F32)],
    )


def solution(mesh):
    both = ("stream", "azi")
    return jax.shard_map(
        shards,
        mesh=mesh,
        in_specs=(
            P(both, None, None),
            P(both, None, None),
            P(both, None, None),
            P(both, None, None),
            P(both, None),
            P(both, None),
            P(both),
        ),
        out_specs=P(both, None, None),
        check_vma=False,
    )
```

time: 79.2 us -> 71.2 us (0.90)
  blocking collectives: 62.6 us -> 57.8 us
  local copies, waits for them, and re-layouts: 2.12 us -> 0.02 us
  Pallas kernels: 14 us -> 12.2 us
    all_gather x6, blocking collectives: 47.8 us -> 43.1 us  [exchange(): gathered = lax.all_gather(value, 'stream', axis_index_groups=groups)]
    pallas_call x13 -> x8, Pallas kernels: 14 us -> 12.2 us  [call(): pl.pallas_call(kernel, out_shape=shapes[0] if single else shapes, in_spec...]
where the time goes in v3:
time: 71.2 us; the launch traced here: 70.1 us
  blocking collectives  57.8 us (81%)
  Pallas kernels  12.2 us (17%)
    all_gather x6, blocking collectives, exchange(): gathered = lax.all_gather(value, 'stream', axis_index_groups=groups)  43.1 us
    all_to_all x1, blocking collectives, shards(): parts = lax.all_to_all(partial.reshape(groups, local, BLOCK), 'azi', 0, 0)  14.7 us
    pallas_call x8, Pallas kernels, call(): pl.pallas_call(kernel, out_shape=shapes[0] if single else shapes, in_spec...  12.2 us

profile of v3, /device:TPU:6, one launch (start us, length us, event | category | flops | bytes accessed | tf_op | source)
XLA Modules:
  0.0 70.1 jit_solution(8539676102409463081)
XLA Ops:
  0.0 1.1 %shard_map.73 = f32[16,320]{1,0:T(8,128)S(1)} custom-call(s32[1,64]{1,0:T(1,128)} %bitcast.17, f32[64,320]{1,0:T(8,128)} %rows_hbm.1), custom_call_target="tpu_custom_call" | custom-call | flops 1000000 | bytes 102656 | tf_op jit(solution)/shard_map/pallas_call | solution.py:295
  1.1 14.7 %all_to_all.5 = f32[8,2,320]{2,1,0:T(2,128)S(1)} all-to-all(f32[8,2,320]{2,1,0:T(2,128)S(1)} %reshape.13), channel_id=1, replica_groups=mesh['stream'=64,'azi'=8] {'azi'}, dimensions={0} | all-to-all | bytes 40960 | tf_op jit(solution)/shard_map/all_to_all | solution.py:353
  15.8 6.5 %shard_map.74 = (f32[80,512]{1,0:T(8,128)S(1)}, f32[2,320,384]{2,1,0:T(8,128)S(1)}) custom-call(f32[2,8,320]{2,1,0:T(8,128)S(1)} %bitcast.16, s32[2,3]{1,0:T(2,128)} %upwind_hbm.1, f32[2,80,240]{2,1,0:T(8,128)} %low_hbm.1, f32[2,80,240]{2,1,0:T(8,128)} %up_hbm.1, f32[2,320,320]{2,1,0:T(8,128)} %inv_hbm.1, f32[2,320,128]{2,1,0:T(8,128)} %rhs_hbm.1), custom_call_target="tpu_custom_call" | custom-call | flops 2000000000 | bytes 2621464 | tf_op jit(solution)/shard_map/pallas_call | solution.py:295
  22.3 2.0 %all-gather = f32[160,512]{1,0:T(8,128)S(1)} all-gather(f32[80,512]{1,0:T(8,128)S(1)} %get-tuple-element.17), channel_id=2, replica_groups={{0,8},{16,24},{32,40},{48,56},{64,72},{80,88},{96,104},{112,120},{128,1..., dimensions={0}, use_global_device_ids=true | all-gather | bytes 491520 | tf_op jit(solution)/shard_map/all_gather | solution.py:328
  24.4 0.5 shard_map.75
  24.9 7.5 %all-gather.1 = f32[160,512]{1,0:T(8,128)S(1)} all-gather(f32[80,512]{1,0:T(8,128)S(1)} %get-tuple-element.18), channel_id=3, replica_groups={{0,16},{8,24},{32,48},{40,56},{64,80},{72,88},{96,112},{104,120},{128,1..., dimensions={0}, use_global_device_ids=true | all-gather | bytes 491520 | tf_op jit(solution)/shard_map/all_gather | solution.py:328
  32.4 0.7 %shard_map.76 = (f32[40,512]{1,0:T(8,128)S(1)}, f32[80,640]{1,0:T(8,128)S(1)}) custom-call(f32[2,80,512]{2,1,0:T(8,128)S(1)} %bitcast.13, f32[80,640]{1,0:T(8,128)S(1)} %get-tuple-element.19.refs_0_), custom_call_target="tpu_custom_call" | custom-call | flops 30000000 | bytes 819200 | tf_op jit(solution)/shard_map/pallas_call | solution.py:295
  33.2 10.6 %all-gather.2 = f32[160,512]{1,0:T(8,128)S(1)} all-gather(f32[40,512]{1,0:T(8,128)S(1)} %get-tuple-element.20), channel_id=4, replica_groups={{0,8,32,40},{16,24,48,56},{64,72,96,104},{80,88,112,120},{128,136,160,1..., dimensions={0}, use_global_device_ids=true | all-gather | bytes 409600 | tf_op jit(solution)/shard_map/all_gather | solution.py:328
  43.7 0.7 %shard_map.77 = (f32[40,512]{1,0:T(8,128)S(1)}, f32[80,640]{1,0:T(8,128)S(1)}) custom-call(f32[2,80,512]{2,1,0:T(8,128)S(1)} %bitcast.10, f32[80,640]{1,0:T(8,128)S(1)} %get-tuple-element.21.refs_0_), custom_call_target="tpu_custom_call" | custom-call | flops 30000000 | bytes 819200 | tf_op jit(solution)/shard_map/pallas_call | solution.py:295
  44.4 9.5 %all-gather.3 = f32[160,512]{1,0:T(8,128)S(1)} all-gather(f32[40,512]{1,0:T(8,128)S(1)} %get-tuple-element.22), channel_id=5, replica_groups={{0,8,96,104},{16,24,112,120},{32,40,64,72},{48,56,80,88},{128,136,224,2..., dimensions={0}, use_global_device_ids=true | all-gather | bytes 409600 | tf_op jit(solution)/shard_map/all_gather | solution.py:328
  54.0 0.7 %shard_map.78 = (f32[80,512]{1,0:T(8,128)S(1)}, f32[80,640]{1,0:T(8,128)S(1)}) custom-call(f32[2,80,512]{2,1,0:T(8,128)S(1)} %bitcast.11, f32[80,640]{1,0:T(8,128)S(1)} %get-tuple-element.23.refs_0_), custom_call_target="tpu_custom_call" | custom-call | flops 30000000 | bytes 901120 | tf_op jit(solution)/shard_map/pallas_call | solution.py:295
  54.7 7.1 %all-gather.4 = f32[160,512]{1,0:T(8,128)S(1)} all-gather(f32[80,512]{1,0:T(8,128)S(1)} %get-tuple-element.24), channel_id=6, replica_groups={{0,128},{8,136},{16,144},{24,152},{32,160},{40,168},{48,176},{56,184},{..., dimensions={0}, use_global_device_ids=true | all-gather | bytes 491520 | tf_op jit(solution)/shard_map/all_gather | solution.py:328
  61.8 0.6 shard_map.79
  62.4 6.3 %all-gather.5 = f32[160,256]{1,0:T(8,128)S(1)} all-gather(f32[80,256]{1,0:T(8,128)S(1)} %get-tuple-element.26), channel_id=7, replica_groups={{0,384},{8,392},{16,400},{24,408},{32,416},{40,424},{48,432},{56,440},{..., dimensions={0}, use_global_device_ids=true | all-gather | bytes 245760 | tf_op jit(solution)/shard_map/all_gather | solution.py:328
  68.8 1.3 %shard_map.80 = f32[2,320,128]{2,1,0:T(8,128)} custom-call(f32[2,80,256]{2,1,0:T(8,128)S(1)} %bitcast.15, f32[80,640]{1,0:T(8,128)S(1)} %get-tuple-element.27.old_ref, f32[2,320,384]{2,1,0:T(8,128)S(1)} %get-tuple-element.28.keep_ref), custom_call_target="tpu_custom_call" | custom-call | flops 100000000 | bytes 1679360 | tf_op jit(solution)/shard_map/pallas_call | solution.py:295
  (2 shorter events, 0.0 us)

commit v4 on v3

--- a/solution.py
+++ b/solution.py
@@ -2,6 +2,7 @@
 
 import jax
 import jax.numpy as jnp
+import numpy as np
 from jax import lax
 from jax.experimental import pallas as pl
 from jax.experimental.pallas import tpu as pltpu
@@ -44,35 +45,53 @@
     return copies
 
 
-def wake_kernel(target_hbm, rows_hbm, out_ref, target_ref, rows_ref, sems):
-    for copy in fetch((target_hbm, rows_hbm), (target_ref, rows_ref), sems):
+def wake_kernel(target_hbm, rows_hbm, upwind_hbm, out_ref, crosses_ref, target_ref, rows_ref, upwind_ref, sems):
+    for copy in fetch((target_hbm, rows_hbm, upwind_hbm), (target_ref, rows_ref, upwind_ref), sems):
         copy.wait()
     ids = lax.broadcasted_iota(jnp.int32, (out_ref.shape[0], target_ref.shape[1]), 0)
     onehot = jnp.where(ids == target_ref[...], 1.0, 0.0).astype(BF16)
     high, low = split(rows_ref[...])
     out_ref[...] = dot(onehot, high) + dot(onehot, low)
+    face = lax.broadcasted_iota(jnp.int32, crosses_ref.shape, 0)
+    crosses = jnp.zeros(crosses_ref.shape, F32)
+    for at in range(3):
+        crosses = jnp.where((face == at) & (upwind_ref[1, at] == 2), 1.0, crosses)
+    crosses_ref[...] = crosses
 
 
 def face_block(ref, element, face):
     return ref[element, :, face * TRACE : (face + 1) * TRACE]
 
 
-def rows_of(slots, transposed):
-    shape = (1, 3 * TRACE) if transposed else (3 * TRACE, 1)
-    place = lax.broadcasted_iota(jnp.int32, shape, 1 if transposed else 0)
-    which = jnp.where(place >= 2 * TRACE, 2, jnp.where(place >= TRACE, 1, 0))
-    trace = place - which * TRACE
-    field, upper, lower = trace >> 4, (trace >> 2) & 3, trace & 3
-    side = 3 * (slots[0] % 2)
-    row = jnp.where(
-        which == 0,
-        side * 16 + upper * 4 + lower,
-        jnp.where(which == 1, upper * 16 + side * 4 + lower, upper * 16 + lower * 4 + side),
-    )
-    row = field * CUBE + row
-    whole = (BLOCK, 3 * TRACE) if transposed else (3 * TRACE, BLOCK)
-    rows = lax.broadcasted_iota(jnp.int32, whole, 0 if transposed else 1)
-    return jnp.where(rows == row, 1.0, 0.0).astype(BF16)
+def face_rows():
+    trace = np.arange(TRACE)
+    field, upper, lower = trace // PLANE, trace // 4 % 4, trace % 4
+    take = np.zeros((2, 3 * TRACE, BLOCK), np.float32)
+    for odd in range(2):
+        side = 3 * odd
+        places = (side * 16 + upper * 4 + lower, upper * 16 + side * 4 + lower, upper * 16 + lower * 4 + side)
+        for face, place in enumerate(places):
+            take[odd, face * TRACE + trace, field * CUBE + place] = 1.0
+    return jnp.asarray(take, BF16), jnp.asarray(take.transpose(0, 2, 1), BF16)
+
+
+WHOLE = 256
+
+
+def left_parts(value):
+    high, low = split(value)
+    ends = [part[:, WHOLE:].astype(F32) for part in (high, low, high)]
+    return high[:, :WHOLE], low[:, :WHOLE], jnp.concatenate(ends, axis=1).astype(BF16)
+
+
+def right_parts(value):
+    high, low = split(value)
+    ends = [part[WHOLE:] for part in (high, high, low)]
+    return high[:WHOLE], low[:WHOLE], jnp.concatenate(ends, axis=0)
+
+
+def long_product(left, right):
+    return (dot(left[0], right[0]) + dot(left[2], right[2])) + (dot(left[0], right[1]) + dot(left[1], right[0]))
 
 
 def last_plane(value):
@@ -121,32 +140,9 @@
     return dot(high, take) + dot(low, take)
 
 
-def local_kernel(
-    wake_ref,
-    upwind_hbm,
-    low_hbm,
-    up_hbm,
-    inv_hbm,
-    rhs_hbm,
-    total_ref,
-    keep_ref,
-    upwind_ref,
-    low_ref,
-    up_ref,
-    first_inv_ref,
-    second_inv_ref,
-    rhs_ref,
-    sems,
-):
-    copies = fetch(
-        (upwind_hbm, low_hbm, up_hbm, inv_hbm.at[0], rhs_hbm, inv_hbm.at[1]),
-        (upwind_ref, low_ref, up_ref, first_inv_ref, rhs_ref, second_inv_ref),
-        sems,
-    )
-    put_even = rows_of((0, 2, 4), True)
-    take_even = rows_of((0, 2, 4), False)
-    put_odd = rows_of((1, 3, 5), True)
-    take_odd = rows_of((1, 3, 5), False)
+def local_kernel(take_ref, put_ref, crosses_ref, wake_ref, low_ref, up_ref, inv_ref, rhs_ref, total_ref, keep_ref):
+    put_even, put_odd = put_ref[0], put_ref[1]
+    take_even, take_odd = take_ref[0], take_ref[1]
     ones = jnp.ones((wake_ref.shape[1], COLUMNS), BF16)
     spare = jnp.zeros((3 * TRACE, HALF - TRACE), F32)
     at = [slice(face * TRACE, (face + 1) * TRACE) for face in range(3)]
@@ -161,9 +157,7 @@
     def put(onehot, rows):
         return sum(select_rows(onehot, split(rows)))
 
-    for copy in copies[:3]:
-        copy.wait()
-    crosses = [upwind_ref[1, face] == 2 for face in range(3)]
+    crosses = [crosses_ref[face : face + 1, :1] > 0.5 for face in range(3)]
 
     def kept(values, crossing):
         return [jnp.where(cross == crossing, v, 0.0) for cross, v in zip(crosses, values)]
@@ -175,38 +169,37 @@
     blocks = [face_block(low_ref, 1, face) for face in range(3)]
     from_second = put(put_even, wide(kept(blocks, True)))
     inside = [expand(blocks[face], take_odd[at[face]]) for face in range(3)]
-    down = split(put(put_even, jnp.concatenate(kept(inside, False), axis=0)))
+    down = left_parts(put(put_even, jnp.concatenate(kept(inside, False), axis=0)))
     inside = [expand(face_block(up_ref, 1, face), take_even[at[face]]) for face in range(3)]
-    up = split(put(put_odd, jnp.concatenate(kept(inside, False), axis=0)))
-    leave_second = split(sum(kept(inside, True)))
-    leave_first = split(expand(up_ref[0], take_even))
-
-    for copy in copies[3:]:
-        copy.wait()
-    inverse = split(first_inv_ref[...])
-    later_inverse = split(second_inv_ref[...])
-    first = product(inverse, split(jnp.concatenate([-from_first, source(0)], axis=1)))
+    up = left_parts(put(put_odd, jnp.concatenate(kept(inside, False), axis=0)))
+    leave_second = left_parts(sum(kept(inside, True)))
+    leave_first = left_parts(expand(up_ref[0], take_even))
+
+    inverse = left_parts(inv_ref[0])
+    later_inverse = left_parts(inv_ref[1])
+    first = long_product(inverse, right_parts(jnp.concatenate([-from_first, source(0)], axis=1)))
 
     side = put_odd[:, :HALF]
     lane = lax.broadcasted_iota(jnp.int32, (BLOCK, HALF), 1)
-    returned = -(dot(later_inverse[0], side) + dot(later_inverse[1], side))
+    high, low = split(inv_ref[1])
+    returned = -(dot(high, side) + dot(low, side))
     returned = jnp.where(lane < TRACE, returned, 0.0)
-    returned_pair = split(returned)
+    returned_pair = right_parts(returned)
     keep_ref[1, :, 2 * HALF :] = returned
 
-    inner = product(down, split(first))
-    earlier = -product(inverse, split(product(up, returned_pair)))
+    inner = long_product(down, right_parts(first))
+    earlier = -long_product(inverse, right_parts(long_product(up, returned_pair)))
     keep_ref[0, :, 2 * HALF :] = earlier
 
     base = jnp.concatenate([-from_second, source(1)], axis=1)
-    second = product(later_inverse, split(base - inner))
+    second = long_product(later_inverse, right_parts(base - inner))
     keep_ref[1, :, : 2 * HALF] = second
-    second_pair = split(second)
-    back = product(leave_second, returned_pair) + product(leave_first, split(earlier))
-    inner = product(up, second_pair)
-    first = first - product(inverse, split(inner))
+    second_pair = right_parts(second)
+    back = long_product(leave_second, returned_pair) + long_product(leave_first, right_parts(earlier))
+    inner = long_product(up, second_pair)
+    first = first - long_product(inverse, right_parts(inner))
     keep_ref[0, :, : 2 * HALF] = first
-    mixed = product(leave_second, second_pair) + product(leave_first, split(first))
+    mixed = long_product(leave_second, second_pair) + long_product(leave_first, right_parts(first))
     total_ref[...] = pack(last_plane(second), None, mixed, back)
 
 
@@ -334,20 +327,18 @@
     local = rhs.shape[0]
     top = len(LEVELS) - 1
     target = target.reshape(1, -1)
-    rhs, inverse, lower, upper, upwind, rows, target = [
-        pltpu.with_memory_space_constraint(v, pltpu.HBM)
-        for v in (rhs, inverse, lower, upper, upwind, rows, target)
-    ]
-    partial = call(
+    rows, target, upwind = [pltpu.with_memory_space_constraint(v, pltpu.HBM) for v in (rows, target, upwind)]
+    partial, crosses = call(
         wake_kernel,
-        [shape(groups * local, BLOCK)],
-        [target, rows],
-        10**6,
-        specs=[HBM, HBM],
+        [shape(groups * local, BLOCK), shape(8, HALF)],
+        [target, rows, upwind],
+        10**10,
+        specs=[HBM, HBM, HBM],
         scratch=[
             pltpu.VMEM(target.shape, jnp.int32),
             pltpu.VMEM(rows.shape, F32),
-            pltpu.SemaphoreType.DMA((2,)),
+            pltpu.SMEM(upwind.shape, jnp.int32),
+            pltpu.SemaphoreType.DMA((3,)),
         ],
     )
     parts = lax.all_to_all(partial.reshape(groups, local, BLOCK), "azi", 0, 0)
@@ -355,18 +346,8 @@
     total, keep = call(
         local_kernel,
         [shape(TRACE, 4 * HALF), shape(local, BLOCK, 3 * HALF)],
-        [parts, upwind, lower, upper, inverse, rhs],
+        [*face_rows(), crosses, parts, lower, upper, inverse, rhs],
         2 * 10**9,
-        specs=[VMEM, HBM, HBM, HBM, HBM, HBM],
-        scratch=[
-            pltpu.SMEM(upwind.shape, jnp.int32),
-            pltpu.VMEM(lower.shape, F32),
-            pltpu.VMEM(upper.shape, F32),
-            pltpu.VMEM(inverse.shape[1:], F32),
-            pltpu.VMEM(inverse.shape[1:], F32),
-            pltpu.VMEM(rhs.shape, F32),
-            pltpu.SemaphoreType.DMA((6,)),
-        ],
         limit=24 * 1024,
     )
     state = []

time: 71.2 us -> 69.1 us (0.971)
  Pallas kernels: 12.2 us -> 10 us
    pallas_call x8, Pallas kernels: 12.2 us -> 10 us  [call(): pl.pallas_call(kernel, out_shape=shapes[0] if single else shapes, in_spec...]
where the time goes in v4:
time: 69.1 us; the launch traced here: 68 us
  blocking collectives  57.8 us (84%)
  Pallas kernels  10 us (14%)
    all_gather x6, blocking collectives, exchange(): gathered = lax.all_gather(value, 'stream', axis_index_groups=groups)  43.1 us
    all_to_all x1, blocking collectives, shards(): parts = lax.all_to_all(partial.reshape(groups, local, BLOCK), 'azi', 0, 0)  14.7 us
    pallas_call x8, Pallas kernels, call(): pl.pallas_call(kernel, out_shape=shapes[0] if single else shapes, in_spec...  10 us

profile of v4, /device:TPU:6, one launch (start us, length us, event | category | flops | bytes accessed | tf_op | source)
XLA Modules:
  0.0 68.0 jit_solution(10879916256634621204)
XLA Ops:
  0.0 0.0 copy-start.3
  0.0 0.0 copy-start.4
  0.0 0.0 copy-start.5
  0.0 1.2 %shard_map.91 = (f32[16,320]{1,0:T(8,128)S(1)}, f32[8,128]{1,0:T(8,128)S(1)}) custom-call(s32[1,64]{1,0:T(1,128)} %bitcast.17, f32[64,320]{1,0:T(8,128)} %rows_hbm.1, s32[2,3]{1,0:T(2,128)} %upwind_hbm.1), custom_call_target="tpu_custom_call" | custom-call | flops 10000000000 | bytes 106776 | tf_op jit(solution)/shard_map/pallas_call | solution.py:288
  1.3 14.7 %all_to_all.5 = f32[8,2,320]{2,1,0:T(2,128)S(1)} all-to-all(f32[8,2,320]{2,1,0:T(2,128)S(1)} %reshape.13), channel_id=1, replica_groups=mesh['stream'=64,'azi'=8] {'azi'}, dimensions={0} | all-to-all | bytes 40960 | tf_op jit(solution)/shard_map/all_to_all | solution.py:344
  16.0 0.0 copy-done
  16.0 0.0 copy-done.1
  16.0 0.0 copy-done.2
  16.0 0.0 copy-done.3
  16.1 0.0 copy-done.4
  16.1 0.0 copy-done.5
  16.1 4.2 %shard_map.92 = (f32[80,512]{1,0:T(8,128)S(1)}, f32[2,320,384]{2,1,0:T(8,128)S(1)}) custom-call(bf16[2,240,320]{2,1,0:T(8,128)(2,1)S(1)} %copy-done.4, bf16[2,320,240]{2,1,0:T(8,128)(2,1)S(1)} %copy-done.5, f32[8,128]{1,0:T(8,128)S(1)} %get-tuple-element.19.crosses_ref, f32[2,8,320]{2,1,0:T(8,128)S(1)} %bitcast.16, f32[2,80,240]{2,1,0:T(8,128)S(1)} %copy-done.2, ...), custom_call_target="tpu_custom_call" | custom-call | flops 2000000000 | bytes 3854336 | tf_op jit(solution)/shard_map/pallas_call | solution.py:288
  20.3 2.0 %all-gather = f32[160,512]{1,0:T(8,128)S(1)} all-gather(f32[80,512]{1,0:T(8,128)S(1)} %get-tuple-element.21), channel_id=2, replica_groups={{0,8},{16,24},{32,40},{48,56},{64,72},{80,88},{96,104},{112,120},{128,1..., dimensions={0}, use_global_device_ids=true | all-gather | bytes 491520 | tf_op jit(solution)/shard_map/all_gather | solution.py:321
  22.3 0.5 shard_map.93
  22.8 7.5 %all-gather.1 = f32[160,512]{1,0:T(8,128)S(1)} all-gather(f32[80,512]{1,0:T(8,128)S(1)} %get-tuple-element.22), channel_id=3, replica_groups={{0,16},{8,24},{32,48},{40,56},{64,80},{72,88},{96,112},{104,120},{128,1..., dimensions={0}, use_global_device_ids=true | all-gather | bytes 491520 | tf_op jit(solution)/shard_map/all_gather | solution.py:321
  30.3 0.7 %shard_map.94 = (f32[40,512]{1,0:T(8,128)S(1)}, f32[80,640]{1,0:T(8,128)S(1)}) custom-call(f32[2,80,512]{2,1,0:T(8,128)S(1)} %bitcast.13, f32[80,640]{1,0:T(8,128)S(1)} %get-tuple-element.23.refs_0_), custom_call_target="tpu_custom_call" | custom-call | flops 30000000 | bytes 819200 | tf_op jit(solution)/shard_map/pallas_call | solution.py:288
  31.1 10.5 %all-gather.2 = f32[160,512]{1,0:T(8,128)S(1)} all-gather(f32[40,512]{1,0:T(8,128)S(1)} %get-tuple-element.24), channel_id=4, replica_groups={{0,8,32,40},{16,24,48,56},{64,72,96,104},{80,88,112,120},{128,136,160,1..., dimensions={0}, use_global_device_ids=true | all-gather | bytes 409600 | tf_op jit(solution)/shard_map/all_gather | solution.py:321
  41.6 0.7 %shard_map.95 = (f32[40,512]{1,0:T(8,128)S(1)}, f32[80,640]{1,0:T(8,128)S(1)}) custom-call(f32[2,80,512]{2,1,0:T(8,128)S(1)} %bitcast.10, f32[80,640]{1,0:T(8,128)S(1)} %get-tuple-element.25.refs_0_), custom_call_target="tpu_custom_call" | custom-call | flops 30000000 | bytes 819200 | tf_op jit(solution)/shard_map/pallas_call | solution.py:288
  42.4 9.5 %all-gather.3 = f32[160,512]{1,0:T(8,128)S(1)} all-gather(f32[40,512]{1,0:T(8,128)S(1)} %get-tuple-element.26), channel_id=5, replica_groups={{0,8,96,104},{16,24,112,120},{32,40,64,72},{48,56,80,88},{128,136,224,2..., dimensions={0}, use_global_device_ids=true | all-gather | bytes 409600 | tf_op jit(solution)/shard_map/all_gather | solution.py:321
  51.9 0.7 %shard_map.96 = (f32[80,512]{1,0:T(8,128)S(1)}, f32[80,640]{1,0:T(8,128)S(1)}) custom-call(f32[2,80,512]{2,1,0:T(8,128)S(1)} %bitcast.11, f32[80,640]{1,0:T(8,128)S(1)} %get-tuple-element.27.refs_0_), custom_call_target="tpu_custom_call" | custom-call | flops 30000000 | bytes 901120 | tf_op jit(solution)/shard_map/pallas_call | solution.py:288
  52.6 7.1 %all-gather.4 = f32[160,512]{1,0:T(8,128)S(1)} all-gather(f32[80,512]{1,0:T(8,128)S(1)} %get-tuple-element.28), channel_id=6, replica_groups={{0,128},{8,136},{16,144},{24,152},{32,160},{40,168},{48,176},{56,184},{..., dimensions={0}, use_global_device_ids=true | all-gather | bytes 491520 | tf_op jit(solution)/shard_map/all_gather | solution.py:321
  59.8 0.6 shard_map.97
  60.4 6.3 %all-gather.5 = f32[160,256]{1,0:T(8,128)S(1)} all-gather(f32[80,256]{1,0:T(8,128)S(1)} %get-tuple-element.30), channel_id=7, replica_groups={{0,384},{8,392},{16,400},{24,408},{32,416},{40,424},{48,432},{56,440},{..., dimensions={0}, use_global_device_ids=true | all-gather | bytes 245760 | tf_op jit(solution)/shard_map/all_gather | solution.py:321
  66.7 1.3 %shard_map.98 = f32[2,320,128]{2,1,0:T(8,128)} custom-call(f32[2,80,256]{2,1,0:T(8,128)S(1)} %bitcast.15, f32[80,640]{1,0:T(8,128)S(1)} %get-tuple-element.31.old_ref, f32[2,320,384]{2,1,0:T(8,128)S(1)} %get-tuple-element.32.keep_ref), custom_call_target="tpu_custom_call" | custom-call | flops 100000000 | bytes 1679360 | tf_op jit(solution)/shard_map/pallas_call | solution.py:288
  (5 shorter events, 0.0 us)
Async XLA Ops:
  0.0 16.0 %copy-start = (f32[2,320,320]{2,1,0:T(8,128)S(1)}, f32[2,320,320]{2,1,0:T(8,128)}, u32[]{:S(2)}) copy-start(f32[2,320,320]{2,1,0:T(8,128)} %inv_ref.1) | copy-start | bytes 2457604
  0.0 16.0 %copy-start.1 = (f32[2,320,128]{2,1,0:T(8,128)S(1)}, f32[2,320,128]{2,1,0:T(8,128)}, u32[]{:S(2)}) copy-start(f32[2,320,128]{2,1,0:T(8,128)} %rhs_ref.1) | copy-start | bytes 983044
  0.0 16.0 %copy-start.2 = (f32[2,80,240]{2,1,0:T(8,128)S(1)}, f32[2,80,240]{2,1,0:T(8,128)}, u32[]{:S(2)}) copy-start(f32[2,80,240]{2,1,0:T(8,128)} %low_ref.1) | copy-start | bytes 460804
  0.0 16.0 %copy-start.3 = (f32[2,80,240]{2,1,0:T(8,128)S(1)}, f32[2,80,240]{2,1,0:T(8,128)}, u32[]{:S(2)}) copy-start(f32[2,80,240]{2,1,0:T(8,128)} %up_ref.1) | copy-start | bytes 460804
  0.0 16.0 %copy-start.4 = (bf16[2,240,320]{2,1,0:T(8,128)(2,1)S(1)}, bf16[2,240,320]{2,1,0:T(8,128)(2,1)}, u32[]{:S(2)}) copy-start(bf16[2,240,320]{2,1,0:T(8,128)(2,1)} %constant.4.clone.take_ref) | copy-start | bytes 921604
  0.0 16.0 %copy-start.5 = (bf16[2,320,240]{2,1,0:T(8,128)(2,1)S(1)}, bf16[2,320,240]{2,1,0:T(8,128)(2,1)}, u32[]{:S(2)}) copy-start(bf16[2,320,240]{2,1,0:T(8,128)(2,1)} %constant.5.clone.put_ref) | copy-start | bytes 921604

commit v5 on v4

--- a/solution.py
+++ b/solution.py
@@ -204,10 +204,15 @@
 
 
 def is_upper(level):
-    return (lax.axis_index("stream") >> level) & 1
-
-
-def combine_kernel(level, sends, pair_ref, *refs):
+    device = lax.axis_index("stream")
+    if level == 0:
+        return (device & 1) == 1
+    chips = lax.axis_size("stream") // 2
+    place = (device >> 1) + chips - OFFSET * (device & 1)
+    return ((place >> (level - 1)) & 1) == 1
+
+
+def combine_kernel(level, pair_ref, *refs):
     total_ref, state_ref = refs[-2:]
     forward1, mixed1, back1 = unpack(pair_ref[0])
     forward2, mixed2, back2 = unpack(pair_ref[1])
@@ -220,16 +225,16 @@
     forward = forward + jnp.where(columns, forward2, 0.0)
     back_pair = split(back1)
     mixed = mixed1 + product(back_pair, split(cross))
-    if sends == "top":
-        total_ref[...] = jnp.where(is_upper(level + 1) == 1, mixed, forward)
-    else:
-        total = pack(forward, None, mixed, product(back_pair, split(back2)))
-        if sends == "half":
-            half = TRACE // 2
-            total = jnp.where(is_upper(0) == 1, total[half:], total[:half])
-        total_ref[...] = total
-
-    upper = is_upper(level) == 1
+    back = product(back_pair, split(back2))
+    if level == 0:
+        chip = lax.axis_index("stream") >> 1
+        begins, ends = chip == 0, chip == lax.axis_size("stream") // 2 - 1
+        forward = jnp.where(ends | (begins & jnp.logical_not(columns)), 0.0, forward)
+        mixed = jnp.where(begins, 0.0, mixed)
+        back = jnp.where(begins | ends, 0.0, back)
+    total_ref[...] = pack(forward, None, mixed, back)
+
+    upper = is_upper(level)
     back2 = jnp.concatenate([back2, jnp.zeros((TRACE, HALF - TRACE), F32)], axis=1)
     if level == 0:
         row = lax.broadcasted_iota(jnp.int32, (TRACE, 2 * HALF), 0)
@@ -256,23 +261,22 @@
         state_ref[:, 4 * HALF :] = product(gain, split(back2))
 
 
-def last_kernel(level, pair_ref, old_ref, keep_ref, out_ref, ends_ref):
-    @pl.when(is_upper(level) == 1)
-    def _():
-        inflow = split(pair_ref[0, :, HALF:])
-        ends_ref[0] = old_ref[:, HALF : 2 * HALF] + product(split(old_ref[:, :TRACE]), inflow)
-        ends_ref[1] = old_ref[:, 3 * HALF : 4 * HALF] + product(split(old_ref[:, 2 * HALF : 2 * HALF + TRACE]), inflow)
-
-    @pl.when(is_upper(level) == 0)
-    def _():
-        outflow = split(pair_ref[0, :, HALF:])
-        value = pair_ref[1, :, HALF:] + product(split(pair_ref[1, :, :TRACE]), outflow)
-        gain = split(old_ref[:, 4 * HALF : 4 * HALF + TRACE])
-        ends_ref[0] = old_ref[:, HALF : 2 * HALF]
-        ends_ref[1] = old_ref[:, 3 * HALF : 4 * HALF] + product(gain, split(value))
-
-    inflow = split(ends_ref[0])
-    incoming = split(ends_ref[1])
+def last_kernel(level, pair_ref, state_ref, keep_ref, out_ref):
+    upper = is_upper(level)
+    mine = unpack(jnp.where(upper, pair_ref[1], pair_ref[0]))
+    other = unpack(jnp.where(upper, pair_ref[0], pair_ref[1]))
+
+    def apply(matrix, value, added):
+        return product(split(matrix[:, :TRACE]), split(value)) + added
+
+    starts, other_starts = mine[0][:, HALF:], other[0][:, HALF:]
+    inflow = apply(other[0], starts, other_starts)
+    outflow = apply(mine[0], other_starts, starts)
+    returned = apply(mine[1], inflow, mine[1][:, HALF:])
+    incoming = apply(other[2], returned, apply(other[1], outflow, other[1][:, HALF:]))
+    here = apply(state_ref[:, 2 * HALF : 3 * HALF], inflow, state_ref[:, 3 * HALF : 4 * HALF])
+    incoming = split(apply(state_ref[:, 4 * HALF :], incoming, here))
+    inflow = split(apply(state_ref[:, :HALF], inflow, state_ref[:, HALF : 2 * HALF]))
     for element in range(2):
         known = keep_ref[element]
         out_ref[element] = (
@@ -300,32 +304,29 @@
     return jax.ShapeDtypeStruct(dims, F32)
 
 
-LEVELS = (
-    ((0, 0, 1), "whole"),
-    ((0, 1, 0), "whole"),
-    ((0, 2, 0), "half"),
-    ((0, 6, 0), "half"),
-    ((1, 0, 0), "whole"),
-    ((3, 0, 0), "top"),
-)
+OFFSET = 10
+MASKS = (1, 2, 6, 8, 24)
 
 
 def exchange(value, level):
-    (across, along, core), sends = LEVELS[level]
-    mask = (across * 8 + along) * 2 + core
-    count = lax.axis_size("stream")
-    if sends == "half":
-        groups = [[k, k + 1, k ^ mask, (k ^ mask) + 1] for k in range(0, count, 2) if k < k ^ mask]
+    chips = lax.axis_size("stream") // 2
+    if level == 0:
+        groups = [[2 * chip, 2 * chip + 1] for chip in range(chips)]
     else:
-        groups = [[k, k ^ mask] for k in range(count) if k < k ^ mask]
-    gathered = lax.all_gather(value, "stream", axis_index_groups=groups)
-    return gathered.reshape(2, TRACE, value.shape[-1])
+        mask = MASKS[level - 1]
+        groups = [
+            [(place + OFFSET * core) % chips * 2 + core for place in (first, first ^ mask)]
+            for core in range(2)
+            for first in range(chips)
+            if first < first ^ mask
+        ]
+    return lax.all_gather(value, "stream", axis_index_groups=groups)
 
 
 def shards(rhs, inverse, lower, upper, upwind, rows, target):
     groups = lax.axis_size("azi")
     local = rhs.shape[0]
-    top = len(LEVELS) - 1
+    top = len(MASKS)
     target = target.reshape(1, -1)
     rows, target, upwind = [pltpu.with_memory_space_constraint(v, pltpu.HBM) for v in (rows, target, upwind)]
     partial, crosses = call(
@@ -352,12 +353,9 @@
     )
     state = []
     for level in range(top):
-        sends = LEVELS[level + 1][1]
-        height = TRACE // 2 if sends == "half" else TRACE
-        width = 2 * HALF if sends == "top" else 4 * HALF
         total, after = call(
-            functools.partial(combine_kernel, level, sends),
-            [shape(height, width), shape(TRACE, 5 * HALF)],
+            functools.partial(combine_kernel, level),
+            [shape(TRACE, 4 * HALF), shape(TRACE, 5 * HALF)],
             [exchange(total, level)] + state,
             3 * 10**7,
         )
@@ -367,7 +365,6 @@
         [shape(local, BLOCK, COLUMNS)],
         [exchange(total, top), state[0], keep],
         10**8,
-        scratch=[pltpu.VMEM((2, TRACE, COLUMNS), F32)],
     )
 
 

time: 69.1 us -> 74 us (1.071)
  the two profiles are of different devices: /device:TPU:6 before, /device:TPU:1 now
where the time goes in v5:
time: 74 us; the launch traced here: 73.8 us
  blocking collectives  63 us (85%)
  Pallas kernels  10.6 us (14%)
    all_gather x6, blocking collectives, exchange(): return lax.all_gather(value, 'stream', axis_index_groups=groups)  48.8 us
    all_to_all x1, blocking collectives, shards(): parts = lax.all_to_all(partial.reshape(groups, local, BLOCK), 'azi', 0, 0)  14.1 us
    pallas_call x8, Pallas kernels, call(): pl.pallas_call(kernel, out_shape=shapes[0] if single else shapes, in_spec...  10.6 us

profile of v5, /device:TPU:1, one launch (start us, length us, event | category | flops | bytes accessed | tf_op | source)
XLA Modules:
  0.0 73.8 jit_solution(3967901671067936586)
XLA Ops:
  0.0 0.0 copy-start.3
  0.0 0.0 copy-start.4
  0.0 0.0 copy-start.5
  0.0 1.2 %shard_map.91 = (f32[16,320]{1,0:T(8,128)S(1)}, f32[8,128]{1,0:T(8,128)S(1)}) custom-call(s32[1,64]{1,0:T(1,128)} %bitcast.17, f32[64,320]{1,0:T(8,128)} %rows_hbm.1, s32[2,3]{1,0:T(2,128)} %upwind_hbm.1), custom_call_target="tpu_custom_call" | custom-call | flops 10000000000 | bytes 106776 | tf_op jit(solution)/shard_map/pallas_call | solution.py:292
  1.3 14.1 %all_to_all.5 = f32[8,2,320]{2,1,0:T(2,128)S(1)} all-to-all(f32[8,2,320]{2,1,0:T(2,128)S(1)} %reshape.7), channel_id=1, replica_groups=mesh['stream'=64,'azi'=8] {'azi'}, dimensions={0} | all-to-all | bytes 40960 | tf_op jit(solution)/shard_map/all_to_all | solution.py:345
  15.4 0.0 copy-done
  15.4 0.0 copy-done.1
  15.4 0.0 copy-done.2
  15.4 0.0 copy-done.3
  15.5 0.0 copy-done.4
  15.5 0.0 copy-done.5
  15.5 4.2 %shard_map.92 = (f32[80,512]{1,0:T(8,128)S(1)}, f32[2,320,384]{2,1,0:T(8,128)S(1)}) custom-call(bf16[2,240,320]{2,1,0:T(8,128)(2,1)S(1)} %copy-done.4, bf16[2,320,240]{2,1,0:T(8,128)(2,1)S(1)} %copy-done.5, f32[8,128]{1,0:T(8,128)S(1)} %get-tuple-element.19.crosses_ref, f32[2,8,320]{2,1,0:T(8,128)S(1)} %bitcast.16, f32[2,80,240]{2,1,0:T(8,128)S(1)} %copy-done.2, ...), custom_call_target="tpu_custom_call" | custom-call | flops 2000000000 | bytes 3854336 | tf_op jit(solution)/shard_map/pallas_call | solution.py:292
  19.7 4.7 %all-gather = f32[160,512]{1,0:T(8,128)S(1)} all-gather(f32[80,512]{1,0:T(8,128)S(1)} %get-tuple-element.21), channel_id=2, replica_groups={{0,8},{16,24},{32,40},{48,56},{64,72},{80,88},{96,104},{112,120},{128,1..., dimensions={0}, use_global_device_ids=true | all-gather | bytes 491520 | tf_op jit(solution)/shard_map/all_gather | solution.py:323
  24.4 0.5 shard_map.93
  24.9 6.1 %all-gather.1 = f32[160,512]{1,0:T(8,128)S(1)} all-gather(f32[80,512]{1,0:T(8,128)S(1)} %get-tuple-element.22), channel_id=3, replica_groups={{0,16},{32,48},{64,80},{96,112},{128,144},{160,176},{192,208},{224,240}..., dimensions={0}, use_global_device_ids=true | all-gather | bytes 491520 | tf_op jit(solution)/shard_map/all_gather | solution.py:323
  31.0 0.7 shard_map.94
  31.7 14.7 %all-gather.2 = f32[160,512]{1,0:T(8,128)S(1)} all-gather(f32[80,512]{1,0:T(8,128)S(1)} %get-tuple-element.24), channel_id=4, replica_groups={{0,32},{16,48},{64,96},{80,112},{128,160},{144,176},{192,224},{208,240}..., dimensions={0}, use_global_device_ids=true | all-gather | bytes 491520 | tf_op jit(solution)/shard_map/all_gather | solution.py:323
  46.4 0.7 shard_map.95
  47.1 9.7 %all-gather.3 = f32[160,512]{1,0:T(8,128)S(1)} all-gather(f32[80,512]{1,0:T(8,128)S(1)} %get-tuple-element.26), channel_id=5, replica_groups={{0,96},{16,112},{32,64},{48,80},{128,224},{144,240},{160,192},{176,208}..., dimensions={0}, use_global_device_ids=true | all-gather | bytes 491520 | tf_op jit(solution)/shard_map/all_gather | solution.py:323
  56.8 0.7 shard_map.96
  57.5 6.4 %all-gather.4 = f32[160,512]{1,0:T(8,128)S(1)} all-gather(f32[80,512]{1,0:T(8,128)S(1)} %get-tuple-element.28), channel_id=6, replica_groups={{0,128},{16,144},{32,160},{48,176},{64,192},{80,208},{96,224},{112,240}..., dimensions={0}, use_global_device_ids=true | all-gather | bytes 491520 | tf_op jit(solution)/shard_map/all_gather | solution.py:323
  63.9 0.7 shard_map.97
  64.6 7.3 %all-gather.5 = f32[160,512]{1,0:T(8,128)S(1)} all-gather(f32[80,512]{1,0:T(8,128)S(1)} %get-tuple-element.30), channel_id=7, replica_groups={{0,384},{16,400},{32,416},{48,432},{64,448},{80,464},{96,480},{112,496}..., dimensions={0}, use_global_device_ids=true | all-gather | bytes 491520 | tf_op jit(solution)/shard_map/all_gather | solution.py:323
  71.9 1.9 %shard_map.98 = f32[2,320,128]{2,1,0:T(8,128)} custom-call(f32[2,80,512]{2,1,0:T(8,128)S(1)} %bitcast.10, f32[80,640]{1,0:T(8,128)S(1)} %get-tuple-element.31.state_ref, f32[2,320,384]{2,1,0:T(8,128)S(1)} %get-tuple-element.32.keep_ref), custom_call_target="tpu_custom_call" | custom-call | flops 100000000 | bytes 1843200 | tf_op jit(solution)/shard_map/pallas_call | solution.py:292
  (5 shorter events, 0.0 us)
Async XLA Ops:
  0.0 15.4 %copy-start = (f32[2,320,320]{2,1,0:T(8,128)S(1)}, f32[2,320,320]{2,1,0:T(8,128)}, u32[]{:S(2)}) copy-start(f32[2,320,320]{2,1,0:T(8,128)} %inv_ref.1) | copy-start | bytes 2457604
  0.0 15.4 %copy-start.1 = (f32[2,320,128]{2,1,0:T(8,128)S(1)}, f32[2,320,128]{2,1,0:T(8,128)}, u32[]{:S(2)}) copy-start(f32[2,320,128]{2,1,0:T(8,128)} %rhs_ref.1) | copy-start | bytes 983044
  0.0 15.4 %copy-start.2 = (f32[2,80,240]{2,1,0:T(8,128)S(1)}, f32[2,80,240]{2,1,0:T(8,128)}, u32[]{:S(2)}) copy-start(f32[2,80,240]{2,1,0:T(8,128)} %low_ref.1) | copy-start | bytes 460804
  0.0 15.4 %copy-start.3 = (f32[2,80,240]{2,1,0:T(8,128)S(1)}, f32[2,80,240]{2,1,0:T(8,128)}, u32[]{:S(2)}) copy-start(f32[2,80,240]{2,1,0:T(8,128)} %up_ref.1) | copy-start | bytes 460804
  0.0 15.4 %copy-start.4 = (bf16[2,240,320]{2,1,0:T(8,128)(2,1)S(1)}, bf16[2,240,320]{2,1,0:T(8,128)(2,1)}, u32[]{:S(2)}) copy-start(bf16[2,240,320]{2,1,0:T(8,128)(2,1)} %constant.4.clone.take_ref) | copy-start | bytes 921604
  0.0 15.4 %copy-start.5 = (bf16[2,320,240]{2,1,0:T(8,128)(2,1)S(1)}, bf16[2,320,240]{2,1,0:T(8,128)(2,1)}, u32[]{:S(2)}) copy-start(bf16[2,320,240]{2,1,0:T(8,128)(2,1)} %constant.5.clone.put_ref) | copy-start | bytes 921604

commit v6 on v5

--- a/solution.py
+++ b/solution.py
@@ -212,7 +212,7 @@
     return ((place >> (level - 1)) & 1) == 1
 
 
-def combine_kernel(level, pair_ref, *refs):
+def combine_kernel(level, halves, pair_ref, *refs):
     total_ref, state_ref = refs[-2:]
     forward1, mixed1, back1 = unpack(pair_ref[0])
     forward2, mixed2, back2 = unpack(pair_ref[1])
@@ -232,7 +232,11 @@
         forward = jnp.where(ends | (begins & jnp.logical_not(columns)), 0.0, forward)
         mixed = jnp.where(begins, 0.0, mixed)
         back = jnp.where(begins | ends, 0.0, back)
-    total_ref[...] = pack(forward, None, mixed, back)
+    total = pack(forward, None, mixed, back)
+    if halves:
+        half = TRACE // 2
+        total = jnp.where((lax.axis_index("stream") & 1) == 1, total[half:], total[:half])
+    total_ref[...] = total
 
     upper = is_upper(level)
     back2 = jnp.concatenate([back2, jnp.zeros((TRACE, HALF - TRACE), F32)], axis=1)
@@ -304,23 +308,25 @@
     return jax.ShapeDtypeStruct(dims, F32)
 
 
-OFFSET = 10
+OFFSET = 8
 MASKS = (1, 2, 6, 8, 24)
+HALVES = (2, 3)
 
 
 def exchange(value, level):
     chips = lax.axis_size("stream") // 2
+    mask = MASKS[level - 1] if level else 0
+    pairs = [(first, first ^ mask) for first in range(chips) if first < first ^ mask]
     if level == 0:
         groups = [[2 * chip, 2 * chip + 1] for chip in range(chips)]
+    elif level in HALVES:
+        groups = [[2 * place + core for place in pair for core in range(2)] for pair in pairs]
     else:
-        mask = MASKS[level - 1]
         groups = [
-            [(place + OFFSET * core) % chips * 2 + core for place in (first, first ^ mask)]
-            for core in range(2)
-            for first in range(chips)
-            if first < first ^ mask
+            [(place + OFFSET * core) % chips * 2 + core for place in pair] for core in range(2) for pair in pairs
         ]
-    return lax.all_gather(value, "stream", axis_index_groups=groups)
+    gathered = lax.all_gather(value, "stream", axis_index_groups=groups)
+    return gathered.reshape(2, TRACE, value.shape[-1])
 
 
 def shards(rhs, inverse, lower, upper, upwind, rows, target):
@@ -353,9 +359,10 @@
     )
     state = []
     for level in range(top):
+        halves = level + 1 in HALVES
         total, after = call(
-            functools.partial(combine_kernel, level),
-            [shape(TRACE, 4 * HALF), shape(TRACE, 5 * HALF)],
+            functools.partial(combine_kernel, level, halves),
+            [shape(TRACE // 2 if halves else TRACE, 4 * HALF), shape(TRACE, 5 * HALF)],
             [exchange(total, level)] + state,
             3 * 10**7,
         )

time: 74 us -> 69.4 us (0.938)
  the two profiles are of different devices: /device:TPU:1 before, /device:TPU:6 now
where the time goes in v6:
time: 69.4 us; the launch traced here: 68.4 us
  blocking collectives  57.6 us (83%)
  Pallas kernels  10.7 us (15%)
    all_gather x6, blocking collectives, exchange(): gathered = lax.all_gather(value, 'stream', axis_index_groups=groups)  42.9 us
    all_to_all x1, blocking collectives, shards(): parts = lax.all_to_all(partial.reshape(groups, local, BLOCK), 'azi', 0, 0)  14.7 us
    pallas_call x8, Pallas kernels, call(): pl.pallas_call(kernel, out_shape=shapes[0] if single else shapes, in_spec...  10.7 us

profile of v6, /device:TPU:6, one launch (start us, length us, event | category | flops | bytes accessed | tf_op | source)
XLA Modules:
  0.0 68.4 jit_solution(7251990052054367252)
XLA Ops:
  0.0 0.0 copy-start.3
  0.0 0.0 copy-start.4
  0.0 0.0 copy-start.5
  0.0 1.2 %shard_map.91 = (f32[16,320]{1,0:T(8,128)S(1)}, f32[8,128]{1,0:T(8,128)S(1)}) custom-call(s32[1,64]{1,0:T(1,128)} %bitcast.17, f32[64,320]{1,0:T(8,128)} %rows_hbm.1, s32[2,3]{1,0:T(2,128)} %upwind_hbm.1), custom_call_target="tpu_custom_call" | custom-call | flops 10000000000 | bytes 106776 | tf_op jit(solution)/shard_map/pallas_call | solution.py:296
  1.3 14.7 %all_to_all.5 = f32[8,2,320]{2,1,0:T(2,128)S(1)} all-to-all(f32[8,2,320]{2,1,0:T(2,128)S(1)} %reshape.13), channel_id=1, replica_groups=mesh['stream'=64,'azi'=8] {'azi'}, dimensions={0} | all-to-all | bytes 40960 | tf_op jit(solution)/shard_map/all_to_all | solution.py:351
  16.0 0.0 copy-done
  16.0 0.0 copy-done.1
  16.0 0.0 copy-done.2
  16.0 0.0 copy-done.3
  16.1 0.0 copy-done.4
  16.1 0.0 copy-done.5
  16.1 4.2 %shard_map.92 = (f32[80,512]{1,0:T(8,128)S(1)}, f32[2,320,384]{2,1,0:T(8,128)S(1)}) custom-call(bf16[2,240,320]{2,1,0:T(8,128)(2,1)S(1)} %copy-done.4, bf16[2,320,240]{2,1,0:T(8,128)(2,1)S(1)} %copy-done.5, f32[8,128]{1,0:T(8,128)S(1)} %get-tuple-element.19.crosses_ref, f32[2,8,320]{2,1,0:T(8,128)S(1)} %bitcast.16, f32[2,80,240]{2,1,0:T(8,128)S(1)} %copy-done.2, ...), custom_call_target="tpu_custom_call" | custom-call | flops 2000000000 | bytes 3854336 | tf_op jit(solution)/shard_map/pallas_call | solution.py:296
  20.3 2.0 %all-gather = f32[160,512]{1,0:T(8,128)S(1)} all-gather(f32[80,512]{1,0:T(8,128)S(1)} %get-tuple-element.21), channel_id=2, replica_groups={{0,8},{16,24},{32,40},{48,56},{64,72},{80,88},{96,104},{112,120},{128,1..., dimensions={0}, use_global_device_ids=true | all-gather | bytes 491520 | tf_op jit(solution)/shard_map/all_gather | solution.py:328
  22.3 0.5 shard_map.93
  22.8 7.5 %all-gather.1 = f32[160,512]{1,0:T(8,128)S(1)} all-gather(f32[80,512]{1,0:T(8,128)S(1)} %get-tuple-element.22), channel_id=3, replica_groups={{0,16},{32,48},{64,80},{96,112},{128,144},{160,176},{192,208},{224,240}..., dimensions={0}, use_global_device_ids=true | all-gather | bytes 491520 | tf_op jit(solution)/shard_map/all_gather | solution.py:328
  30.4 0.7 %shard_map.94 = (f32[40,512]{1,0:T(8,128)S(1)}, f32[80,640]{1,0:T(8,128)S(1)}) custom-call(f32[2,80,512]{2,1,0:T(8,128)S(1)} %bitcast.14, f32[80,640]{1,0:T(8,128)S(1)} %get-tuple-element.23.refs_0_), custom_call_target="tpu_custom_call" | custom-call | flops 30000000 | bytes 819200 | tf_op jit(solution)/shard_map/pallas_call | solution.py:296
  31.1 10.5 %all-gather.2 = f32[160,512]{1,0:T(8,128)S(1)} all-gather(f32[40,512]{1,0:T(8,128)S(1)} %get-tuple-element.24), channel_id=4, replica_groups={{0,8,32,40},{16,24,48,56},{64,72,96,104},{80,88,112,120},{128,136,160,1..., dimensions={0}, use_global_device_ids=true | all-gather | bytes 409600 | tf_op jit(solution)/shard_map/all_gather | solution.py:328
  41.6 0.7 %shard_map.95 = (f32[40,512]{1,0:T(8,128)S(1)}, f32[80,640]{1,0:T(8,128)S(1)}) custom-call(f32[2,80,512]{2,1,0:T(8,128)S(1)} %bitcast.10, f32[80,640]{1,0:T(8,128)S(1)} %get-tuple-element.25.refs_0_), custom_call_target="tpu_custom_call" | custom-call | flops 30000000 | bytes 819200 | tf_op jit(solution)/shard_map/pallas_call | solution.py:296
  42.4 9.5 %all-gather.3 = f32[160,512]{1,0:T(8,128)S(1)} all-gather(f32[40,512]{1,0:T(8,128)S(1)} %get-tuple-element.26), channel_id=5, replica_groups={{0,8,96,104},{16,24,112,120},{32,40,64,72},{48,56,80,88},{128,136,224,2..., dimensions={0}, use_global_device_ids=true | all-gather | bytes 409600 | tf_op jit(solution)/shard_map/all_gather | solution.py:328
  51.9 0.7 %shard_map.96 = (f32[80,512]{1,0:T(8,128)S(1)}, f32[80,640]{1,0:T(8,128)S(1)}) custom-call(f32[2,80,512]{2,1,0:T(8,128)S(1)} %bitcast.11, f32[80,640]{1,0:T(8,128)S(1)} %get-tuple-element.27.refs_0_), custom_call_target="tpu_custom_call" | custom-call | flops 30000000 | bytes 901120 | tf_op jit(solution)/shard_map/pallas_call | solution.py:296
  52.6 6.0 %all-gather.4 = f32[160,512]{1,0:T(8,128)S(1)} all-gather(f32[80,512]{1,0:T(8,128)S(1)} %get-tuple-element.28), channel_id=6, replica_groups={{0,128},{16,144},{32,160},{48,176},{64,192},{80,208},{96,224},{112,240}..., dimensions={0}, use_global_device_ids=true | all-gather | bytes 491520 | tf_op jit(solution)/shard_map/all_gather | solution.py:328
  58.6 0.7 %shard_map.97 = (f32[80,512]{1,0:T(8,128)S(1)}, f32[80,640]{1,0:T(8,128)S(1)}) custom-call(f32[2,80,512]{2,1,0:T(8,128)S(1)} %bitcast.15, f32[80,640]{1,0:T(8,128)S(1)} %get-tuple-element.29.refs_0_), custom_call_target="tpu_custom_call" | custom-call | flops 30000000 | bytes 901120 | tf_op jit(solution)/shard_map/pallas_call | solution.py:296
  59.4 7.2 %all-gather.5 = f32[160,512]{1,0:T(8,128)S(1)} all-gather(f32[80,512]{1,0:T(8,128)S(1)} %get-tuple-element.30), channel_id=7, replica_groups={{0,384},{16,400},{32,416},{48,432},{64,448},{80,464},{96,480},{112,496}..., dimensions={0}, use_global_device_ids=true | all-gather | bytes 491520 | tf_op jit(solution)/shard_map/all_gather | solution.py:328
  66.6 1.9 %shard_map.98 = f32[2,320,128]{2,1,0:T(8,128)} custom-call(f32[2,80,512]{2,1,0:T(8,128)S(1)} %bitcast.12, f32[80,640]{1,0:T(8,128)S(1)} %get-tuple-element.31.state_ref, f32[2,320,384]{2,1,0:T(8,128)S(1)} %get-tuple-element.32.keep_ref), custom_call_target="tpu_custom_call" | custom-call | flops 100000000 | bytes 1843200 | tf_op jit(solution)/shard_map/pallas_call | solution.py:296
  (5 shorter events, 0.0 us)
Async XLA Ops:
  0.0 16.0 %copy-start = (f32[2,320,320]{2,1,0:T(8,128)S(1)}, f32[2,320,320]{2,1,0:T(8,128)}, u32[]{:S(2)}) copy-start(f32[2,320,320]{2,1,0:T(8,128)} %inv_ref.1) | copy-start | bytes 2457604
  0.0 16.0 %copy-start.1 = (f32[2,320,128]{2,1,0:T(8,128)S(1)}, f32[2,320,128]{2,1,0:T(8,128)}, u32[]{:S(2)}) copy-start(f32[2,320,128]{2,1,0:T(8,128)} %rhs_ref.1) | copy-start | bytes 983044
  0.0 16.0 %copy-start.2 = (f32[2,80,240]{2,1,0:T(8,128)S(1)}, f32[2,80,240]{2,1,0:T(8,128)}, u32[]{:S(2)}) copy-start(f32[2,80,240]{2,1,0:T(8,128)} %low_ref.1) | copy-start | bytes 460804
  0.0 16.0 %copy-start.3 = (f32[2,80,240]{2,1,0:T(8,128)S(1)}, f32[2,80,240]{2,1,0:T(8,128)}, u32[]{:S(2)}) copy-start(f32[2,80,240]{2,1,0:T(8,128)} %up_ref.1) | copy-start | bytes 460804
  0.0 16.0 %copy-start.4 = (bf16[2,240,320]{2,1,0:T(8,128)(2,1)S(1)}, bf16[2,240,320]{2,1,0:T(8,128)(2,1)}, u32[]{:S(2)}) copy-start(bf16[2,240,320]{2,1,0:T(8,128)(2,1)} %constant.4.clone.take_ref) | copy-start | bytes 921604
  0.0 16.0 %copy-start.5 = (bf16[2,320,240]{2,1,0:T(8,128)(2,1)S(1)}, bf16[2,320,240]{2,1,0:T(8,128)(2,1)}, u32[]{:S(2)}) copy-start(bf16[2,320,240]{2,1,0:T(8,128)(2,1)} %constant.5.clone.put_ref) | copy-start | bytes 921604

commit v7 on v4

--- a/solution.py
+++ b/solution.py
@@ -207,10 +207,9 @@
     return (lax.axis_index("stream") >> level) & 1
 
 
-def combine_kernel(level, sends, pair_ref, *refs):
-    total_ref, state_ref = refs[-2:]
-    forward1, mixed1, back1 = unpack(pair_ref[0])
-    forward2, mixed2, back2 = unpack(pair_ref[1])
+def merge(run1, run2):
+    forward1, mixed1, back1 = run1
+    forward2, mixed2, back2 = run2
     lane = lax.broadcasted_iota(jnp.int32, (TRACE, 2 * HALF), 1)
     columns = lane >= HALF
     forward1 = jnp.where(columns | (lane < TRACE), forward1, 0.0)
@@ -220,28 +219,18 @@
     forward = forward + jnp.where(columns, forward2, 0.0)
     back_pair = split(back1)
     mixed = mixed1 + product(back_pair, split(cross))
-    if sends == "top":
-        total_ref[...] = jnp.where(is_upper(level + 1) == 1, mixed, forward)
-    else:
-        total = pack(forward, None, mixed, product(back_pair, split(back2)))
-        if sends == "half":
-            half = TRACE // 2
-            total = jnp.where(is_upper(0) == 1, total[half:], total[:half])
-        total_ref[...] = total
-
-    upper = is_upper(level) == 1
+    back = product(back_pair, split(back2))
     back2 = jnp.concatenate([back2, jnp.zeros((TRACE, HALF - TRACE), F32)], axis=1)
-    if level == 0:
-        row = lax.broadcasted_iota(jnp.int32, (TRACE, 2 * HALF), 0)
-        eye = jnp.where(lane == row, 1.0, 0.0)
-        state_ref[:, : 2 * HALF] = jnp.where(upper, forward1, eye)
-        state_ref[:, 2 * HALF : 4 * HALF] = jnp.where(upper, 0.0, cross)
-        state_ref[:, 4 * HALF :] = jnp.where(upper, eye[:, :HALF], back2)
-        return
-    old_ref = refs[0]
+    return (forward, mixed, back), (forward1, cross, back2)
+
+
+def track(upper, pieces, old_ref, state_ref):
+    forward1, cross, back2 = pieces
+    columns = lax.broadcasted_iota(jnp.int32, (TRACE, 2 * HALF), 1) >= HALF
 
     @pl.when(upper)
     def _():
+        forward_pair = split(forward1)
         here = old_ref[:, : 2 * HALF]
         back = old_ref[:, 2 * HALF : 4 * HALF]
         state_ref[:, : 2 * HALF] = product(split(here[:, :TRACE]), forward_pair) + jnp.where(columns, here, 0.0)
@@ -254,6 +243,48 @@
         state_ref[:, : 2 * HALF] = old_ref[:, : 2 * HALF]
         state_ref[:, 2 * HALF : 4 * HALF] = old_ref[:, 2 * HALF : 4 * HALF] + product(gain, split(cross))
         state_ref[:, 4 * HALF :] = product(gain, split(back2))
+
+
+def first_kernel(pair_ref, total_ref, half_ref, state_ref):
+    upper = is_upper(0) == 1
+    total, (forward1, cross, back2) = merge(unpack(pair_ref[0]), unpack(pair_ref[1]))
+    total = pack(total[0], None, total[1], total[2])
+    total_ref[...] = total
+    half_ref[...] = jnp.where(upper, total[TRACE // 2 :], total[: TRACE // 2])
+    lane = lax.broadcasted_iota(jnp.int32, (TRACE, 2 * HALF), 1)
+    row = lax.broadcasted_iota(jnp.int32, (TRACE, 2 * HALF), 0)
+    eye = jnp.where(lane == row, 1.0, 0.0)
+    state_ref[:, : 2 * HALF] = jnp.where(upper, forward1, eye)
+    state_ref[:, 2 * HALF : 4 * HALF] = jnp.where(upper, 0.0, cross)
+    state_ref[:, 4 * HALF :] = jnp.where(upper, eye[:, :HALF], back2)
+
+
+def four_kernel(own_ref, others_ref, old_ref, half_ref, state_ref, middle_ref):
+    odd, late = is_upper(1) == 1, is_upper(2) == 1
+    own, near, far = own_ref[...], others_ref[0, :TRACE], others_ref[1, :TRACE]
+    middle = jnp.concatenate([others_ref[0, TRACE:], others_ref[1, TRACE:]], axis=0)
+
+    def ordered(swap, one, two):
+        return unpack(jnp.where(swap, two, one)), unpack(jnp.where(swap, one, two))
+
+    mine, pieces = merge(*ordered(odd, own, near))
+    other, _ = merge(*ordered(odd, middle, far))
+    track(odd, pieces, old_ref, middle_ref)
+    earlier = [jnp.where(late, b, a) for a, b in zip(mine, other)]
+    later = [jnp.where(late, a, b) for a, b in zip(mine, other)]
+    total, pieces = merge(earlier, later)
+    total = pack(total[0], None, total[1], total[2])
+    half_ref[...] = jnp.where(is_upper(0) == 1, total[TRACE // 2 :], total[: TRACE // 2])
+    track(late, pieces, middle_ref, state_ref)
+
+
+def combine_kernel(level, sends, pair_ref, old_ref, total_ref, state_ref):
+    total, pieces = merge(unpack(pair_ref[0]), unpack(pair_ref[1]))
+    if sends == "top":
+        total_ref[...] = jnp.where(is_upper(level + 1) == 1, total[1], total[0])
+    else:
+        total_ref[...] = pack(total[0], None, total[1], total[2])
+    track(is_upper(level) == 1, pieces, old_ref, state_ref)
 
 
 def last_kernel(level, pair_ref, old_ref, keep_ref, out_ref, ends_ref):
@@ -300,32 +331,29 @@
     return jax.ShapeDtypeStruct(dims, F32)
 
 
-LEVELS = (
-    ((0, 0, 1), "whole"),
-    ((0, 1, 0), "whole"),
-    ((0, 2, 0), "half"),
-    ((0, 6, 0), "half"),
-    ((1, 0, 0), "whole"),
-    ((3, 0, 0), "top"),
-)
-
-
-def exchange(value, level):
-    (across, along, core), sends = LEVELS[level]
-    mask = (across * 8 + along) * 2 + core
+def gather(value, masks):
     count = lax.axis_size("stream")
-    if sends == "half":
-        groups = [[k, k + 1, k ^ mask, (k ^ mask) + 1] for k in range(0, count, 2) if k < k ^ mask]
-    else:
-        groups = [[k, k ^ mask] for k in range(count) if k < k ^ mask]
-    gathered = lax.all_gather(value, "stream", axis_index_groups=groups)
-    return gathered.reshape(2, TRACE, value.shape[-1])
+    masks = [(across * 8 + along) * 2 + core for across, along, core in masks]
+    seen, groups = set(), []
+    for device in range(count):
+        if device in seen:
+            continue
+        group = {device}
+        for mask in masks:
+            group |= {member ^ mask for member in group}
+        seen |= group
+        groups.append(sorted(group))
+    return lax.all_gather(value, "stream", axis_index_groups=groups)
+
+
+def swap(value, along):
+    count = lax.axis_size("stream")
+    return lax.ppermute(value, "stream", [(k, k ^ (2 * along[k % 2])) for k in range(count)])
 
 
 def shards(rhs, inverse, lower, upper, upwind, rows, target):
     groups = lax.axis_size("azi")
     local = rhs.shape[0]
-    top = len(LEVELS) - 1
     target = target.reshape(1, -1)
     rows, target, upwind = [pltpu.with_memory_space_constraint(v, pltpu.HBM) for v in (rows, target, upwind)]
     partial, crosses = call(
@@ -350,22 +378,26 @@
         2 * 10**9,
         limit=24 * 1024,
     )
-    state = []
-    for level in range(top):
-        sends = LEVELS[level + 1][1]
-        height = TRACE // 2 if sends == "half" else TRACE
-        width = 2 * HALF if sends == "top" else 4 * HALF
-        total, after = call(
-            functools.partial(combine_kernel, level, sends),
-            [shape(height, width), shape(TRACE, 5 * HALF)],
-            [exchange(total, level)] + state,
-            3 * 10**7,
-        )
-        state = [after]
+    full, half, state = shape(TRACE, 4 * HALF), shape(TRACE // 2, 4 * HALF), shape(TRACE, 5 * HALF)
+    total, part, tracked = call(first_kernel, [full, half, state], [gather(total, [(0, 0, 1)])], 3 * 10**7)
+    received = jnp.concatenate([swap(total, (1, 3)), swap(part, (2, 2))], axis=0)
+    received = gather(received, [(0, 0, 1)])
+    part, tracked = call(
+        four_kernel,
+        [half, state],
+        [total, received, tracked],
+        10**8,
+        scratch=[pltpu.VMEM((TRACE, 5 * HALF), F32)],
+    )
+    pair = gather(part, [(0, 0, 1), (0, 6, 0)]).reshape(2, TRACE, 4 * HALF)
+    total, tracked = call(functools.partial(combine_kernel, 3, "whole"), [full, state], [pair, tracked], 3 * 10**7)
+    pair = gather(total, [(1, 0, 0)])
+    crossing = shape(TRACE, 2 * HALF)
+    total, tracked = call(functools.partial(combine_kernel, 4, "top"), [crossing, state], [pair, tracked], 3 * 10**7)
     return call(
-        functools.partial(last_kernel, top),
+        functools.partial(last_kernel, 5),
         [shape(local, BLOCK, COLUMNS)],
-        [exchange(total, top), state[0], keep],
+        [gather(total, [(3, 0, 0)]), tracked, keep],
         10**8,
         scratch=[pltpu.VMEM((2, TRACE, COLUMNS), F32)],
     )

time: 69.1 us -> 68.5 us (level)
  blocking collectives: 57.8 us -> 42.1 us
  starting transfers between devices: 0 us -> 10.4 us
  waiting for transfers between devices: 0 us -> 4.43 us
    all_gather x6 -> x5, blocking collectives: 43.1 us -> 27.3 us  [gather(): return lax.all_gather(value, 'stream', axis_index_groups=groups)]
    ppermute x0 -> x2, starting transfers between devices: none -> 10.4 us  [swap(): lax.ppermute(value, 'stream', [(k, k ^ 2 * along[k % 2]) for k in range(c...]
    ppermute x0 -> x2, waiting for transfers between devices: none -> 4.43 us  [swap(): lax.ppermute(value, 'stream', [(k, k ^ 2 * along[k % 2]) for k in range(c...]
    pallas_call x8 -> x7, Pallas kernels: 10 us -> 10.2 us  [call(): pl.pallas_call(kernel, out_shape=shapes[0] if single else shapes, in_spec...]
  transfers between devices with their start and end apart: 0 -> 2, of which waited for: 0 -> 1; matrix products, arithmetic and copies ran while one was open for 0% -> 0% of each run, Pallas kernels for 0% -> 0%
where the time goes in v7:
time: 68.5 us; the launch traced here: 67.2 us
  blocking collectives  42.1 us (61%)
  starting transfers between devices  10.4 us (15%)
  Pallas kernels  10.2 us (15%)
  waiting for transfers between devices  4.43 us (6%)
    all_gather x5, blocking collectives, gather(): return lax.all_gather(value, 'stream', axis_index_groups=groups)  27.3 us
    all_to_all x1, blocking collectives, shards(): parts = lax.all_to_all(partial.reshape(groups, local, BLOCK), 'azi', 0, 0)  14.7 us
    ppermute x2, starting transfers between devices, swap(): lax.ppermute(value, 'stream', [(k, k ^ 2 * along[k % 2]) for k in range(c...  10.4 us
    pallas_call x7, Pallas kernels, call(): pl.pallas_call(kernel, out_shape=shapes[0] if single else shapes, in_spec...  10.2 us
    ppermute x2, waiting for transfers between devices, swap(): lax.ppermute(value, 'stream', [(k, k ^ 2 * along[k % 2]) for k in range(c...  4.43 us
  transfers between devices with their start and end apart: 2, of which 1 were waited for; matrix products, arithmetic and copies ran while one was open for 0% of the time, Pallas kernels for 0%

profile of v7, /device:TPU:6, one launch (start us, length us, event | category | flops | bytes accessed | tf_op | source)
XLA Modules:
  0.0 67.2 jit_solution(2317402673318804089)
XLA Ops:
  0.0 0.0 copy-start.3
  0.0 0.0 copy-start.4
  0.0 0.0 copy-start.5
  0.0 1.2 %shard_map.91 = (f32[16,320]{1,0:T(8,128)S(1)}, f32[8,128]{1,0:T(8,128)S(1)}) custom-call(s32[1,64]{1,0:T(1,128)} %bitcast.15, f32[64,320]{1,0:T(8,128)} %rows_hbm.1, s32[2,3]{1,0:T(2,128)} %upwind_hbm.1), custom_call_target="tpu_custom_call" | custom-call | flops 10000000000 | bytes 106776 | tf_op jit(solution)/shard_map/pallas_call | solution.py:319
  1.3 14.7 %all_to_all.5 = f32[8,2,320]{2,1,0:T(2,128)S(1)} all-to-all(f32[8,2,320]{2,1,0:T(2,128)S(1)} %reshape.10), channel_id=1, replica_groups=mesh['stream'=64,'azi'=8] {'azi'}, dimensions={0} | all-to-all | bytes 40960 | tf_op jit(solution)/shard_map/all_to_all | solution.py:372
  16.0 0.0 copy-done
  16.0 0.0 copy-done.1
  16.0 0.0 copy-done.2
  16.0 0.0 copy-done.3
  16.1 4.2 %shard_map.92 = (f32[80,512]{1,0:T(8,128)S(1)}, f32[2,320,384]{2,1,0:T(8,128)S(1)}) custom-call(bf16[2,240,320]{2,1,0:T(8,128)(2,1)S(1)} %copy-done.4, bf16[2,320,240]{2,1,0:T(8,128)(2,1)S(1)} %copy-done.5, f32[8,128]{1,0:T(8,128)S(1)} %get-tuple-element.18.crosses_ref, f32[2,8,320]{2,1,0:T(8,128)S(1)} %bitcast.14, f32[2,80,240]{2,1,0:T(8,128)S(1)} %copy-done.2, ...), custom_call_target="tpu_custom_call" | custom-call | flops 2000000000 | bytes 3854336 | tf_op jit(solution)/shard_map/pallas_call | solution.py:319
  20.3 2.0 %all-gather = f32[160,512]{1,0:T(8,128)S(1)} all-gather(f32[80,512]{1,0:T(8,128)S(1)} %get-tuple-element.20), channel_id=2, replica_groups={{0,8},{16,24},{32,40},{48,56},{64,72},{80,88},{96,104},{112,120},{128,1..., dimensions={0}, use_global_device_ids=true | all-gather | bytes 491520 | tf_op jit(solution)/shard_map/all_gather | solution.py:346
  22.3 0.5 shard_map.93
  22.8 4.3 %collective-permute-start = (f32[80,512]{1,0:T(8,128)S(1)}, f32[80,512]{1,0:T(8,128)S(1)}, u32[]{:S(2)}, u32[]{:S(2)}) collective-permute-start(f32[80,512]{1,0:T(8,128)S(1)} %get-tuple-element.21.own_ref), channel_id=1, source_target_pairs={{0,16},{8,56},{16,0},{24,40},{32,48},{40,24},{48,32},{56,8},{64,80... | collective-permute-start | bytes 491528 | tf_op jit(solution)/shard_map/ppermute | solution.py:351
  27.1 6.1 %collective-permute-start.1 = (f32[40,512]{1,0:T(8,128)S(1)}, f32[40,512]{1,0:T(8,128)S(1)}, u32[]{:S(2)}, u32[]{:S(2)}) collective-permute-start(f32[40,512]{1,0:T(8,128)S(1)} %get-tuple-element.22), channel_id=1, source_target_pairs={{0,32},{8,40},{16,48},{24,56},{32,0},{40,8},{48,16},{56,24},{64,96... | collective-permute-start | bytes 245768 | tf_op jit(solution)/shard_map/ppermute | solution.py:351
  33.2 4.4 %collective-permute-done.1 = f32[40,512]{1,0:T(8,128)S(1)} collective-permute-done((f32[40,512]{1,0:T(8,128)S(1)}, f32[40,512]{1,0:T(8,128)S(1)}, u32[]{:S(2)}, u32[]{:S(2)}) %collective-permute-start.1) | collective-permute-done | bytes 81952 | tf_op jit(solution)/shard_map/ppermute | solution.py:351
  37.6 0.0 collective-permute-done
  37.7 2.2 %all-gather.1 = f32[240,512]{1,0:T(8,128)S(1)} all-gather(f32[120,512]{1,0:T(8,128)S(1)} %pad_maximum_fusion), channel_id=3, replica_groups={{0,8},{16,24},{32,40},{48,56},{64,72},{80,88},{96,104},{112,120},{128,1..., dimensions={0}, use_global_device_ids=true | all-gather | bytes 737280 | tf_op jit(solution)/shard_map/all_gather | solution.py:346
  39.9 1.6 %shard_map.94 = (f32[40,512]{1,0:T(8,128)S(1)}, f32[80,640]{1,0:T(8,128)S(1)}) custom-call(f32[80,512]{1,0:T(8,128)S(1)} %get-tuple-element.21.own_ref, f32[2,120,512]{2,1,0:T(8,128)S(1)} %bitcast.9, f32[80,640]{1,0:T(8,128)S(1)} %get-tuple-element.23.old_ref), custom_call_target="tpu_custom_call" | custom-call | flops 100000000 | bytes 1146880 | tf_op jit(solution)/shard_map/pallas_call | solution.py:319
  41.5 9.6 %all-gather.2 = f32[160,512]{1,0:T(8,128)S(1)} all-gather(f32[40,512]{1,0:T(8,128)S(1)} %get-tuple-element.24), channel_id=4, replica_groups={{0,8,96,104},{16,24,112,120},{32,40,64,72},{48,56,80,88},{128,136,224,2..., dimensions={0}, use_global_device_ids=true | all-gather | bytes 409600 | tf_op jit(solution)/shard_map/all_gather | solution.py:346
  51.1 0.7 %shard_map.95 = (f32[80,512]{1,0:T(8,128)S(1)}, f32[80,640]{1,0:T(8,128)S(1)}) custom-call(f32[2,80,512]{2,1,0:T(8,128)S(1)} %bitcast.10, f32[80,640]{1,0:T(8,128)S(1)} %get-tuple-element.25.old_ref), custom_call_target="tpu_custom_call" | custom-call | flops 30000000 | bytes 901120 | tf_op jit(solution)/shard_map/pallas_call | solution.py:319
  51.8 7.1 %all-gather.3 = f32[160,512]{1,0:T(8,128)S(1)} all-gather(f32[80,512]{1,0:T(8,128)S(1)} %get-tuple-element.26), channel_id=5, replica_groups={{0,128},{8,136},{16,144},{24,152},{32,160},{40,168},{48,176},{56,184},{..., dimensions={0}, use_global_device_ids=true | all-gather | bytes 491520 | tf_op jit(solution)/shard_map/all_gather | solution.py:346
  59.0 0.6 shard_map.96
  59.6 6.3 %all-gather.4 = f32[160,256]{1,0:T(8,128)S(1)} all-gather(f32[80,256]{1,0:T(8,128)S(1)} %get-tuple-element.28), channel_id=6, replica_groups={{0,384},{8,392},{16,400},{24,408},{32,416},{40,424},{48,432},{56,440},{..., dimensions={0}, use_global_device_ids=true | all-gather | bytes 245760 | tf_op jit(solution)/shard_map/all_gather | solution.py:346
  65.9 1.3 %shard_map.97 = f32[2,320,128]{2,1,0:T(8,128)} custom-call(f32[2,80,256]{2,1,0:T(8,128)S(1)} %bitcast.13, f32[80,640]{1,0:T(8,128)S(1)} %get-tuple-element.29.old_ref, f32[2,320,384]{2,1,0:T(8,128)S(1)} %get-tuple-element.30.keep_ref), custom_call_target="tpu_custom_call" | custom-call | flops 100000000 | bytes 1679360 | tf_op jit(solution)/shard_map/pallas_call | solution.py:319
  (8 shorter events, 0.0 us)
Async XLA Ops:
  0.0 16.0 %copy-start = (f32[2,320,320]{2,1,0:T(8,128)S(1)}, f32[2,320,320]{2,1,0:T(8,128)}, u32[]{:S(2)}) copy-start(f32[2,320,320]{2,1,0:T(8,128)} %inv_ref.1) | copy-start | bytes 2457604
  0.0 16.0 %copy-start.1 = (f32[2,320,128]{2,1,0:T(8,128)S(1)}, f32[2,320,128]{2,1,0:T(8,128)}, u32[]{:S(2)}) copy-start(f32[2,320,128]{2,1,0:T(8,128)} %rhs_ref.1) | copy-start | bytes 983044
  0.0 16.0 %copy-start.2 = (f32[2,80,240]{2,1,0:T(8,128)S(1)}, f32[2,80,240]{2,1,0:T(8,128)}, u32[]{:S(2)}) copy-start(f32[2,80,240]{2,1,0:T(8,128)} %low_ref.1) | copy-start | bytes 460804
  0.0 16.0 %copy-start.3 = (f32[2,80,240]{2,1,0:T(8,128)S(1)}, f32[2,80,240]{2,1,0:T(8,128)}, u32[]{:S(2)}) copy-start(f32[2,80,240]{2,1,0:T(8,128)} %up_ref.1) | copy-start | bytes 460804
  0.0 16.0 %copy-start.4 = (bf16[2,240,320]{2,1,0:T(8,128)(2,1)S(1)}, bf16[2,240,320]{2,1,0:T(8,128)(2,1)}, u32[]{:S(2)}) copy-start(bf16[2,240,320]{2,1,0:T(8,128)(2,1)} %constant.4.clone.take_ref) | copy-start | bytes 921604
  0.0 16.0 %copy-start.5 = (bf16[2,320,240]{2,1,0:T(8,128)(2,1)S(1)}, bf16[2,320,240]{2,1,0:T(8,128)(2,1)}, u32[]{:S(2)}) copy-start(bf16[2,320,240]{2,1,0:T(8,128)(2,1)} %constant.5.clone.put_ref) | copy-start | bytes 921604
  22.8 14.8 %collective-permute-start = (f32[80,512]{1,0:T(8,128)S(1)}, f32[80,512]{1,0:T(8,128)S(1)}, u32[]{:S(2)}, u32[]{:S(2)}) collective-permute-start(f32[80,512]{1,0:T(8,128)S(1)} %get-tuple-element.21.own_ref), channel_id=1, source_target_pairs={{0,16},{8,56},{16,0},{24,40},{32,48},{40,24},{48,32},{56,8},{64,80... | collective-permute-start | bytes 491528 | tf_op jit(solution)/shard_map/ppermute | solution.py:351
  27.1 10.5 %collective-permute-start.1 = (f32[40,512]{1,0:T(8,128)S(1)}, f32[40,512]{1,0:T(8,128)S(1)}, u32[]{:S(2)}, u32[]{:S(2)}) collective-permute-start(f32[40,512]{1,0:T(8,128)S(1)} %get-tuple-element.22), channel_id=1, source_target_pairs={{0,32},{8,40},{16,48},{24,56},{32,0},{40,8},{48,16},{56,24},{64,96... | collective-permute-start | bytes 245768 | tf_op jit(solution)/shard_map/ppermute | solution.py:351

commit v8 on v7

--- a/solution.py
+++ b/solution.py
@@ -245,12 +245,22 @@
         state_ref[:, 4 * HALF :] = product(gain, split(back2))
 
 
-def first_kernel(pair_ref, total_ref, half_ref, state_ref):
+def spread_half(total, half_ref):
+    packed = pack(total[0], None, total[1], total[2])
+    half = TRACE // 2
+    packed = jnp.where(is_upper(0) == 1, packed[half:], packed[:half])
+    for chip in range(half_ref.shape[0]):
+        half_ref[chip] = packed
+
+
+def run_of(halves_ref, chip):
+    return unpack(jnp.concatenate([halves_ref[0, chip], halves_ref[1, chip]], axis=0))
+
+
+def first_kernel(pair_ref, half_ref, state_ref):
     upper = is_upper(0) == 1
     total, (forward1, cross, back2) = merge(unpack(pair_ref[0]), unpack(pair_ref[1]))
-    total = pack(total[0], None, total[1], total[2])
-    total_ref[...] = total
-    half_ref[...] = jnp.where(upper, total[TRACE // 2 :], total[: TRACE // 2])
+    spread_half(total, half_ref)
     lane = lax.broadcasted_iota(jnp.int32, (TRACE, 2 * HALF), 1)
     row = lax.broadcasted_iota(jnp.int32, (TRACE, 2 * HALF), 0)
     eye = jnp.where(lane == row, 1.0, 0.0)
@@ -259,51 +269,45 @@
     state_ref[:, 4 * HALF :] = jnp.where(upper, eye[:, :HALF], back2)
 
 
-def four_kernel(own_ref, others_ref, old_ref, half_ref, state_ref, middle_ref):
+def four_kernel(halves_ref, old_ref, half_ref, state_ref, middle_ref):
     odd, late = is_upper(1) == 1, is_upper(2) == 1
-    own, near, far = own_ref[...], others_ref[0, :TRACE], others_ref[1, :TRACE]
-    middle = jnp.concatenate([others_ref[0, TRACE:], others_ref[1, TRACE:]], axis=0)
-
-    def ordered(swap, one, two):
-        return unpack(jnp.where(swap, two, one)), unpack(jnp.where(swap, one, two))
-
-    mine, pieces = merge(*ordered(odd, own, near))
-    other, _ = merge(*ordered(odd, middle, far))
-    track(odd, pieces, old_ref, middle_ref)
-    earlier = [jnp.where(late, b, a) for a, b in zip(mine, other)]
-    later = [jnp.where(late, a, b) for a, b in zip(mine, other)]
-    total, pieces = merge(earlier, later)
+    front, front_pieces = merge(run_of(halves_ref, 0), run_of(halves_ref, 1))
+    rear, rear_pieces = merge(run_of(halves_ref, 2), run_of(halves_ref, 3))
+    total, pieces = merge(front, rear)
     total = pack(total[0], None, total[1], total[2])
     half_ref[...] = jnp.where(is_upper(0) == 1, total[TRACE // 2 :], total[: TRACE // 2])
+    track(odd, [jnp.where(late, b, a) for a, b in zip(front_pieces, rear_pieces)], old_ref, middle_ref)
     track(late, pieces, middle_ref, state_ref)
 
 
-def combine_kernel(level, sends, pair_ref, old_ref, total_ref, state_ref):
+def combine_kernel(level, pair_ref, old_ref, half_ref, state_ref):
     total, pieces = merge(unpack(pair_ref[0]), unpack(pair_ref[1]))
-    if sends == "top":
-        total_ref[...] = jnp.where(is_upper(level + 1) == 1, total[1], total[0])
-    else:
-        total_ref[...] = pack(total[0], None, total[1], total[2])
+    spread_half(total, half_ref)
     track(is_upper(level) == 1, pieces, old_ref, state_ref)
 
 
-def last_kernel(level, pair_ref, old_ref, keep_ref, out_ref, ends_ref):
-    @pl.when(is_upper(level) == 1)
-    def _():
-        inflow = split(pair_ref[0, :, HALF:])
-        ends_ref[0] = old_ref[:, HALF : 2 * HALF] + product(split(old_ref[:, :TRACE]), inflow)
-        ends_ref[1] = old_ref[:, 3 * HALF : 4 * HALF] + product(split(old_ref[:, 2 * HALF : 2 * HALF + TRACE]), inflow)
-
-    @pl.when(is_upper(level) == 0)
-    def _():
-        outflow = split(pair_ref[0, :, HALF:])
-        value = pair_ref[1, :, HALF:] + product(split(pair_ref[1, :, :TRACE]), outflow)
-        gain = split(old_ref[:, 4 * HALF : 4 * HALF + TRACE])
-        ends_ref[0] = old_ref[:, HALF : 2 * HALF]
-        ends_ref[1] = old_ref[:, 3 * HALF : 4 * HALF] + product(gain, split(value))
-
-    inflow = split(ends_ref[0])
-    incoming = split(ends_ref[1])
+def last_kernel(level, halves_ref, state_ref, keep_ref, out_ref):
+    mine = lax.axis_index("stream") >> level
+    runs = [run_of(halves_ref, line) for line in range(4)]
+
+    def apply(matrix, value, added):
+        return product(split(matrix[:, :TRACE]), split(value)) + added
+
+    zeros = jnp.zeros((TRACE, COLUMNS), F32)
+    flow = [zeros, runs[0][0][:, HALF:]]
+    for line in (1, 2):
+        flow.append(apply(runs[line][0], flow[line], runs[line][0][:, HALF:]))
+    back = [zeros]
+    for line in (3, 2, 1):
+        value = apply(runs[line][1], flow[line], runs[line][1][:, HALF:])
+        back.insert(0, value if line == 3 else apply(runs[line][2], back[0], value))
+    inflow, incoming = flow[0], back[0]
+    for line in (1, 2, 3):
+        inflow = jnp.where(mine == line, flow[line], inflow)
+        incoming = jnp.where(mine == line, back[line], incoming)
+    here = apply(state_ref[:, 2 * HALF : 3 * HALF], inflow, state_ref[:, 3 * HALF : 4 * HALF])
+    incoming = split(apply(state_ref[:, 4 * HALF :], incoming, here))
+    inflow = split(apply(state_ref[:, :HALF], inflow, state_ref[:, HALF : 2 * HALF]))
     for element in range(2):
         known = keep_ref[element]
         out_ref[element] = (
@@ -331,11 +335,10 @@
     return jax.ShapeDtypeStruct(dims, F32)
 
 
-def gather(value, masks):
-    count = lax.axis_size("stream")
+def groups_of(masks):
     masks = [(across * 8 + along) * 2 + core for across, along, core in masks]
     seen, groups = set(), []
-    for device in range(count):
+    for device in range(lax.axis_size("stream")):
         if device in seen:
             continue
         group = {device}
@@ -343,12 +346,16 @@
             group |= {member ^ mask for member in group}
         seen |= group
         groups.append(sorted(group))
-    return lax.all_gather(value, "stream", axis_index_groups=groups)
-
-
-def swap(value, along):
-    count = lax.axis_size("stream")
-    return lax.ppermute(value, "stream", [(k, k ^ (2 * along[k % 2])) for k in range(count)])
+    return groups
+
+
+def gather(value, masks):
+    return lax.all_gather(value, "stream", axis_index_groups=groups_of(masks))
+
+
+def share(halves, masks):
+    halves = lax.all_to_all(halves, "stream", 0, 0, axis_index_groups=groups_of(masks))
+    return gather(halves, [(0, 0, 1)])
 
 
 def shards(rhs, inverse, lower, upper, upwind, rows, target):
@@ -378,28 +385,23 @@
         2 * 10**9,
         limit=24 * 1024,
     )
-    full, half, state = shape(TRACE, 4 * HALF), shape(TRACE // 2, 4 * HALF), shape(TRACE, 5 * HALF)
-    total, part, tracked = call(first_kernel, [full, half, state], [gather(total, [(0, 0, 1)])], 3 * 10**7)
-    received = jnp.concatenate([swap(total, (1, 3)), swap(part, (2, 2))], axis=0)
-    received = gather(received, [(0, 0, 1)])
+    half, state = shape(TRACE // 2, 4 * HALF), shape(TRACE, 5 * HALF)
+    halves = shape(4, TRACE // 2, 4 * HALF)
+    parts, tracked = call(first_kernel, [halves, state], [gather(total, [(0, 0, 1)])], 3 * 10**7)
     part, tracked = call(
         four_kernel,
         [half, state],
-        [total, received, tracked],
+        [share(parts, [(0, 1, 0), (0, 2, 0)]), tracked],
         10**8,
         scratch=[pltpu.VMEM((TRACE, 5 * HALF), F32)],
     )
     pair = gather(part, [(0, 0, 1), (0, 6, 0)]).reshape(2, TRACE, 4 * HALF)
-    total, tracked = call(functools.partial(combine_kernel, 3, "whole"), [full, state], [pair, tracked], 3 * 10**7)
-    pair = gather(total, [(1, 0, 0)])
-    crossing = shape(TRACE, 2 * HALF)
-    total, tracked = call(functools.partial(combine_kernel, 4, "top"), [crossing, state], [pair, tracked], 3 * 10**7)
+    parts, tracked = call(functools.partial(combine_kernel, 3), [halves, state], [pair, tracked], 3 * 10**7)
     return call(
-        functools.partial(last_kernel, 5),
+        functools.partial(last_kernel, 4),
         [shape(local, BLOCK, COLUMNS)],
-        [gather(total, [(3, 0, 0)]), tracked, keep],
+        [share(parts, [(1, 0, 0), (2, 0, 0)]), tracked, keep],
         10**8,
-        scratch=[pltpu.VMEM((2, TRACE, COLUMNS), F32)],
     )
 
 

time: 68.5 us -> 71.8 us (1.048)
  the two profiles are of different devices: /device:TPU:6 before, /device:TPU:1 now
where the time goes in v8:
time: 71.8 us; the launch traced here: 71.5 us
  blocking collectives  61.1 us (85%)
  Pallas kernels  10.3 us (14%)
    all_to_all x2, blocking collectives, share(): lax.all_to_all(halves, 'stream', 0, 0, axis_index_groups=groups_of(masks))  26 us
    all_gather x4, blocking collectives, gather(): return lax.all_gather(value, 'stream', axis_index_groups=groups_of(masks))  20.9 us
    all_to_all x1, blocking collectives, shards(): parts = lax.all_to_all(partial.reshape(groups, local, BLOCK), 'azi', 0, 0)  14.1 us
    pallas_call x6, Pallas kernels, call(): pl.pallas_call(kernel, out_shape=shapes[0] if single else shapes, in_spec...  10.3 us

profile of v8, /device:TPU:1, one launch (start us, length us, event | category | flops | bytes accessed | tf_op | source)
XLA Modules:
  0.0 71.5 jit_solution(16287008083240743456)
XLA Ops:
  0.0 0.0 copy-start
  0.0 0.0 copy-start.1
  0.0 0.0 copy-start.3
  0.0 0.0 copy-start.4
  0.0 0.0 copy-start.5
  0.0 1.2 %shard_map.91 = (f32[16,320]{1,0:T(8,128)S(1)}, f32[8,128]{1,0:T(8,128)S(1)}) custom-call(s32[1,64]{1,0:T(1,128)} %bitcast.13, f32[64,320]{1,0:T(8,128)} %rows_hbm.1, s32[2,3]{1,0:T(2,128)} %upwind_hbm.1), custom_call_target="tpu_custom_call" | custom-call | flops 10000000000 | bytes 106776 | tf_op jit(solution)/shard_map/pallas_call | solution.py:323
  1.3 14.1 %all_to_all.15 = f32[8,2,320]{2,1,0:T(2,128)S(1)} all-to-all(f32[8,2,320]{2,1,0:T(2,128)S(1)} %reshape.10), channel_id=1, replica_groups=mesh['stream'=64,'azi'=8] {'azi'}, dimensions={0} | all-to-all | bytes 40960 | tf_op jit(solution)/shard_map/all_to_all | solution.py:379
  15.4 0.0 copy-done
  15.4 0.0 copy-done.1
  15.4 0.0 copy-done.2
  15.4 0.0 copy-done.3
  15.5 0.0 copy-done.4
  15.5 0.0 copy-done.5
  15.5 4.2 %shard_map.92 = (f32[80,512]{1,0:T(8,128)S(1)}, f32[2,320,384]{2,1,0:T(8,128)S(1)}) custom-call(bf16[2,240,320]{2,1,0:T(8,128)(2,1)S(1)} %copy-done.4, bf16[2,320,240]{2,1,0:T(8,128)(2,1)S(1)} %copy-done.5, f32[8,128]{1,0:T(8,128)S(1)} %get-tuple-element.15.crosses_ref, f32[2,8,320]{2,1,0:T(8,128)S(1)} %bitcast.12, f32[2,80,240]{2,1,0:T(8,128)S(1)} %copy-done.2, ...), custom_call_target="tpu_custom_call" | custom-call | flops 2000000000 | bytes 3854336 | tf_op jit(solution)/shard_map/pallas_call | solution.py:323
  19.7 4.7 %all-gather = f32[160,512]{1,0:T(8,128)S(1)} all-gather(f32[80,512]{1,0:T(8,128)S(1)} %get-tuple-element.17), channel_id=2, replica_groups={{0,8},{16,24},{32,40},{48,56},{64,72},{80,88},{96,104},{112,120},{128,1..., dimensions={0}, use_global_device_ids=true | all-gather | bytes 491520 | tf_op jit(solution)/shard_map/all_gather | solution.py:353
  24.4 0.5 shard_map.93
  24.9 15.5 %all_to_all.16 = f32[4,40,512]{2,1,0:T(8,128)S(1)} all-to-all(f32[4,40,512]{2,1,0:T(8,128)S(1)} %get-tuple-element.18), channel_id=1, replica_groups={{0,16,32,48},{8,24,40,56},{64,80,96,112},{72,88,104,120},{128,144,160,1..., dimensions={0} | all-to-all | bytes 655360 | tf_op jit(solution)/shard_map/all_to_all | solution.py:357
  40.4 3.5 %all-gather.1 = f32[8,40,512]{2,1,0:T(8,128)S(1)} all-gather(f32[4,40,512]{2,1,0:T(8,128)S(1)} %all_to_all.16), channel_id=3, replica_groups={{0,8},{16,24},{32,40},{48,56},{64,72},{80,88},{96,104},{112,120},{128,1..., dimensions={0}, use_global_device_ids=true | all-gather | bytes 983040 | tf_op jit(solution)/shard_map/all_gather | solution.py:353
  43.9 1.5 %shard_map.94 = (f32[40,512]{1,0:T(8,128)S(1)}, f32[80,640]{1,0:T(8,128)S(1)}) custom-call(f32[2,4,40,512]{3,2,1,0:T(8,128)S(1)} %bitcast.9, f32[80,640]{1,0:T(8,128)S(1)} %get-tuple-element.19.old_ref), custom_call_target="tpu_custom_call" | custom-call | flops 100000000 | bytes 1146880 | tf_op jit(solution)/shard_map/pallas_call | solution.py:323
  45.4 9.3 %all-gather.2 = f32[160,512]{1,0:T(8,128)S(1)} all-gather(f32[40,512]{1,0:T(8,128)S(1)} %get-tuple-element.20), channel_id=4, replica_groups={{0,8,96,104},{16,24,112,120},{32,40,64,72},{48,56,80,88},{128,136,224,2..., dimensions={0}, use_global_device_ids=true | all-gather | bytes 409600 | tf_op jit(solution)/shard_map/all_gather | solution.py:353
  54.7 0.7 %shard_map.95 = (f32[4,40,512]{2,1,0:T(8,128)S(1)}, f32[80,640]{1,0:T(8,128)S(1)}) custom-call(f32[2,80,512]{2,1,0:T(8,128)S(1)} %bitcast.10, f32[80,640]{1,0:T(8,128)S(1)} %get-tuple-element.21.old_ref), custom_call_target="tpu_custom_call" | custom-call | flops 30000000 | bytes 1064960 | tf_op jit(solution)/shard_map/pallas_call | solution.py:323
  55.4 10.6 %all_to_all.17 = f32[4,40,512]{2,1,0:T(8,128)S(1)} all-to-all(f32[4,40,512]{2,1,0:T(8,128)S(1)} %get-tuple-element.22), channel_id=1, replica_groups={{0,128,256,384},{8,136,264,392},{16,144,272,400},{24,152,280,408},{32,1..., dimensions={0} | all-to-all | bytes 655360 | tf_op jit(solution)/shard_map/all_to_all | solution.py:357
  66.0 3.5 %all-gather.3 = f32[8,40,512]{2,1,0:T(8,128)S(1)} all-gather(f32[4,40,512]{2,1,0:T(8,128)S(1)} %all_to_all.17), channel_id=5, replica_groups={{0,8},{16,24},{32,40},{48,56},{64,72},{80,88},{96,104},{112,120},{128,1..., dimensions={0}, use_global_device_ids=true | all-gather | bytes 983040 | tf_op jit(solution)/shard_map/all_gather | solution.py:353
  69.5 2.1 %shard_map.96 = f32[2,320,128]{2,1,0:T(8,128)} custom-call(f32[2,4,40,512]{3,2,1,0:T(8,128)S(1)} %bitcast.8, f32[80,640]{1,0:T(8,128)S(1)} %get-tuple-element.23.state_ref, f32[2,320,384]{2,1,0:T(8,128)S(1)} %get-tuple-element.24.keep_ref), custom_call_target="tpu_custom_call" | custom-call | flops 100000000 | bytes 2170880 | tf_op jit(solution)/shard_map/pallas_call | solution.py:323
  (3 shorter events, 0.0 us)
Async XLA Ops:
  0.0 15.4 %copy-start = (f32[2,320,320]{2,1,0:T(8,128)S(1)}, f32[2,320,320]{2,1,0:T(8,128)}, u32[]{:S(2)}) copy-start(f32[2,320,320]{2,1,0:T(8,128)} %inv_ref.1) | copy-start | bytes 2457604
  0.0 15.4 %copy-start.1 = (f32[2,320,128]{2,1,0:T(8,128)S(1)}, f32[2,320,128]{2,1,0:T(8,128)}, u32[]{:S(2)}) copy-start(f32[2,320,128]{2,1,0:T(8,128)} %rhs_ref.1) | copy-start | bytes 983044
  0.0 15.4 %copy-start.2 = (f32[2,80,240]{2,1,0:T(8,128)S(1)}, f32[2,80,240]{2,1,0:T(8,128)}, u32[]{:S(2)}) copy-start(f32[2,80,240]{2,1,0:T(8,128)} %low_ref.1) | copy-start | bytes 460804
  0.0 15.4 %copy-start.3 = (f32[2,80,240]{2,1,0:T(8,128)S(1)}, f32[2,80,240]{2,1,0:T(8,128)}, u32[]{:S(2)}) copy-start(f32[2,80,240]{2,1,0:T(8,128)} %up_ref.1) | copy-start | bytes 460804
  0.0 15.4 %copy-start.4 = (bf16[2,240,320]{2,1,0:T(8,128)(2,1)S(1)}, bf16[2,240,320]{2,1,0:T(8,128)(2,1)}, u32[]{:S(2)}) copy-start(bf16[2,240,320]{2,1,0:T(8,128)(2,1)} %constant.4.clone.take_ref) | copy-start | bytes 921604
  0.0 15.4 %copy-start.5 = (bf16[2,320,240]{2,1,0:T(8,128)(2,1)S(1)}, bf16[2,320,240]{2,1,0:T(8,128)(2,1)}, u32[]{:S(2)}) copy-start(bf16[2,320,240]{2,1,0:T(8,128)(2,1)} %constant.5.clone.put_ref) | copy-start | bytes 921604

commit v9 on v7

--- a/solution.py
+++ b/solution.py
@@ -278,39 +278,38 @@
     track(late, pieces, middle_ref, state_ref)
 
 
-def combine_kernel(level, sends, pair_ref, old_ref, total_ref, state_ref):
+def combine_kernel(level, sends, pair_ref, old_ref, half_ref, state_ref):
     total, pieces = merge(unpack(pair_ref[0]), unpack(pair_ref[1]))
     if sends == "top":
-        total_ref[...] = jnp.where(is_upper(level + 1) == 1, total[1], total[0])
+        total = jnp.where(is_upper(level + 1) == 1, total[1], total[0])
     else:
-        total_ref[...] = pack(total[0], None, total[1], total[2])
+        total = pack(total[0], None, total[1], total[2])
+    half_ref[...] = jnp.where(is_upper(0) == 1, total[TRACE // 2 :], total[: TRACE // 2])
     track(is_upper(level) == 1, pieces, old_ref, state_ref)
 
 
 def last_kernel(level, pair_ref, old_ref, keep_ref, out_ref, ends_ref):
+    ends_ref[:, TRACE:] = jnp.zeros((2, HALF - TRACE, COLUMNS), F32)
+
     @pl.when(is_upper(level) == 1)
     def _():
         inflow = split(pair_ref[0, :, HALF:])
-        ends_ref[0] = old_ref[:, HALF : 2 * HALF] + product(split(old_ref[:, :TRACE]), inflow)
-        ends_ref[1] = old_ref[:, 3 * HALF : 4 * HALF] + product(split(old_ref[:, 2 * HALF : 2 * HALF + TRACE]), inflow)
+        ends_ref[0, :TRACE] = old_ref[:, HALF : 2 * HALF] + product(split(old_ref[:, :TRACE]), inflow)
+        ends_ref[1, :TRACE] = old_ref[:, 3 * HALF : 4 * HALF] + product(split(old_ref[:, 2 * HALF : 2 * HALF + TRACE]), inflow)
 
     @pl.when(is_upper(level) == 0)
     def _():
         outflow = split(pair_ref[0, :, HALF:])
         value = pair_ref[1, :, HALF:] + product(split(pair_ref[1, :, :TRACE]), outflow)
         gain = split(old_ref[:, 4 * HALF : 4 * HALF + TRACE])
-        ends_ref[0] = old_ref[:, HALF : 2 * HALF]
-        ends_ref[1] = old_ref[:, 3 * HALF : 4 * HALF] + product(gain, split(value))
-
-    inflow = split(ends_ref[0])
-    incoming = split(ends_ref[1])
+        ends_ref[0, :TRACE] = old_ref[:, HALF : 2 * HALF]
+        ends_ref[1, :TRACE] = old_ref[:, 3 * HALF : 4 * HALF] + product(gain, split(value))
+
+    ends = split(ends_ref[...].reshape(2 * HALF, COLUMNS))
     for element in range(2):
         known = keep_ref[element]
-        out_ref[element] = (
-            known[:, HALF : 2 * HALF]
-            + product(split(known[:, :TRACE]), inflow)
-            + product(split(known[:, 2 * HALF : 2 * HALF + TRACE]), incoming)
-        )
+        maps = jnp.concatenate([known[:, :HALF], known[:, 2 * HALF :]], axis=1)
+        out_ref[element] = known[:, HALF : 2 * HALF] + product(split(maps), ends)
 
 
 def call(kernel, shapes, operands, flops, specs=None, scratch=(), limit=8 * 1024):
@@ -390,16 +389,17 @@
         scratch=[pltpu.VMEM((TRACE, 5 * HALF), F32)],
     )
     pair = gather(part, [(0, 0, 1), (0, 6, 0)]).reshape(2, TRACE, 4 * HALF)
-    total, tracked = call(functools.partial(combine_kernel, 3, "whole"), [full, state], [pair, tracked], 3 * 10**7)
-    pair = gather(total, [(1, 0, 0)])
-    crossing = shape(TRACE, 2 * HALF)
-    total, tracked = call(functools.partial(combine_kernel, 4, "top"), [crossing, state], [pair, tracked], 3 * 10**7)
+    part, tracked = call(functools.partial(combine_kernel, 3, "whole"), [half, state], [pair, tracked], 3 * 10**7)
+    pair = gather(part, [(0, 0, 1), (1, 0, 0)]).reshape(2, TRACE, 4 * HALF)
+    crossing = shape(TRACE // 2, 2 * HALF)
+    part, tracked = call(functools.partial(combine_kernel, 4, "top"), [crossing, state], [pair, tracked], 3 * 10**7)
+    pair = gather(part, [(0, 0, 1), (3, 0, 0)]).reshape(2, TRACE, 2 * HALF)
     return call(
         functools.partial(last_kernel, 5),
         [shape(local, BLOCK, COLUMNS)],
-        [gather(total, [(3, 0, 0)]), tracked, keep],
+        [pair, tracked, keep],
         10**8,
-        scratch=[pltpu.VMEM((2, TRACE, COLUMNS), F32)],
+        scratch=[pltpu.VMEM((2, HALF, COLUMNS), F32)],
     )
 
 

time: 68.5 us -> 68.5 us (level)
  the two profiles are of different devices: /device:TPU:6 before, /device:TPU:1 now
where the time goes in v9:
time: 68.5 us; the launch traced here: 68.3 us
  blocking collectives  43.6 us (64%)
  Pallas kernels  10.4 us (15%)
  starting transfers between devices  8.59 us (13%)
  waiting for transfers between devices  5.55 us (8%)
    all_gather x5, blocking collectives, gather(): return lax.all_gather(value, 'stream', axis_index_groups=groups)  29.4 us
    all_to_all x1, blocking collectives, shards(): parts = lax.all_to_all(partial.reshape(groups, local, BLOCK), 'azi', 0, 0)  14.1 us
    pallas_call x7, Pallas kernels, call(): pl.pallas_call(kernel, out_shape=shapes[0] if single else shapes, in_spec...  10.4 us
    ppermute x2, starting transfers between devices, swap(): lax.ppermute(value, 'stream', [(k, k ^ 2 * along[k % 2]) for k in range(c...  8.59 us
    ppermute x2, waiting for transfers between devices, swap(): lax.ppermute(value, 'stream', [(k, k ^ 2 * along[k % 2]) for k in range(c...  5.55 us
  transfers between devices with their start and end apart: 2, of which 1 were waited for; matrix products, arithmetic and copies ran while one was open for 0% of the time, Pallas kernels for 0%

profile of v9, /device:TPU:1, one launch (start us, length us, event | category | flops | bytes accessed | tf_op | source)
XLA Modules:
  0.0 68.3 jit_solution(2140497622905373581)
XLA Ops:
  0.0 0.0 copy-start.3
  0.0 0.0 copy-start.4
  0.0 0.0 copy-start.5
  0.0 1.2 %shard_map.91 = (f32[16,320]{1,0:T(8,128)S(1)}, f32[8,128]{1,0:T(8,128)S(1)}) custom-call(s32[1,64]{1,0:T(1,128)} %bitcast.15, f32[64,320]{1,0:T(8,128)} %rows_hbm.1, s32[2,3]{1,0:T(2,128)} %upwind_hbm.1), custom_call_target="tpu_custom_call" | custom-call | flops 10000000000 | bytes 106776 | tf_op jit(solution)/shard_map/pallas_call | solution.py:318
  1.3 14.1 %all_to_all.5 = f32[8,2,320]{2,1,0:T(2,128)S(1)} all-to-all(f32[8,2,320]{2,1,0:T(2,128)S(1)} %reshape.16), channel_id=1, replica_groups=mesh['stream'=64,'azi'=8] {'azi'}, dimensions={0} | all-to-all | bytes 40960 | tf_op jit(solution)/shard_map/all_to_all | solution.py:371
  15.4 0.0 copy-done
  15.4 0.0 copy-done.1
  15.4 0.0 copy-done.2
  15.4 0.0 copy-done.3
  15.5 4.2 %shard_map.92 = (f32[80,512]{1,0:T(8,128)S(1)}, f32[2,320,384]{2,1,0:T(8,128)S(1)}) custom-call(bf16[2,240,320]{2,1,0:T(8,128)(2,1)S(1)} %copy-done.4, bf16[2,320,240]{2,1,0:T(8,128)(2,1)S(1)} %copy-done.5, f32[8,128]{1,0:T(8,128)S(1)} %get-tuple-element.18.crosses_ref, f32[2,8,320]{2,1,0:T(8,128)S(1)} %bitcast.14, f32[2,80,240]{2,1,0:T(8,128)S(1)} %copy-done.2, ...), custom_call_target="tpu_custom_call" | custom-call | flops 2000000000 | bytes 3854336 | tf_op jit(solution)/shard_map/pallas_call | solution.py:318
  19.7 4.7 %all-gather = f32[160,512]{1,0:T(8,128)S(1)} all-gather(f32[80,512]{1,0:T(8,128)S(1)} %get-tuple-element.20), channel_id=2, replica_groups={{0,8},{16,24},{32,40},{48,56},{64,72},{80,88},{96,104},{112,120},{128,1..., dimensions={0}, use_global_device_ids=true | all-gather | bytes 491520 | tf_op jit(solution)/shard_map/all_gather | solution.py:345
  24.4 0.5 shard_map.93
  24.9 6.7 %collective-permute-start = (f32[80,512]{1,0:T(8,128)S(1)}, f32[80,512]{1,0:T(8,128)S(1)}, u32[]{:S(2)}, u32[]{:S(2)}) collective-permute-start(f32[80,512]{1,0:T(8,128)S(1)} %get-tuple-element.21.own_ref), channel_id=1, source_target_pairs={{0,16},{8,56},{16,0},{24,40},{32,48},{40,24},{48,32},{56,8},{64,80... | collective-permute-start | bytes 491528 | tf_op jit(solution)/shard_map/ppermute | solution.py:350
  31.6 1.9 %collective-permute-start.1 = (f32[40,512]{1,0:T(8,128)S(1)}, f32[40,512]{1,0:T(8,128)S(1)}, u32[]{:S(2)}, u32[]{:S(2)}) collective-permute-start(f32[40,512]{1,0:T(8,128)S(1)} %get-tuple-element.22), channel_id=1, source_target_pairs={{0,32},{8,40},{16,48},{24,56},{32,0},{40,8},{48,16},{56,24},{64,96... | collective-permute-start | bytes 245768 | tf_op jit(solution)/shard_map/ppermute | solution.py:350
  33.5 5.5 %collective-permute-done.1 = f32[40,512]{1,0:T(8,128)S(1)} collective-permute-done((f32[40,512]{1,0:T(8,128)S(1)}, f32[40,512]{1,0:T(8,128)S(1)}, u32[]{:S(2)}, u32[]{:S(2)}) %collective-permute-start.1) | collective-permute-done | bytes 81952 | tf_op jit(solution)/shard_map/ppermute | solution.py:350
  39.1 0.0 collective-permute-done
  39.1 2.2 %all-gather.1 = f32[240,512]{1,0:T(8,128)S(1)} all-gather(f32[120,512]{1,0:T(8,128)S(1)} %pad_maximum_fusion), channel_id=3, replica_groups={{0,8},{16,24},{32,40},{48,56},{64,72},{80,88},{96,104},{112,120},{128,1..., dimensions={0}, use_global_device_ids=true | all-gather | bytes 737280 | tf_op jit(solution)/shard_map/all_gather | solution.py:345
  41.3 1.6 %shard_map.94 = (f32[40,512]{1,0:T(8,128)S(1)}, f32[80,640]{1,0:T(8,128)S(1)}) custom-call(f32[80,512]{1,0:T(8,128)S(1)} %get-tuple-element.21.own_ref, f32[2,120,512]{2,1,0:T(8,128)S(1)} %bitcast.9, f32[80,640]{1,0:T(8,128)S(1)} %get-tuple-element.23.old_ref), custom_call_target="tpu_custom_call" | custom-call | flops 100000000 | bytes 1146880 | tf_op jit(solution)/shard_map/pallas_call | solution.py:318
  42.8 9.6 %all-gather.2 = f32[160,512]{1,0:T(8,128)S(1)} all-gather(f32[40,512]{1,0:T(8,128)S(1)} %get-tuple-element.24), channel_id=4, replica_groups={{0,8,96,104},{16,24,112,120},{32,40,64,72},{48,56,80,88},{128,136,224,2..., dimensions={0}, use_global_device_ids=true | all-gather | bytes 409600 | tf_op jit(solution)/shard_map/all_gather | solution.py:345
  52.5 0.7 %shard_map.95 = (f32[40,512]{1,0:T(8,128)S(1)}, f32[80,640]{1,0:T(8,128)S(1)}) custom-call(f32[2,80,512]{2,1,0:T(8,128)S(1)} %bitcast.10, f32[80,640]{1,0:T(8,128)S(1)} %get-tuple-element.25.old_ref), custom_call_target="tpu_custom_call" | custom-call | flops 30000000 | bytes 819200 | tf_op jit(solution)/shard_map/pallas_call | solution.py:318
  53.2 6.2 %all-gather.3 = f32[160,512]{1,0:T(8,128)S(1)} all-gather(f32[40,512]{1,0:T(8,128)S(1)} %get-tuple-element.26), channel_id=5, replica_groups={{0,8,128,136},{16,24,144,152},{32,40,160,168},{48,56,176,184},{64,72,19..., dimensions={0}, use_global_device_ids=true | all-gather | bytes 409600 | tf_op jit(solution)/shard_map/all_gather | solution.py:345
  59.4 0.6 shard_map.96
  60.1 6.7 %all-gather.4 = f32[160,256]{1,0:T(8,128)S(1)} all-gather(f32[40,256]{1,0:T(8,128)S(1)} %get-tuple-element.28), channel_id=6, replica_groups={{0,8,384,392},{16,24,400,408},{32,40,416,424},{48,56,432,440},{64,72,44..., dimensions={0}, use_global_device_ids=true | all-gather | bytes 204800 | tf_op jit(solution)/shard_map/all_gather | solution.py:345
  66.8 1.5 %shard_map.97 = f32[2,320,128]{2,1,0:T(8,128)} custom-call(f32[2,80,256]{2,1,0:T(8,128)S(1)} %bitcast.13, f32[80,640]{1,0:T(8,128)S(1)} %get-tuple-element.29.old_ref, f32[2,320,384]{2,1,0:T(8,128)S(1)} %get-tuple-element.30.keep_ref), custom_call_target="tpu_custom_call" | custom-call | flops 100000000 | bytes 1679360 | tf_op jit(solution)/shard_map/pallas_call | solution.py:318
  (8 shorter events, 0.0 us)
Async XLA Ops:
  0.0 15.4 %copy-start = (f32[2,320,320]{2,1,0:T(8,128)S(1)}, f32[2,320,320]{2,1,0:T(8,128)}, u32[]{:S(2)}) copy-start(f32[2,320,320]{2,1,0:T(8,128)} %inv_ref.1) | copy-start | bytes 2457604
  0.0 15.4 %copy-start.1 = (f32[2,320,128]{2,1,0:T(8,128)S(1)}, f32[2,320,128]{2,1,0:T(8,128)}, u32[]{:S(2)}) copy-start(f32[2,320,128]{2,1,0:T(8,128)} %rhs_ref.1) | copy-start | bytes 983044
  0.0 15.4 %copy-start.2 = (f32[2,80,240]{2,1,0:T(8,128)S(1)}, f32[2,80,240]{2,1,0:T(8,128)}, u32[]{:S(2)}) copy-start(f32[2,80,240]{2,1,0:T(8,128)} %low_ref.1) | copy-start | bytes 460804
  0.0 15.4 %copy-start.3 = (f32[2,80,240]{2,1,0:T(8,128)S(1)}, f32[2,80,240]{2,1,0:T(8,128)}, u32[]{:S(2)}) copy-start(f32[2,80,240]{2,1,0:T(8,128)} %up_ref.1) | copy-start | bytes 460804
  0.0 15.4 %copy-start.4 = (bf16[2,240,320]{2,1,0:T(8,128)(2,1)S(1)}, bf16[2,240,320]{2,1,0:T(8,128)(2,1)}, u32[]{:S(2)}) copy-start(bf16[2,240,320]{2,1,0:T(8,128)(2,1)} %constant.4.clone.take_ref) | copy-start | bytes 921604
  0.0 15.4 %copy-start.5 = (bf16[2,320,240]{2,1,0:T(8,128)(2,1)S(1)}, bf16[2,320,240]{2,1,0:T(8,128)(2,1)}, u32[]{:S(2)}) copy-start(bf16[2,320,240]{2,1,0:T(8,128)(2,1)} %constant.5.clone.put_ref) | copy-start | bytes 921604
  24.9 14.2 %collective-permute-start = (f32[80,512]{1,0:T(8,128)S(1)}, f32[80,512]{1,0:T(8,128)S(1)}, u32[]{:S(2)}, u32[]{:S(2)}) collective-permute-start(f32[80,512]{1,0:T(8,128)S(1)} %get-tuple-element.21.own_ref), channel_id=1, source_target_pairs={{0,16},{8,56},{16,0},{24,40},{32,48},{40,24},{48,32},{56,8},{64,80... | collective-permute-start | bytes 491528 | tf_op jit(solution)/shard_map/ppermute | solution.py:350
  31.6 7.5 %collective-permute-start.1 = (f32[40,512]{1,0:T(8,128)S(1)}, f32[40,512]{1,0:T(8,128)S(1)}, u32[]{:S(2)}, u32[]{:S(2)}) collective-permute-start(f32[40,512]{1,0:T(8,128)S(1)} %get-tuple-element.22), channel_id=1, source_target_pairs={{0,32},{8,40},{16,48},{24,56},{32,0},{40,8},{48,16},{56,24},{64,96... | collective-permute-start | bytes 245768 | tf_op jit(solution)/shard_map/ppermute | solution.py:350

commit v10 on v9

--- a/solution.py
+++ b/solution.py
@@ -278,13 +278,15 @@
     track(late, pieces, middle_ref, state_ref)
 
 
-def combine_kernel(level, sends, pair_ref, old_ref, half_ref, state_ref):
+def combine_kernel(level, sends, pair_ref, old_ref, total_ref, state_ref):
     total, pieces = merge(unpack(pair_ref[0]), unpack(pair_ref[1]))
     if sends == "top":
         total = jnp.where(is_upper(level + 1) == 1, total[1], total[0])
     else:
         total = pack(total[0], None, total[1], total[2])
-    half_ref[...] = jnp.where(is_upper(0) == 1, total[TRACE // 2 :], total[: TRACE // 2])
+    if sends != "top":
+        total = jnp.where(is_upper(0) == 1, total[TRACE // 2 :], total[: TRACE // 2])
+    total_ref[...] = total
     track(is_upper(level) == 1, pieces, old_ref, state_ref)
 
 
@@ -379,7 +381,8 @@
     )
     full, half, state = shape(TRACE, 4 * HALF), shape(TRACE // 2, 4 * HALF), shape(TRACE, 5 * HALF)
     total, part, tracked = call(first_kernel, [full, half, state], [gather(total, [(0, 0, 1)])], 3 * 10**7)
-    received = jnp.concatenate([swap(total, (1, 3)), swap(part, (2, 2))], axis=0)
+    part = swap(part, (2, 2))
+    received = jnp.concatenate([swap(total, (1, 3)), part], axis=0)
     received = gather(received, [(0, 0, 1)])
     part, tracked = call(
         four_kernel,
@@ -391,9 +394,9 @@
     pair = gather(part, [(0, 0, 1), (0, 6, 0)]).reshape(2, TRACE, 4 * HALF)
     part, tracked = call(functools.partial(combine_kernel, 3, "whole"), [half, state], [pair, tracked], 3 * 10**7)
     pair = gather(part, [(0, 0, 1), (1, 0, 0)]).reshape(2, TRACE, 4 * HALF)
-    crossing = shape(TRACE // 2, 2 * HALF)
-    part, tracked = call(functools.partial(combine_kernel, 4, "top"), [crossing, state], [pair, tracked], 3 * 10**7)
-    pair = gather(part, [(0, 0, 1), (3, 0, 0)]).reshape(2, TRACE, 2 * HALF)
+    crossing = shape(TRACE, 2 * HALF)
+    total, tracked = call(functools.partial(combine_kernel, 4, "top"), [crossing, state], [pair, tracked], 3 * 10**7)
+    pair = gather(total, [(3, 0, 0)])
     return call(
         functools.partial(last_kernel, 5),
         [shape(local, BLOCK, COLUMNS)],

time: 68.5 us -> 67.9 us (level)
  the two profiles are of different devices: /device:TPU:1 before, /device:TPU:6 now
where the time goes in v10:
time: 67.9 us; the launch traced here: 66.6 us
  blocking collectives  41.4 us (61%)
  starting transfers between devices  10.4 us (15%)
  Pallas kernels  10.2 us (15%)
  waiting for transfers between devices  4.43 us (7%)
    all_gather x5, blocking collectives, gather(): return lax.all_gather(value, 'stream', axis_index_groups=groups)  26.7 us
    all_to_all x1, blocking collectives, shards(): parts = lax.all_to_all(partial.reshape(groups, local, BLOCK), 'azi', 0, 0)  14.7 us
    ppermute x2, starting transfers between devices, swap(): lax.ppermute(value, 'stream', [(k, k ^ 2 * along[k % 2]) for k in range(c...  10.4 us
    pallas_call x7, Pallas kernels, call(): pl.pallas_call(kernel, out_shape=shapes[0] if single else shapes, in_spec...  10.2 us
    ppermute x2, waiting for transfers between devices, swap(): lax.ppermute(value, 'stream', [(k, k ^ 2 * along[k % 2]) for k in range(c...  4.43 us
  transfers between devices with their start and end apart: 2, of which 1 were waited for; matrix products, arithmetic and copies ran while one was open for 0% of the time, Pallas kernels for 0%

profile of v10, /device:TPU:6, one launch (start us, length us, event | category | flops | bytes accessed | tf_op | source)
XLA Modules:
  0.0 66.6 jit_solution(10465154851918294511)
XLA Ops:
  0.0 0.0 copy-start.3
  0.0 0.0 copy-start.4
  0.0 0.0 copy-start.5
  0.0 1.2 %shard_map.91 = (f32[16,320]{1,0:T(8,128)S(1)}, f32[8,128]{1,0:T(8,128)S(1)}) custom-call(s32[1,64]{1,0:T(1,128)} %bitcast.15, f32[64,320]{1,0:T(8,128)} %rows_hbm.1, s32[2,3]{1,0:T(2,128)} %upwind_hbm.1), custom_call_target="tpu_custom_call" | custom-call | flops 10000000000 | bytes 106776 | tf_op jit(solution)/shard_map/pallas_call | solution.py:320
  1.3 14.7 %all_to_all.5 = f32[8,2,320]{2,1,0:T(2,128)S(1)} all-to-all(f32[8,2,320]{2,1,0:T(2,128)S(1)} %reshape.13), channel_id=1, replica_groups=mesh['stream'=64,'azi'=8] {'azi'}, dimensions={0} | all-to-all | bytes 40960 | tf_op jit(solution)/shard_map/all_to_all | solution.py:373
  16.0 0.0 copy-done
  16.0 0.0 copy-done.1
  16.0 0.0 copy-done.2
  16.0 0.0 copy-done.3
  16.1 4.2 %shard_map.92 = (f32[80,512]{1,0:T(8,128)S(1)}, f32[2,320,384]{2,1,0:T(8,128)S(1)}) custom-call(bf16[2,240,320]{2,1,0:T(8,128)(2,1)S(1)} %copy-done.4, bf16[2,320,240]{2,1,0:T(8,128)(2,1)S(1)} %copy-done.5, f32[8,128]{1,0:T(8,128)S(1)} %get-tuple-element.18.crosses_ref, f32[2,8,320]{2,1,0:T(8,128)S(1)} %bitcast.14, f32[2,80,240]{2,1,0:T(8,128)S(1)} %copy-done.2, ...), custom_call_target="tpu_custom_call" | custom-call | flops 2000000000 | bytes 3854336 | tf_op jit(solution)/shard_map/pallas_call | solution.py:320
  20.3 2.0 %all-gather = f32[160,512]{1,0:T(8,128)S(1)} all-gather(f32[80,512]{1,0:T(8,128)S(1)} %get-tuple-element.20), channel_id=2, replica_groups={{0,8},{16,24},{32,40},{48,56},{64,72},{80,88},{96,104},{112,120},{128,1..., dimensions={0}, use_global_device_ids=true | all-gather | bytes 491520 | tf_op jit(solution)/shard_map/all_gather | solution.py:347
  22.3 0.5 shard_map.93
  22.8 4.3 %collective-permute-start = (f32[80,512]{1,0:T(8,128)S(1)}, f32[80,512]{1,0:T(8,128)S(1)}, u32[]{:S(2)}, u32[]{:S(2)}) collective-permute-start(f32[80,512]{1,0:T(8,128)S(1)} %get-tuple-element.21.own_ref), channel_id=1, source_target_pairs={{0,16},{8,56},{16,0},{24,40},{32,48},{40,24},{48,32},{56,8},{64,80... | collective-permute-start | bytes 491528 | tf_op jit(solution)/shard_map/ppermute | solution.py:352
  27.1 6.1 %collective-permute-start.1 = (f32[40,512]{1,0:T(8,128)S(1)}, f32[40,512]{1,0:T(8,128)S(1)}, u32[]{:S(2)}, u32[]{:S(2)}) collective-permute-start(f32[40,512]{1,0:T(8,128)S(1)} %get-tuple-element.22), channel_id=1, source_target_pairs={{0,32},{8,40},{16,48},{24,56},{32,0},{40,8},{48,16},{56,24},{64,96... | collective-permute-start | bytes 245768 | tf_op jit(solution)/shard_map/ppermute | solution.py:352
  33.2 4.4 %collective-permute-done.1 = f32[40,512]{1,0:T(8,128)S(1)} collective-permute-done((f32[40,512]{1,0:T(8,128)S(1)}, f32[40,512]{1,0:T(8,128)S(1)}, u32[]{:S(2)}, u32[]{:S(2)}) %collective-permute-start.1) | collective-permute-done | bytes 81952 | tf_op jit(solution)/shard_map/ppermute | solution.py:352
  37.6 0.0 collective-permute-done
  37.7 2.2 %all-gather.1 = f32[240,512]{1,0:T(8,128)S(1)} all-gather(f32[120,512]{1,0:T(8,128)S(1)} %pad_maximum_fusion), channel_id=3, replica_groups={{0,8},{16,24},{32,40},{48,56},{64,72},{80,88},{96,104},{112,120},{128,1..., dimensions={0}, use_global_device_ids=true | all-gather | bytes 737280 | tf_op jit(solution)/shard_map/all_gather | solution.py:347
  39.9 1.6 %shard_map.94 = (f32[40,512]{1,0:T(8,128)S(1)}, f32[80,640]{1,0:T(8,128)S(1)}) custom-call(f32[80,512]{1,0:T(8,128)S(1)} %get-tuple-element.21.own_ref, f32[2,120,512]{2,1,0:T(8,128)S(1)} %bitcast.9, f32[80,640]{1,0:T(8,128)S(1)} %get-tuple-element.23.old_ref), custom_call_target="tpu_custom_call" | custom-call | flops 100000000 | bytes 1146880 | tf_op jit(solution)/shard_map/pallas_call | solution.py:320
  41.5 9.6 %all-gather.2 = f32[160,512]{1,0:T(8,128)S(1)} all-gather(f32[40,512]{1,0:T(8,128)S(1)} %get-tuple-element.24), channel_id=4, replica_groups={{0,8,96,104},{16,24,112,120},{32,40,64,72},{48,56,80,88},{128,136,224,2..., dimensions={0}, use_global_device_ids=true | all-gather | bytes 409600 | tf_op jit(solution)/shard_map/all_gather | solution.py:347
  51.1 0.7 %shard_map.95 = (f32[40,512]{1,0:T(8,128)S(1)}, f32[80,640]{1,0:T(8,128)S(1)}) custom-call(f32[2,80,512]{2,1,0:T(8,128)S(1)} %bitcast.10, f32[80,640]{1,0:T(8,128)S(1)} %get-tuple-element.25.old_ref), custom_call_target="tpu_custom_call" | custom-call | flops 30000000 | bytes 819200 | tf_op jit(solution)/shard_map/pallas_call | solution.py:320
  51.8 6.2 %all-gather.3 = f32[160,512]{1,0:T(8,128)S(1)} all-gather(f32[40,512]{1,0:T(8,128)S(1)} %get-tuple-element.26), channel_id=5, replica_groups={{0,8,128,136},{16,24,144,152},{32,40,160,168},{48,56,176,184},{64,72,19..., dimensions={0}, use_global_device_ids=true | all-gather | bytes 409600 | tf_op jit(solution)/shard_map/all_gather | solution.py:347
  58.1 0.6 shard_map.96
  58.7 6.6 %all-gather.4 = f32[160,256]{1,0:T(8,128)S(1)} all-gather(f32[80,256]{1,0:T(8,128)S(1)} %get-tuple-element.28), channel_id=6, replica_groups={{0,384},{8,392},{16,400},{24,408},{32,416},{40,424},{48,432},{56,440},{..., dimensions={0}, use_global_device_ids=true | all-gather | bytes 245760 | tf_op jit(solution)/shard_map/all_gather | solution.py:347
  65.3 1.4 %shard_map.97 = f32[2,320,128]{2,1,0:T(8,128)} custom-call(f32[2,80,256]{2,1,0:T(8,128)S(1)} %bitcast.13, f32[80,640]{1,0:T(8,128)S(1)} %get-tuple-element.29.old_ref, f32[2,320,384]{2,1,0:T(8,128)S(1)} %get-tuple-element.30.keep_ref), custom_call_target="tpu_custom_call" | custom-call | flops 100000000 | bytes 1679360 | tf_op jit(solution)/shard_map/pallas_call | solution.py:320
  (8 shorter events, 0.0 us)
Async XLA Ops:
  0.0 16.0 %copy-start = (f32[2,320,320]{2,1,0:T(8,128)S(1)}, f32[2,320,320]{2,1,0:T(8,128)}, u32[]{:S(2)}) copy-start(f32[2,320,320]{2,1,0:T(8,128)} %inv_ref.1) | copy-start | bytes 2457604
  0.0 16.0 %copy-start.1 = (f32[2,320,128]{2,1,0:T(8,128)S(1)}, f32[2,320,128]{2,1,0:T(8,128)}, u32[]{:S(2)}) copy-start(f32[2,320,128]{2,1,0:T(8,128)} %rhs_ref.1) | copy-start | bytes 983044
  0.0 16.0 %copy-start.2 = (f32[2,80,240]{2,1,0:T(8,128)S(1)}, f32[2,80,240]{2,1,0:T(8,128)}, u32[]{:S(2)}) copy-start(f32[2,80,240]{2,1,0:T(8,128)} %low_ref.1) | copy-start | bytes 460804
  0.0 16.0 %copy-start.3 = (f32[2,80,240]{2,1,0:T(8,128)S(1)}, f32[2,80,240]{2,1,0:T(8,128)}, u32[]{:S(2)}) copy-start(f32[2,80,240]{2,1,0:T(8,128)} %up_ref.1) | copy-start | bytes 460804
  0.0 16.0 %copy-start.4 = (bf16[2,240,320]{2,1,0:T(8,128)(2,1)S(1)}, bf16[2,240,320]{2,1,0:T(8,128)(2,1)}, u32[]{:S(2)}) copy-start(bf16[2,240,320]{2,1,0:T(8,128)(2,1)} %constant.4.clone.take_ref) | copy-start | bytes 921604
  0.0 16.0 %copy-start.5 = (bf16[2,320,240]{2,1,0:T(8,128)(2,1)S(1)}, bf16[2,320,240]{2,1,0:T(8,128)(2,1)}, u32[]{:S(2)}) copy-start(bf16[2,320,240]{2,1,0:T(8,128)(2,1)} %constant.5.clone.put_ref) | copy-start | bytes 921604
  22.8 14.8 %collective-permute-start = (f32[80,512]{1,0:T(8,128)S(1)}, f32[80,512]{1,0:T(8,128)S(1)}, u32[]{:S(2)}, u32[]{:S(2)}) collective-permute-start(f32[80,512]{1,0:T(8,128)S(1)} %get-tuple-element.21.own_ref), channel_id=1, source_target_pairs={{0,16},{8,56},{16,0},{24,40},{32,48},{40,24},{48,32},{56,8},{64,80... | collective-permute-start | bytes 491528 | tf_op jit(solution)/shard_map/ppermute | solution.py:352
  27.1 10.5 %collective-permute-start.1 = (f32[40,512]{1,0:T(8,128)S(1)}, f32[40,512]{1,0:T(8,128)S(1)}, u32[]{:S(2)}, u32[]{:S(2)}) collective-permute-start(f32[40,512]{1,0:T(8,128)S(1)} %get-tuple-element.22), channel_id=1, source_target_pairs={{0,32},{8,40},{16,48},{24,56},{32,0},{40,8},{48,16},{56,24},{64,96... | collective-permute-start | bytes 245768 | tf_op jit(solution)/shard_map/ppermute | solution.py:352

commit v11 on v10

--- a/solution.py
+++ b/solution.py
@@ -224,25 +224,20 @@
     return (forward, mixed, back), (forward1, cross, back2)
 
 
-def track(upper, pieces, old_ref, state_ref):
+def track(upper, pieces, old):
     forward1, cross, back2 = pieces
+    here, back, gain = old
     columns = lax.broadcasted_iota(jnp.int32, (TRACE, 2 * HALF), 1) >= HALF
-
-    @pl.when(upper)
-    def _():
-        forward_pair = split(forward1)
-        here = old_ref[:, : 2 * HALF]
-        back = old_ref[:, 2 * HALF : 4 * HALF]
-        state_ref[:, : 2 * HALF] = product(split(here[:, :TRACE]), forward_pair) + jnp.where(columns, here, 0.0)
-        state_ref[:, 2 * HALF : 4 * HALF] = product(split(back[:, :TRACE]), forward_pair) + jnp.where(columns, back, 0.0)
-        state_ref[:, 4 * HALF :] = old_ref[:, 4 * HALF :]
-
-    @pl.when(jnp.logical_not(upper))
-    def _():
-        gain = split(old_ref[:, 4 * HALF : 4 * HALF + TRACE])
-        state_ref[:, : 2 * HALF] = old_ref[:, : 2 * HALF]
-        state_ref[:, 2 * HALF : 4 * HALF] = old_ref[:, 2 * HALF : 4 * HALF] + product(gain, split(cross))
-        state_ref[:, 4 * HALF :] = product(gain, split(back2))
+    through = product(split(here[:, :TRACE]), split(forward1)) + jnp.where(columns, here, 0.0)
+    factor = jnp.where(upper, back[:, :TRACE], gain[:, :TRACE])
+    added = jnp.where(columns | jnp.logical_not(upper), back, 0.0)
+    back = product(split(factor), split(jnp.where(upper, forward1, cross))) + added
+    gained = product(split(gain[:, :TRACE]), split(back2))
+    return jnp.where(upper, through, here), back, jnp.where(upper, gain, gained)
+
+
+def state_of(ref):
+    return ref[:, : 2 * HALF], ref[:, 2 * HALF : 4 * HALF], ref[:, 4 * HALF :]
 
 
 def first_kernel(pair_ref, total_ref, half_ref, state_ref):
@@ -259,7 +254,7 @@
     state_ref[:, 4 * HALF :] = jnp.where(upper, eye[:, :HALF], back2)
 
 
-def four_kernel(own_ref, others_ref, old_ref, half_ref, state_ref, middle_ref):
+def four_kernel(own_ref, others_ref, old_ref, half_ref, state_ref):
     odd, late = is_upper(1) == 1, is_upper(2) == 1
     own, near, far = own_ref[...], others_ref[0, :TRACE], others_ref[1, :TRACE]
     middle = jnp.concatenate([others_ref[0, TRACE:], others_ref[1, TRACE:]], axis=0)
@@ -269,13 +264,13 @@
 
     mine, pieces = merge(*ordered(odd, own, near))
     other, _ = merge(*ordered(odd, middle, far))
-    track(odd, pieces, old_ref, middle_ref)
+    state = track(odd, pieces, state_of(old_ref))
     earlier = [jnp.where(late, b, a) for a, b in zip(mine, other)]
     later = [jnp.where(late, a, b) for a, b in zip(mine, other)]
     total, pieces = merge(earlier, later)
     total = pack(total[0], None, total[1], total[2])
     half_ref[...] = jnp.where(is_upper(0) == 1, total[TRACE // 2 :], total[: TRACE // 2])
-    track(late, pieces, middle_ref, state_ref)
+    state_ref[...] = jnp.concatenate(track(late, pieces, state), axis=1)
 
 
 def combine_kernel(level, sends, pair_ref, old_ref, total_ref, state_ref):
@@ -287,7 +282,7 @@
     if sends != "top":
         total = jnp.where(is_upper(0) == 1, total[TRACE // 2 :], total[: TRACE // 2])
     total_ref[...] = total
-    track(is_upper(level) == 1, pieces, old_ref, state_ref)
+    state_ref[...] = jnp.concatenate(track(is_upper(level) == 1, pieces, state_of(old_ref)), axis=1)
 
 
 def last_kernel(level, pair_ref, old_ref, keep_ref, out_ref, ends_ref):
@@ -389,7 +384,6 @@
         [half, state],
         [total, received, tracked],
         10**8,
-        scratch=[pltpu.VMEM((TRACE, 5 * HALF), F32)],
     )
     pair = gather(part, [(0, 0, 1), (0, 6, 0)]).reshape(2, TRACE, 4 * HALF)
     part, tracked = call(functools.partial(combine_kernel, 3, "whole"), [half, state], [pair, tracked], 3 * 10**7)

time: 67.9 us -> 67.2 us (0.990)
    pallas_call x7, Pallas kernels: 10.2 us -> 9.54 us  [call(): pl.pallas_call(kernel, out_shape=shapes[0] if single else shapes, in_spec...]
where the time goes in v11:
time: 67.2 us; the launch traced here: 65.9 us
  blocking collectives  41.4 us (62%)
  starting transfers between devices  10.4 us (15%)
  Pallas kernels  9.54 us (14%)
  waiting for transfers between devices  4.43 us (7%)
    all_gather x5, blocking collectives, gather(): return lax.all_gather(value, 'stream', axis_index_groups=groups)  26.7 us
    all_to_all x1, blocking collectives, shards(): parts = lax.all_to_all(partial.reshape(groups, local, BLOCK), 'azi', 0, 0)  14.7 us
    ppermute x2, starting transfers between devices, swap(): lax.ppermute(value, 'stream', [(k, k ^ 2 * along[k % 2]) for k in range(c...  10.4 us
    pallas_call x7, Pallas kernels, call(): pl.pallas_call(kernel, out_shape=shapes[0] if single else shapes, in_spec...  9.54 us
    ppermute x2, waiting for transfers between devices, swap(): lax.ppermute(value, 'stream', [(k, k ^ 2 * along[k % 2]) for k in range(c...  4.43 us
  transfers between devices with their start and end apart: 2, of which 1 were waited for; matrix products, arithmetic and copies ran while one was open for 0% of the time, Pallas kernels for 0%

profile of v11, /device:TPU:6, one launch (start us, length us, event | category | flops | bytes accessed | tf_op | source)
XLA Modules:
  0.0 65.9 jit_solution(18130582183875816060)
XLA Ops:
  0.0 0.0 copy-start.3
  0.0 0.0 copy-start.4
  0.0 0.0 copy-start.5
  0.0 1.2 %shard_map.91 = (f32[16,320]{1,0:T(8,128)S(1)}, f32[8,128]{1,0:T(8,128)S(1)}) custom-call(s32[1,64]{1,0:T(1,128)} %bitcast.15, f32[64,320]{1,0:T(8,128)} %rows_hbm.1, s32[2,3]{1,0:T(2,128)} %upwind_hbm.1), custom_call_target="tpu_custom_call" | custom-call | flops 10000000000 | bytes 106776 | tf_op jit(solution)/shard_map/pallas_call | solution.py:315
  1.3 14.7 %all_to_all.5 = f32[8,2,320]{2,1,0:T(2,128)S(1)} all-to-all(f32[8,2,320]{2,1,0:T(2,128)S(1)} %reshape.13), channel_id=1, replica_groups=mesh['stream'=64,'azi'=8] {'azi'}, dimensions={0} | all-to-all | bytes 40960 | tf_op jit(solution)/shard_map/all_to_all | solution.py:368
  16.0 0.0 copy-done
  16.0 0.0 copy-done.1
  16.0 0.0 copy-done.2
  16.0 0.0 copy-done.3
  16.1 4.2 %shard_map.92 = (f32[80,512]{1,0:T(8,128)S(1)}, f32[2,320,384]{2,1,0:T(8,128)S(1)}) custom-call(bf16[2,240,320]{2,1,0:T(8,128)(2,1)S(1)} %copy-done.4, bf16[2,320,240]{2,1,0:T(8,128)(2,1)S(1)} %copy-done.5, f32[8,128]{1,0:T(8,128)S(1)} %get-tuple-element.18.crosses_ref, f32[2,8,320]{2,1,0:T(8,128)S(1)} %bitcast.14, f32[2,80,240]{2,1,0:T(8,128)S(1)} %copy-done.2, ...), custom_call_target="tpu_custom_call" | custom-call | flops 2000000000 | bytes 3854336 | tf_op jit(solution)/shard_map/pallas_call | solution.py:315
  20.3 2.0 %all-gather = f32[160,512]{1,0:T(8,128)S(1)} all-gather(f32[80,512]{1,0:T(8,128)S(1)} %get-tuple-element.20), channel_id=2, replica_groups={{0,8},{16,24},{32,40},{48,56},{64,72},{80,88},{96,104},{112,120},{128,1..., dimensions={0}, use_global_device_ids=true | all-gather | bytes 491520 | tf_op jit(solution)/shard_map/all_gather | solution.py:342
  22.3 0.5 shard_map.93
  22.8 4.3 %collective-permute-start = (f32[80,512]{1,0:T(8,128)S(1)}, f32[80,512]{1,0:T(8,128)S(1)}, u32[]{:S(2)}, u32[]{:S(2)}) collective-permute-start(f32[80,512]{1,0:T(8,128)S(1)} %get-tuple-element.21.own_ref), channel_id=1, source_target_pairs={{0,16},{8,56},{16,0},{24,40},{32,48},{40,24},{48,32},{56,8},{64,80... | collective-permute-start | bytes 491528 | tf_op jit(solution)/shard_map/ppermute | solution.py:347
  27.1 6.1 %collective-permute-start.1 = (f32[40,512]{1,0:T(8,128)S(1)}, f32[40,512]{1,0:T(8,128)S(1)}, u32[]{:S(2)}, u32[]{:S(2)}) collective-permute-start(f32[40,512]{1,0:T(8,128)S(1)} %get-tuple-element.22), channel_id=1, source_target_pairs={{0,32},{8,40},{16,48},{24,56},{32,0},{40,8},{48,16},{56,24},{64,96... | collective-permute-start | bytes 245768 | tf_op jit(solution)/shard_map/ppermute | solution.py:347
  33.2 4.4 %collective-permute-done.1 = f32[40,512]{1,0:T(8,128)S(1)} collective-permute-done((f32[40,512]{1,0:T(8,128)S(1)}, f32[40,512]{1,0:T(8,128)S(1)}, u32[]{:S(2)}, u32[]{:S(2)}) %collective-permute-start.1) | collective-permute-done | bytes 81952 | tf_op jit(solution)/shard_map/ppermute | solution.py:347
  37.6 0.0 collective-permute-done
  37.7 2.2 %all-gather.1 = f32[240,512]{1,0:T(8,128)S(1)} all-gather(f32[120,512]{1,0:T(8,128)S(1)} %pad_maximum_fusion), channel_id=3, replica_groups={{0,8},{16,24},{32,40},{48,56},{64,72},{80,88},{96,104},{112,120},{128,1..., dimensions={0}, use_global_device_ids=true | all-gather | bytes 737280 | tf_op jit(solution)/shard_map/all_gather | solution.py:342
  39.9 1.2 %shard_map.94 = (f32[40,512]{1,0:T(8,128)S(1)}, f32[80,640]{1,0:T(8,128)S(1)}) custom-call(f32[80,512]{1,0:T(8,128)S(1)} %get-tuple-element.21.own_ref, f32[2,120,512]{2,1,0:T(8,128)S(1)} %bitcast.9, f32[80,640]{1,0:T(8,128)S(1)} %get-tuple-element.23.old_ref), custom_call_target="tpu_custom_call" | custom-call | flops 100000000 | bytes 1146880 | tf_op jit(solution)/shard_map/pallas_call | solution.py:315
  41.1 9.6 %all-gather.2 = f32[160,512]{1,0:T(8,128)S(1)} all-gather(f32[40,512]{1,0:T(8,128)S(1)} %get-tuple-element.24), channel_id=4, replica_groups={{0,8,96,104},{16,24,112,120},{32,40,64,72},{48,56,80,88},{128,136,224,2..., dimensions={0}, use_global_device_ids=true | all-gather | bytes 409600 | tf_op jit(solution)/shard_map/all_gather | solution.py:342
  50.7 0.5 shard_map.95
  51.2 6.2 %all-gather.3 = f32[160,512]{1,0:T(8,128)S(1)} all-gather(f32[40,512]{1,0:T(8,128)S(1)} %get-tuple-element.26), channel_id=5, replica_groups={{0,8,128,136},{16,24,144,152},{32,40,160,168},{48,56,176,184},{64,72,19..., dimensions={0}, use_global_device_ids=true | all-gather | bytes 409600 | tf_op jit(solution)/shard_map/all_gather | solution.py:342
  57.4 0.5 shard_map.96
  58.0 6.6 %all-gather.4 = f32[160,256]{1,0:T(8,128)S(1)} all-gather(f32[80,256]{1,0:T(8,128)S(1)} %get-tuple-element.28), channel_id=6, replica_groups={{0,384},{8,392},{16,400},{24,408},{32,416},{40,424},{48,432},{56,440},{..., dimensions={0}, use_global_device_ids=true | all-gather | bytes 245760 | tf_op jit(solution)/shard_map/all_gather | solution.py:342
  64.5 1.4 %shard_map.97 = f32[2,320,128]{2,1,0:T(8,128)} custom-call(f32[2,80,256]{2,1,0:T(8,128)S(1)} %bitcast.13, f32[80,640]{1,0:T(8,128)S(1)} %get-tuple-element.29.old_ref, f32[2,320,384]{2,1,0:T(8,128)S(1)} %get-tuple-element.30.keep_ref), custom_call_target="tpu_custom_call" | custom-call | flops 100000000 | bytes 1679360 | tf_op jit(solution)/shard_map/pallas_call | solution.py:315
  (8 shorter events, 0.0 us)
Async XLA Ops:
  0.0 16.0 %copy-start = (f32[2,320,320]{2,1,0:T(8,128)S(1)}, f32[2,320,320]{2,1,0:T(8,128)}, u32[]{:S(2)}) copy-start(f32[2,320,320]{2,1,0:T(8,128)} %inv_ref.1) | copy-start | bytes 2457604
  0.0 16.0 %copy-start.1 = (f32[2,320,128]{2,1,0:T(8,128)S(1)}, f32[2,320,128]{2,1,0:T(8,128)}, u32[]{:S(2)}) copy-start(f32[2,320,128]{2,1,0:T(8,128)} %rhs_ref.1) | copy-start | bytes 983044
  0.0 16.0 %copy-start.2 = (f32[2,80,240]{2,1,0:T(8,128)S(1)}, f32[2,80,240]{2,1,0:T(8,128)}, u32[]{:S(2)}) copy-start(f32[2,80,240]{2,1,0:T(8,128)} %low_ref.1) | copy-start | bytes 460804
  0.0 16.0 %copy-start.3 = (f32[2,80,240]{2,1,0:T(8,128)S(1)}, f32[2,80,240]{2,1,0:T(8,128)}, u32[]{:S(2)}) copy-start(f32[2,80,240]{2,1,0:T(8,128)} %up_ref.1) | copy-start | bytes 460804
  0.0 16.0 %copy-start.4 = (bf16[2,240,320]{2,1,0:T(8,128)(2,1)S(1)}, bf16[2,240,320]{2,1,0:T(8,128)(2,1)}, u32[]{:S(2)}) copy-start(bf16[2,240,320]{2,1,0:T(8,128)(2,1)} %constant.4.clone.take_ref) | copy-start | bytes 921604
  0.0 16.0 %copy-start.5 = (bf16[2,320,240]{2,1,0:T(8,128)(2,1)S(1)}, bf16[2,320,240]{2,1,0:T(8,128)(2,1)}, u32[]{:S(2)}) copy-start(bf16[2,320,240]{2,1,0:T(8,128)(2,1)} %constant.5.clone.put_ref) | copy-start | bytes 921604
  22.8 14.8 %collective-permute-start = (f32[80,512]{1,0:T(8,128)S(1)}, f32[80,512]{1,0:T(8,128)S(1)}, u32[]{:S(2)}, u32[]{:S(2)}) collective-permute-start(f32[80,512]{1,0:T(8,128)S(1)} %get-tuple-element.21.own_ref), channel_id=1, source_target_pairs={{0,16},{8,56},{16,0},{24,40},{32,48},{40,24},{48,32},{56,8},{64,80... | collective-permute-start | bytes 491528 | tf_op jit(solution)/shard_map/ppermute | solution.py:347
  27.1 10.5 %collective-permute-start.1 = (f32[40,512]{1,0:T(8,128)S(1)}, f32[40,512]{1,0:T(8,128)S(1)}, u32[]{:S(2)}, u32[]{:S(2)}) collective-permute-start(f32[40,512]{1,0:T(8,128)S(1)} %get-tuple-element.22), channel_id=1, source_target_pairs={{0,32},{8,40},{16,48},{24,56},{32,0},{40,8},{48,16},{56,24},{64,96... | collective-permute-start | bytes 245768 | tf_op jit(solution)/shard_map/ppermute | solution.py:347

commit v12 on v11

--- a/solution.py
+++ b/solution.py
@@ -285,24 +285,18 @@
     state_ref[...] = jnp.concatenate(track(is_upper(level) == 1, pieces, state_of(old_ref)), axis=1)
 
 
-def last_kernel(level, pair_ref, old_ref, keep_ref, out_ref, ends_ref):
-    ends_ref[:, TRACE:] = jnp.zeros((2, HALF - TRACE, COLUMNS), F32)
-
-    @pl.when(is_upper(level) == 1)
-    def _():
-        inflow = split(pair_ref[0, :, HALF:])
-        ends_ref[0, :TRACE] = old_ref[:, HALF : 2 * HALF] + product(split(old_ref[:, :TRACE]), inflow)
-        ends_ref[1, :TRACE] = old_ref[:, 3 * HALF : 4 * HALF] + product(split(old_ref[:, 2 * HALF : 2 * HALF + TRACE]), inflow)
-
-    @pl.when(is_upper(level) == 0)
-    def _():
-        outflow = split(pair_ref[0, :, HALF:])
-        value = pair_ref[1, :, HALF:] + product(split(pair_ref[1, :, :TRACE]), outflow)
-        gain = split(old_ref[:, 4 * HALF : 4 * HALF + TRACE])
-        ends_ref[0, :TRACE] = old_ref[:, HALF : 2 * HALF]
-        ends_ref[1, :TRACE] = old_ref[:, 3 * HALF : 4 * HALF] + product(gain, split(value))
-
-    ends = split(ends_ref[...].reshape(2 * HALF, COLUMNS))
+def last_kernel(level, pair_ref, old_ref, keep_ref, out_ref):
+    upper = is_upper(level) == 1
+    here, back, gain = state_of(old_ref)
+    inflow = pair_ref[0, :, HALF:]
+    inflow_pair = split(inflow)
+    value = pair_ref[1, :, HALF:] + product(split(pair_ref[1, :, :TRACE]), inflow_pair)
+    factor = jnp.where(upper, back[:, :TRACE], gain[:, :TRACE])
+    incoming = back[:, HALF:] + product(split(factor), split(jnp.where(upper, inflow, value)))
+    through = product(split(here[:, :TRACE]), inflow_pair)
+    inflow = here[:, HALF:] + jnp.where(upper, through, 0.0)
+    spare = jnp.zeros((HALF - TRACE, COLUMNS), F32)
+    ends = split(jnp.concatenate([inflow, spare, incoming, spare], axis=0))
     for element in range(2):
         known = keep_ref[element]
         maps = jnp.concatenate([known[:, :HALF], known[:, 2 * HALF :]], axis=1)
@@ -396,7 +390,6 @@
         [shape(local, BLOCK, COLUMNS)],
         [pair, tracked, keep],
         10**8,
-        scratch=[pltpu.VMEM((2, HALF, COLUMNS), F32)],
     )
 
 

time: 67.2 us -> 67.2 us (level)
  no operation moved by 1% of the time
where the time goes in v12:
time: 67.2 us; the launch traced here: 66.1 us
  blocking collectives  41.4 us (62%)
  starting transfers between devices  10.4 us (15%)
  Pallas kernels  9.73 us (14%)
  waiting for transfers between devices  4.43 us (7%)
    all_gather x5, blocking collectives, gather(): return lax.all_gather(value, 'stream', axis_index_groups=groups)  26.7 us
    all_to_all x1, blocking collectives, shards(): parts = lax.all_to_all(partial.reshape(groups, local, BLOCK), 'azi', 0, 0)  14.7 us
    ppermute x2, starting transfers between devices, swap(): lax.ppermute(value, 'stream', [(k, k ^ 2 * along[k % 2]) for k in range(c...  10.4 us
    pallas_call x7, Pallas kernels, call(): pl.pallas_call(kernel, out_shape=shapes[0] if single else shapes, in_spec...  9.73 us
    ppermute x2, waiting for transfers between devices, swap(): lax.ppermute(value, 'stream', [(k, k ^ 2 * along[k % 2]) for k in range(c...  4.43 us
  transfers between devices with their start and end apart: 2, of which 1 were waited for; matrix products, arithmetic and copies ran while one was open for 0% of the time, Pallas kernels for 0%

profile of v12, /device:TPU:6, one launch (start us, length us, event | category | flops | bytes accessed | tf_op | source)
XLA Modules:
  0.0 66.1 jit_solution(14633248511542449067)
XLA Ops:
  0.0 0.0 copy-start.3
  0.0 0.0 copy-start.4
  0.0 0.0 copy-start.5
  0.0 1.2 %shard_map.91 = (f32[16,320]{1,0:T(8,128)S(1)}, f32[8,128]{1,0:T(8,128)S(1)}) custom-call(s32[1,64]{1,0:T(1,128)} %bitcast.15, f32[64,320]{1,0:T(8,128)} %rows_hbm.1, s32[2,3]{1,0:T(2,128)} %upwind_hbm.1), custom_call_target="tpu_custom_call" | custom-call | flops 10000000000 | bytes 106776 | tf_op jit(solution)/shard_map/pallas_call | solution.py:309
  1.3 14.7 %all_to_all.5 = f32[8,2,320]{2,1,0:T(2,128)S(1)} all-to-all(f32[8,2,320]{2,1,0:T(2,128)S(1)} %reshape.13), channel_id=1, replica_groups=mesh['stream'=64,'azi'=8] {'azi'}, dimensions={0} | all-to-all | bytes 40960 | tf_op jit(solution)/shard_map/all_to_all | solution.py:362
  16.0 0.0 copy-done
  16.0 0.0 copy-done.1
  16.0 0.0 copy-done.2
  16.0 0.0 copy-done.3
  16.1 4.2 %shard_map.92 = (f32[80,512]{1,0:T(8,128)S(1)}, f32[2,320,384]{2,1,0:T(8,128)S(1)}) custom-call(bf16[2,240,320]{2,1,0:T(8,128)(2,1)S(1)} %copy-done.4, bf16[2,320,240]{2,1,0:T(8,128)(2,1)S(1)} %copy-done.5, f32[8,128]{1,0:T(8,128)S(1)} %get-tuple-element.18.crosses_ref, f32[2,8,320]{2,1,0:T(8,128)S(1)} %bitcast.14, f32[2,80,240]{2,1,0:T(8,128)S(1)} %copy-done.2, ...), custom_call_target="tpu_custom_call" | custom-call | flops 2000000000 | bytes 3854336 | tf_op jit(solution)/shard_map/pallas_call | solution.py:309
  20.3 2.0 %all-gather = f32[160,512]{1,0:T(8,128)S(1)} all-gather(f32[80,512]{1,0:T(8,128)S(1)} %get-tuple-element.20), channel_id=2, replica_groups={{0,8},{16,24},{32,40},{48,56},{64,72},{80,88},{96,104},{112,120},{128,1..., dimensions={0}, use_global_device_ids=true | all-gather | bytes 491520 | tf_op jit(solution)/shard_map/all_gather | solution.py:336
  22.3 0.5 shard_map.93
  22.8 4.3 %collective-permute-start = (f32[80,512]{1,0:T(8,128)S(1)}, f32[80,512]{1,0:T(8,128)S(1)}, u32[]{:S(2)}, u32[]{:S(2)}) collective-permute-start(f32[80,512]{1,0:T(8,128)S(1)} %get-tuple-element.21.own_ref), channel_id=1, source_target_pairs={{0,16},{8,56},{16,0},{24,40},{32,48},{40,24},{48,32},{56,8},{64,80... | collective-permute-start | bytes 491528 | tf_op jit(solution)/shard_map/ppermute | solution.py:341
  27.1 6.1 %collective-permute-start.1 = (f32[40,512]{1,0:T(8,128)S(1)}, f32[40,512]{1,0:T(8,128)S(1)}, u32[]{:S(2)}, u32[]{:S(2)}) collective-permute-start(f32[40,512]{1,0:T(8,128)S(1)} %get-tuple-element.22), channel_id=1, source_target_pairs={{0,32},{8,40},{16,48},{24,56},{32,0},{40,8},{48,16},{56,24},{64,96... | collective-permute-start | bytes 245768 | tf_op jit(solution)/shard_map/ppermute | solution.py:341
  33.2 4.4 %collective-permute-done.1 = f32[40,512]{1,0:T(8,128)S(1)} collective-permute-done((f32[40,512]{1,0:T(8,128)S(1)}, f32[40,512]{1,0:T(8,128)S(1)}, u32[]{:S(2)}, u32[]{:S(2)}) %collective-permute-start.1) | collective-permute-done | bytes 81952 | tf_op jit(solution)/shard_map/ppermute | solution.py:341
  37.6 0.0 collective-permute-done
  37.7 2.2 %all-gather.1 = f32[240,512]{1,0:T(8,128)S(1)} all-gather(f32[120,512]{1,0:T(8,128)S(1)} %pad_maximum_fusion), channel_id=3, replica_groups={{0,8},{16,24},{32,40},{48,56},{64,72},{80,88},{96,104},{112,120},{128,1..., dimensions={0}, use_global_device_ids=true | all-gather | bytes 737280 | tf_op jit(solution)/shard_map/all_gather | solution.py:336
  39.9 1.2 %shard_map.94 = (f32[40,512]{1,0:T(8,128)S(1)}, f32[80,640]{1,0:T(8,128)S(1)}) custom-call(f32[80,512]{1,0:T(8,128)S(1)} %get-tuple-element.21.own_ref, f32[2,120,512]{2,1,0:T(8,128)S(1)} %bitcast.9, f32[80,640]{1,0:T(8,128)S(1)} %get-tuple-element.23.old_ref), custom_call_target="tpu_custom_call" | custom-call | flops 100000000 | bytes 1146880 | tf_op jit(solution)/shard_map/pallas_call | solution.py:309
  41.1 9.6 %all-gather.2 = f32[160,512]{1,0:T(8,128)S(1)} all-gather(f32[40,512]{1,0:T(8,128)S(1)} %get-tuple-element.24), channel_id=4, replica_groups={{0,8,96,104},{16,24,112,120},{32,40,64,72},{48,56,80,88},{128,136,224,2..., dimensions={0}, use_global_device_ids=true | all-gather | bytes 409600 | tf_op jit(solution)/shard_map/all_gather | solution.py:336
  50.7 0.5 shard_map.95
  51.2 6.2 %all-gather.3 = f32[160,512]{1,0:T(8,128)S(1)} all-gather(f32[40,512]{1,0:T(8,128)S(1)} %get-tuple-element.26), channel_id=5, replica_groups={{0,8,128,136},{16,24,144,152},{32,40,160,168},{48,56,176,184},{64,72,19..., dimensions={0}, use_global_device_ids=true | all-gather | bytes 409600 | tf_op jit(solution)/shard_map/all_gather | solution.py:336
  57.4 0.5 shard_map.96
  58.0 6.6 %all-gather.4 = f32[160,256]{1,0:T(8,128)S(1)} all-gather(f32[80,256]{1,0:T(8,128)S(1)} %get-tuple-element.28), channel_id=6, replica_groups={{0,384},{8,392},{16,400},{24,408},{32,416},{40,424},{48,432},{56,440},{..., dimensions={0}, use_global_device_ids=true | all-gather | bytes 245760 | tf_op jit(solution)/shard_map/all_gather | solution.py:336
  64.5 1.6 %shard_map.97 = f32[2,320,128]{2,1,0:T(8,128)} custom-call(f32[2,80,256]{2,1,0:T(8,128)S(1)} %bitcast.13, f32[80,640]{1,0:T(8,128)S(1)} %get-tuple-element.29.old_ref, f32[2,320,384]{2,1,0:T(8,128)S(1)} %get-tuple-element.30.keep_ref), custom_call_target="tpu_custom_call" | custom-call | flops 100000000 | bytes 1679360 | tf_op jit(solution)/shard_map/pallas_call | solution.py:309
  (8 shorter events, 0.0 us)
Async XLA Ops:
  0.0 16.0 %copy-start = (f32[2,320,320]{2,1,0:T(8,128)S(1)}, f32[2,320,320]{2,1,0:T(8,128)}, u32[]{:S(2)}) copy-start(f32[2,320,320]{2,1,0:T(8,128)} %inv_ref.1) | copy-start | bytes 2457604
  0.0 16.0 %copy-start.1 = (f32[2,320,128]{2,1,0:T(8,128)S(1)}, f32[2,320,128]{2,1,0:T(8,128)}, u32[]{:S(2)}) copy-start(f32[2,320,128]{2,1,0:T(8,128)} %rhs_ref.1) | copy-start | bytes 983044
  0.0 16.0 %copy-start.2 = (f32[2,80,240]{2,1,0:T(8,128)S(1)}, f32[2,80,240]{2,1,0:T(8,128)}, u32[]{:S(2)}) copy-start(f32[2,80,240]{2,1,0:T(8,128)} %low_ref.1) | copy-start | bytes 460804
  0.0 16.0 %copy-start.3 = (f32[2,80,240]{2,1,0:T(8,128)S(1)}, f32[2,80,240]{2,1,0:T(8,128)}, u32[]{:S(2)}) copy-start(f32[2,80,240]{2,1,0:T(8,128)} %up_ref.1) | copy-start | bytes 460804
  0.0 16.0 %copy-start.4 = (bf16[2,240,320]{2,1,0:T(8,128)(2,1)S(1)}, bf16[2,240,320]{2,1,0:T(8,128)(2,1)}, u32[]{:S(2)}) copy-start(bf16[2,240,320]{2,1,0:T(8,128)(2,1)} %constant.4.clone.take_ref) | copy-start | bytes 921604
  0.0 16.0 %copy-start.5 = (bf16[2,320,240]{2,1,0:T(8,128)(2,1)S(1)}, bf16[2,320,240]{2,1,0:T(8,128)(2,1)}, u32[]{:S(2)}) copy-start(bf16[2,320,240]{2,1,0:T(8,128)(2,1)} %constant.5.clone.put_ref) | copy-start | bytes 921604
  22.8 14.8 %collective-permute-start = (f32[80,512]{1,0:T(8,128)S(1)}, f32[80,512]{1,0:T(8,128)S(1)}, u32[]{:S(2)}, u32[]{:S(2)}) collective-permute-start(f32[80,512]{1,0:T(8,128)S(1)} %get-tuple-element.21.own_ref), channel_id=1, source_target_pairs={{0,16},{8,56},{16,0},{24,40},{32,48},{40,24},{48,32},{56,8},{64,80... | collective-permute-start | bytes 491528 | tf_op jit(solution)/shard_map/ppermute | solution.py:341
  27.1 10.5 %collective-permute-start.1 = (f32[40,512]{1,0:T(8,128)S(1)}, f32[40,512]{1,0:T(8,128)S(1)}, u32[]{:S(2)}, u32[]{:S(2)}) collective-permute-start(f32[40,512]{1,0:T(8,128)S(1)} %get-tuple-element.22), channel_id=1, source_target_pairs={{0,32},{8,40},{16,48},{24,56},{32,0},{40,8},{48,16},{56,24},{64,96... | collective-permute-start | bytes 245768 | tf_op jit(solution)/shard_map/ppermute | solution.py:341

commit v13 on v11

--- a/solution.py
+++ b/solution.py
@@ -256,8 +256,8 @@
 
 def four_kernel(own_ref, others_ref, old_ref, half_ref, state_ref):
     odd, late = is_upper(1) == 1, is_upper(2) == 1
-    own, near, far = own_ref[...], others_ref[0, :TRACE], others_ref[1, :TRACE]
-    middle = jnp.concatenate([others_ref[0, TRACE:], others_ref[1, TRACE:]], axis=0)
+    own, near, middle = own_ref[...], others_ref[0, :TRACE], others_ref[1, :TRACE]
+    far = jnp.concatenate([others_ref[0, TRACE:], others_ref[1, TRACE:]], axis=0)
 
     def ordered(swap, one, two):
         return unpack(jnp.where(swap, two, one)), unpack(jnp.where(swap, one, two))
@@ -376,8 +376,8 @@
     )
     full, half, state = shape(TRACE, 4 * HALF), shape(TRACE // 2, 4 * HALF), shape(TRACE, 5 * HALF)
     total, part, tracked = call(first_kernel, [full, half, state], [gather(total, [(0, 0, 1)])], 3 * 10**7)
-    part = swap(part, (2, 2))
-    received = jnp.concatenate([swap(total, (1, 3)), part], axis=0)
+    part = swap(part, (3, 3))
+    received = jnp.concatenate([swap(total, (1, 2)), part], axis=0)
     received = gather(received, [(0, 0, 1)])
     part, tracked = call(
         four_kernel,

time: 67.2 us -> 68.6 us (1.021)
  blocking collectives: 41.4 us -> 43.7 us
    all_gather x5, blocking collectives: 26.7 us -> 29 us  [gather(): return lax.all_gather(value, 'stream', axis_index_groups=groups)]
where the time goes in v13:
time: 68.6 us; the launch traced here: 67.6 us
  blocking collectives  43.7 us (64%)
  starting transfers between devices  9.81 us (14%)
  Pallas kernels  9.54 us (14%)
  waiting for transfers between devices  4.43 us (6%)
    all_gather x5, blocking collectives, gather(): return lax.all_gather(value, 'stream', axis_index_groups=groups)  29 us
    all_to_all x1, blocking collectives, shards(): parts = lax.all_to_all(partial.reshape(groups, local, BLOCK), 'azi', 0, 0)  14.7 us
    ppermute x2, starting transfers between devices, swap(): lax.ppermute(value, 'stream', [(k, k ^ 2 * along[k % 2]) for k in range(c...  9.81 us
    pallas_call x7, Pallas kernels, call(): pl.pallas_call(kernel, out_shape=shapes[0] if single else shapes, in_spec...  9.54 us
    ppermute x2, waiting for transfers between devices, swap(): lax.ppermute(value, 'stream', [(k, k ^ 2 * along[k % 2]) for k in range(c...  4.43 us
  transfers between devices with their start and end apart: 2, of which 1 were waited for; matrix products, arithmetic and copies ran while one was open for 0% of the time, Pallas kernels for 0%

profile of v13, /device:TPU:6, one launch (start us, length us, event | category | flops | bytes accessed | tf_op | source)
XLA Modules:
  0.0 67.6 jit_solution(9825934538779755684)
XLA Ops:
  0.0 0.0 copy-start.3
  0.0 0.0 copy-start.4
  0.0 0.0 copy-start.5
  0.0 1.2 %shard_map.91 = (f32[16,320]{1,0:T(8,128)S(1)}, f32[8,128]{1,0:T(8,128)S(1)}) custom-call(s32[1,64]{1,0:T(1,128)} %bitcast.15, f32[64,320]{1,0:T(8,128)} %rows_hbm.1, s32[2,3]{1,0:T(2,128)} %upwind_hbm.1), custom_call_target="tpu_custom_call" | custom-call | flops 10000000000 | bytes 106776 | tf_op jit(solution)/shard_map/pallas_call | solution.py:315
  1.3 14.7 %all_to_all.5 = f32[8,2,320]{2,1,0:T(2,128)S(1)} all-to-all(f32[8,2,320]{2,1,0:T(2,128)S(1)} %reshape.13), channel_id=1, replica_groups=mesh['stream'=64,'azi'=8] {'azi'}, dimensions={0} | all-to-all | bytes 40960 | tf_op jit(solution)/shard_map/all_to_all | solution.py:368
  16.0 0.0 copy-done.2
  16.0 0.0 copy-done.3
  16.1 0.0 copy-done.4
  16.1 0.0 copy-done.5
  16.1 4.2 %shard_map.92 = (f32[80,512]{1,0:T(8,128)S(1)}, f32[2,320,384]{2,1,0:T(8,128)S(1)}) custom-call(bf16[2,240,320]{2,1,0:T(8,128)(2,1)S(1)} %copy-done.4, bf16[2,320,240]{2,1,0:T(8,128)(2,1)S(1)} %copy-done.5, f32[8,128]{1,0:T(8,128)S(1)} %get-tuple-element.18.crosses_ref, f32[2,8,320]{2,1,0:T(8,128)S(1)} %bitcast.14, f32[2,80,240]{2,1,0:T(8,128)S(1)} %copy-done.2, ...), custom_call_target="tpu_custom_call" | custom-call | flops 2000000000 | bytes 3854336 | tf_op jit(solution)/shard_map/pallas_call | solution.py:315
  20.3 2.0 %all-gather = f32[160,512]{1,0:T(8,128)S(1)} all-gather(f32[80,512]{1,0:T(8,128)S(1)} %get-tuple-element.20), channel_id=2, replica_groups={{0,8},{16,24},{32,40},{48,56},{64,72},{80,88},{96,104},{112,120},{128,1..., dimensions={0}, use_global_device_ids=true | all-gather | bytes 491520 | tf_op jit(solution)/shard_map/all_gather | solution.py:342
  22.3 0.5 shard_map.93
  22.8 4.3 %collective-permute-start = (f32[80,512]{1,0:T(8,128)S(1)}, f32[80,512]{1,0:T(8,128)S(1)}, u32[]{:S(2)}, u32[]{:S(2)}) collective-permute-start(f32[80,512]{1,0:T(8,128)S(1)} %get-tuple-element.21.own_ref), channel_id=1, source_target_pairs={{0,16},{8,40},{16,0},{24,56},{32,48},{40,8},{48,32},{56,24},{64,80... | collective-permute-start | bytes 491528 | tf_op jit(solution)/shard_map/ppermute | solution.py:347
  27.1 5.5 %collective-permute-start.1 = (f32[40,512]{1,0:T(8,128)S(1)}, f32[40,512]{1,0:T(8,128)S(1)}, u32[]{:S(2)}, u32[]{:S(2)}) collective-permute-start(f32[40,512]{1,0:T(8,128)S(1)} %get-tuple-element.22), channel_id=1, source_target_pairs={{0,48},{8,56},{16,32},{24,40},{32,16},{40,24},{48,0},{56,8},{64,11... | collective-permute-start | bytes 245768 | tf_op jit(solution)/shard_map/ppermute | solution.py:347
  32.7 4.4 %collective-permute-done.1 = f32[40,512]{1,0:T(8,128)S(1)} collective-permute-done((f32[40,512]{1,0:T(8,128)S(1)}, f32[40,512]{1,0:T(8,128)S(1)}, u32[]{:S(2)}, u32[]{:S(2)}) %collective-permute-start.1) | collective-permute-done | bytes 81952 | tf_op jit(solution)/shard_map/ppermute | solution.py:347
  37.1 0.0 collective-permute-done
  37.1 2.2 %all-gather.1 = f32[240,512]{1,0:T(8,128)S(1)} all-gather(f32[120,512]{1,0:T(8,128)S(1)} %pad_maximum_fusion), channel_id=3, replica_groups={{0,8},{16,24},{32,40},{48,56},{64,72},{80,88},{96,104},{112,120},{128,1..., dimensions={0}, use_global_device_ids=true | all-gather | bytes 737280 | tf_op jit(solution)/shard_map/all_gather | solution.py:342
  39.3 1.2 %shard_map.94 = (f32[40,512]{1,0:T(8,128)S(1)}, f32[80,640]{1,0:T(8,128)S(1)}) custom-call(f32[80,512]{1,0:T(8,128)S(1)} %get-tuple-element.21.own_ref, f32[2,120,512]{2,1,0:T(8,128)S(1)} %bitcast.9, f32[80,640]{1,0:T(8,128)S(1)} %get-tuple-element.23.old_ref), custom_call_target="tpu_custom_call" | custom-call | flops 100000000 | bytes 1146880 | tf_op jit(solution)/shard_map/pallas_call | solution.py:315
  40.5 12.0 %all-gather.2 = f32[160,512]{1,0:T(8,128)S(1)} all-gather(f32[40,512]{1,0:T(8,128)S(1)} %get-tuple-element.24), channel_id=4, replica_groups={{0,8,96,104},{16,24,112,120},{32,40,64,72},{48,56,80,88},{128,136,224,2..., dimensions={0}, use_global_device_ids=true | all-gather | bytes 409600 | tf_op jit(solution)/shard_map/all_gather | solution.py:342
  52.4 0.5 shard_map.95
  53.0 6.2 %all-gather.3 = f32[160,512]{1,0:T(8,128)S(1)} all-gather(f32[40,512]{1,0:T(8,128)S(1)} %get-tuple-element.26), channel_id=5, replica_groups={{0,8,128,136},{16,24,144,152},{32,40,160,168},{48,56,176,184},{64,72,19..., dimensions={0}, use_global_device_ids=true | all-gather | bytes 409600 | tf_op jit(solution)/shard_map/all_gather | solution.py:342
  59.2 0.5 shard_map.96
  59.7 6.6 %all-gather.4 = f32[160,256]{1,0:T(8,128)S(1)} all-gather(f32[80,256]{1,0:T(8,128)S(1)} %get-tuple-element.28), channel_id=6, replica_groups={{0,384},{8,392},{16,400},{24,408},{32,416},{40,424},{48,432},{56,440},{..., dimensions={0}, use_global_device_ids=true | all-gather | bytes 245760 | tf_op jit(solution)/shard_map/all_gather | solution.py:342
  66.3 1.4 %shard_map.97 = f32[2,320,128]{2,1,0:T(8,128)} custom-call(f32[2,80,256]{2,1,0:T(8,128)S(1)} %bitcast.13, f32[80,640]{1,0:T(8,128)S(1)} %get-tuple-element.29.old_ref, f32[2,320,384]{2,1,0:T(8,128)S(1)} %get-tuple-element.30.keep_ref), custom_call_target="tpu_custom_call" | custom-call | flops 100000000 | bytes 1679360 | tf_op jit(solution)/shard_map/pallas_call | solution.py:315
  (8 shorter events, 0.0 us)
Async XLA Ops:
  0.0 16.0 %copy-start = (f32[2,320,320]{2,1,0:T(8,128)S(1)}, f32[2,320,320]{2,1,0:T(8,128)}, u32[]{:S(2)}) copy-start(f32[2,320,320]{2,1,0:T(8,128)} %inv_ref.1) | copy-start | bytes 2457604
  0.0 16.0 %copy-start.1 = (f32[2,320,128]{2,1,0:T(8,128)S(1)}, f32[2,320,128]{2,1,0:T(8,128)}, u32[]{:S(2)}) copy-start(f32[2,320,128]{2,1,0:T(8,128)} %rhs_ref.1) | copy-start | bytes 983044
  0.0 16.0 %copy-start.2 = (f32[2,80,240]{2,1,0:T(8,128)S(1)}, f32[2,80,240]{2,1,0:T(8,128)}, u32[]{:S(2)}) copy-start(f32[2,80,240]{2,1,0:T(8,128)} %low_ref.1) | copy-start | bytes 460804
  0.0 16.0 %copy-start.3 = (f32[2,80,240]{2,1,0:T(8,128)S(1)}, f32[2,80,240]{2,1,0:T(8,128)}, u32[]{:S(2)}) copy-start(f32[2,80,240]{2,1,0:T(8,128)} %up_ref.1) | copy-start | bytes 460804
  0.0 16.0 %copy-start.4 = (bf16[2,240,320]{2,1,0:T(8,128)(2,1)S(1)}, bf16[2,240,320]{2,1,0:T(8,128)(2,1)}, u32[]{:S(2)}) copy-start(bf16[2,240,320]{2,1,0:T(8,128)(2,1)} %constant.4.clone.take_ref) | copy-start | bytes 921604
  0.0 16.0 %copy-start.5 = (bf16[2,320,240]{2,1,0:T(8,128)(2,1)S(1)}, bf16[2,320,240]{2,1,0:T(8,128)(2,1)}, u32[]{:S(2)}) copy-start(bf16[2,320,240]{2,1,0:T(8,128)(2,1)} %constant.5.clone.put_ref) | copy-start | bytes 921604
  22.8 14.3 %collective-permute-start = (f32[80,512]{1,0:T(8,128)S(1)}, f32[80,512]{1,0:T(8,128)S(1)}, u32[]{:S(2)}, u32[]{:S(2)}) collective-permute-start(f32[80,512]{1,0:T(8,128)S(1)} %get-tuple-element.21.own_ref), channel_id=1, source_target_pairs={{0,16},{8,40},{16,0},{24,56},{32,48},{40,8},{48,32},{56,24},{64,80... | collective-permute-start | bytes 491528 | tf_op jit(solution)/shard_map/ppermute | solution.py:347
  27.1 10.0 %collective-permute-start.1 = (f32[40,512]{1,0:T(8,128)S(1)}, f32[40,512]{1,0:T(8,128)S(1)}, u32[]{:S(2)}, u32[]{:S(2)}) collective-permute-start(f32[40,512]{1,0:T(8,128)S(1)} %get-tuple-element.22), channel_id=1, source_target_pairs={{0,48},{8,56},{16,32},{24,40},{32,16},{40,24},{48,0},{56,8},{64,11... | collective-permute-start | bytes 245768 | tf_op jit(solution)/shard_map/ppermute | solution.py:347
